TPU v7x, 256 devices: a whole 4x4x8 slice. The times are simulated.
256 devices in a mesh: chan: 128 (over z, y_lo, x, core), freq: 2 (over y_hi).
Axes of the slice: x: 4, y: 4 (y_hi: 2, y_lo: 2; y = y_hi * 2 + y_lo), z: 8, core: 2. Of those that a mesh axis runs over, the one named last changes fastest.
Arguments:
- spectra: bfloat16 [2, 8, 4096, 1024], P(None, None, 'chan', 'freq'), may hold values from -60 to 60
- seg_mask: int32 [4096, 8], P('chan'), may hold values 0 or 1
Outputs:
- correlations: bfloat16 [2, 256, 4096, 512], P('freq', None, 'chan')
All inputs are finite; a program needn't handle non-finite values. No bound on the sum of `seg_mask` on one device may be relied on, other than what follows from the above.
Results may differ from a plain program's by a relative error of at most 0.017.
Values may be sent and summed in bfloat16 or wider, within the bound.
No kernel may reach another device: no remote copies, remote signals or barrier semaphores. Data moves between devices by JAX's collectives and lax.ppermute only.
A program may use at most 192 MiB of HBM per device.

v0:
```python
import math

import jax
import jax.numpy as jnp
from jax import lax
from jax.sharding import PartitionSpec as P

BAND = 512
FBINS = 1024
HALF = 64
LAGS = 256
NFFT = 2048


EPSILON = 1e-06


def with_halo(cells, sides, width):
    for axis, dim in sides:
        count = lax.axis_size(axis)
        ends = count - 1
        head = lax.slice_in_dim(cells, 0, width, axis=dim)
        tail = lax.slice_in_dim(cells, cells.shape[dim] - width, cells.shape[dim], axis=dim)
        cells = jnp.concatenate(
            [
                lax.ppermute(tail, axis, [(i, (i + 1) % count) for i in range(ends)]),
                cells,
                lax.ppermute(head, axis, [((i + 1) % count, i) for i in range(ends)]),
            ],
            axis=dim,
        )
    return cells


def passed_along(value, axis, by):
    size = lax.axis_size(axis)
    pairs = [(i, i + by) for i in range(size) if 0 <= i + by < size]
    return lax.ppermute(value, axis, pairs)


def band_rows(matrix, band):
    leading = matrix.shape[:-2]
    height = matrix.shape[-2]
    breadth = matrix.shape[-1]
    flattened = matrix.reshape(leading + (height * breadth,))
    padded = jnp.pad(flattened, [(0, 0)] * len(leading) + [(0, height)])
    return padded.reshape(leading + (height, breadth + 1))[..., :band]


def lag_weights(lag_row, first_bin, bin_count, lag_count):
    freq_index = first_bin + jnp.arange(bin_count, dtype=jnp.int32)
    lag_index = jnp.arange(lag_count, dtype=jnp.int32)
    cycles = lag_index[:, None] * freq_index[None, :] % NFFT
    angles = cycles.astype(jnp.float32) * (2.0 * math.pi / NFFT)
    values = jnp.where(lag_row == 0, jnp.cos(angles), -jnp.sin(angles)) * FBINS ** (-0.5)
    return values.astype(jnp.bfloat16)


def lag_partial(extended, lag_row, first_bin, inverse, channels, lag_count, band):
    bin_count = extended.shape[3]
    block_size = 128

    def add_block(number, running):
        block_start = number * block_size
        block = lax.dynamic_slice_in_dim(extended, block_start, block_size, 3)
        rotated = jnp.stack([block[1], -block[0]])
        partner = jnp.where(lag_row == 0, block, rotated)
        source = block[:, :, :channels]
        product = jnp.einsum("ksCf,ksWf->fCW", source, partner, preferred_element_type=jnp.float32)
        scaled = (product * inverse[None]).astype(jnp.bfloat16)
        spectrum = band_rows(scaled, band).reshape(block_size, channels * band)
        weights = lag_weights(lag_row, first_bin + block_start, block_size, lag_count)
        return running + jnp.dot(weights, spectrum, preferred_element_type=jnp.float32)

    return lax.fori_loop(
        0, bin_count // block_size, add_block, jnp.zeros((lag_count, channels * band), jnp.float32)
    )


def local(spectra, seg_mask):
    segments = spectra.shape[1]
    channels = spectra.shape[2]
    bin_count = spectra.shape[3]
    freq_rank = lax.axis_index("freq")
    total_bins = bin_count * lax.axis_size("freq")
    spectral = spectra.astype(jnp.float32)
    magnitude = jnp.sqrt(spectral[0] * spectral[0] + spectral[1] * spectral[1])
    rimmed = with_halo(magnitude.astype(jnp.bfloat16), (("freq", 2),), HALF).astype(magnitude.dtype)
    running_total = jnp.cumsum(rimmed, axis=2)
    running_total = jnp.concatenate(
        [jnp.zeros(rimmed.shape[:2] + (1,), jnp.float32), running_total], 2
    )
    summed = (
        running_total[:, :, 2 * HALF + 1 : 2 * HALF + 1 + bin_count]
        - running_total[:, :, :bin_count]
    )
    global_bin = freq_rank * bin_count + jnp.arange(bin_count, dtype=jnp.int32)
    counted = (
        jnp.minimum(global_bin + HALF, total_bins - 1) - jnp.maximum(global_bin - HALF, 0) + 1
    ).astype(jnp.float32)
    levels = summed / counted + EPSILON
    validity = seg_mask.astype(jnp.float32)
    whitened = (spectral / levels[None] * validity.T[None, :, :, None]).astype(jnp.bfloat16)
    valid_flags = validity.astype(jnp.bfloat16)
    reach = BAND // channels
    stacked = jnp.zeros((reach, 2, segments, channels, bin_count), jnp.bfloat16)
    stacked_flags = jnp.zeros((reach, channels, segments), jnp.bfloat16)

    def fetch(step_index, carried):
        panels, flags, current, current_flags = carried
        current, current_flags = passed_along((current, current_flags), "chan", -1)
        panels = lax.dynamic_update_index_in_dim(panels, current, step_index, 0)
        flags = lax.dynamic_update_index_in_dim(flags, current_flags, step_index, 0)
        return (panels, flags, current, current_flags)

    stacked, stacked_flags, unused_panel, unused_flags = lax.fori_loop(
        0, reach, fetch, (stacked, stacked_flags, whitened, valid_flags)
    )
    arrived = jnp.moveaxis(stacked, 0, 2).reshape(2, segments, reach * channels, bin_count)
    extended = jnp.concatenate([whitened, arrived], 2)
    valid_band = jnp.concatenate(
        [valid_flags, stacked_flags.reshape(reach * channels, segments)], 0
    )
    full_count = jnp.dot(
        validity, valid_band.astype(jnp.float32).T, precision=lax.Precision.HIGHEST
    )
    inverse = 1.0 / jnp.maximum(full_count, 1.0)
    begin_row = jnp.int32(0)
    results = [
        lag_partial(
            extended, begin_row + offset, freq_rank * bin_count, inverse, channels, LAGS, BAND
        ).reshape(LAGS, channels, BAND)
        for offset in range(1 * lax.axis_size("freq"))
    ]
    return lax.psum_scatter(
        jnp.stack(results).astype(jnp.bfloat16), "freq", scatter_dimension=0, tiled=True
    )


def solution(mesh):
    placed = (P(None, None, "chan", "freq"), P("chan", None))
    return jax.shard_map(
        local, mesh=mesh, in_specs=placed, out_specs=P("freq", None, "chan", None), check_vma=False
    )
```

profile of v0, /device:TPU:1, one launch (start us, length us, event | category | flops | bytes accessed | tf_op | source)
XLA Modules:
  0.0 862.7 jit_solution(3749762118251121879)
XLA Ops:
  20.4 11.5 %reduce-window.6 = f32[8,32,5,128]{3,1,2,0:T(8,128)S(1)} reduce-window(f32[8,32,5,128]{3,1,2,0:T(8,128)S(1)} %copy_bitcast_fusion.1, f32[]{:T(128)} %constant.217.clone.1), window={size=1x1x1x128 pad=0_0x0_0x0_0x127_0}, to_apply=%region_0.0 | reduce-window | flops 20807680 | bytes 1310724 | tf_op jit(solution)/shard_map/reduce-window
  33.4 185.0 %while.51 = (s32[]{:T(128)}, bf16[16,2,8,32,512]{4,3,0,2,1:T(8,128)(2,1)}, bf16[16,32,8]{1,2,0:T(8,128)(2,1)S(1)}, bf16[2,8,32,512]{3,2,1,0:T(8,128)(2,1)S(1)}, bf16[32,8]{0,1:T(8,128)(2,1)S(1)}, /*index=5*/s32[]{:T(128)}) while((s32[]{:T(128)}, bf16[16,2,8,32,512]{4,3,0,2,1:T(8,128)(2,1)}, bf16[16,32,8]{1,2,0:T(8,128)(2,1)S(1)}, ...), condition=%wide.region_3.4_spmd, body=%wide.region_2.3_spmd.sunk | while | flops 2 | bytes 4201637 | solution.py:116
  50.2 6.7 collective-permute-done.1
  130.1 6.7 collective-permute-done.1
  198.5 6.7 collective-permute-done.1
  210.0 7.5 collective-permute-done.1
  218.5 7.7 pad_maximum_fusion.1
  226.4 17.6 %copy.26 = bf16[2,8,544,512]{2,1,0,3:T(8,128)(2,1)} copy(bf16[2,8,544,512]{3,2,1,0:T(8,128)(2,1)} %pad_maximum_fusion.1) | data formatting | bytes 17825792
  244.0 152.8 %while.53 = (s32[]{:T(128)}, f32[256,16384]{1,0:T(8,128)}, s32[]{:T(128)}, bf16[2,8,544,512]{2,1,0,3:T(8,128)(2,1)}, f32[32,544]{1,0:T(8,128)S(1)}, /*index=5*/s...) while((s32[]{:T(128)}, f32[256,16384]{1,0:T(8,128)}, s32[]{:T(128)}, ...), condition=%wide.region_7.8_spmd.clone, body=%wide.region_6.7_spmd.clone.sunk | while | flops 1160118400 | bytes 88831216 | solution.py:75
  250.9 8.6 copy.41
  272.3 7.3 convolution_add_fusion.5
  286.6 8.6 copy.41
  308.0 10.7 %convolution_add_fusion.5 = f32[256,16384]{1,0:T(8,128)} fusion(bf16[128,16384]{0,1:T(8,128)(2,1)S(1)} %bitcast.78, f32[256,16384]{1,0:T(8,128)} %get-tuple-element.596, pred[]{:T(512)S(6)} %compare.12, s32[128]{0:T(128)S(1)} %iota_add_fusion.5), kind=kOutput, calls=%fused_computation.32.clone.1 | convolution fusion | flops 1082687488 | bytes 37749248 | tf_op jit(solution)/shard_map/while/body/eval_jaxpr/dot_general | solution.py:73
  325.6 8.6 copy.41
  347.0 10.7 %convolution_add_fusion.5 = f32[256,16384]{1,0:T(8,128)} fusion(bf16[128,16384]{0,1:T(8,128)(2,1)S(1)} %bitcast.78, f32[256,16384]{1,0:T(8,128)} %get-tuple-element.596, pred[]{:T(512)S(6)} %compare.12, s32[128]{0:T(128)S(1)} %iota_add_fusion.5), kind=kOutput, calls=%fused_computation.32.clone.1 | convolution fusion | flops 1082687488 | bytes 37749248 | tf_op jit(solution)/shard_map/while/body/eval_jaxpr/dot_general | solution.py:73
  364.7 8.6 copy.41
  386.1 10.7 %convolution_add_fusion.5 = f32[256,16384]{1,0:T(8,128)} fusion(bf16[128,16384]{0,1:T(8,128)(2,1)S(1)} %bitcast.78, f32[256,16384]{1,0:T(8,128)} %get-tuple-element.596, pred[]{:T(512)S(6)} %compare.12, s32[128]{0:T(128)S(1)} %iota_add_fusion.5), kind=kOutput, calls=%fused_computation.32.clone.1 | convolution fusion | flops 1082687488 | bytes 37749248 | tf_op jit(solution)/shard_map/while/body/eval_jaxpr/dot_general | solution.py:73
  396.8 8.9 %convert.10 = bf16[256,16384]{1,0:T(8,128)(2,1)} convert(f32[256,16384]{1,0:T(8,128)} %get-tuple-element.371) | non-fusion elementwise | flops 4194304 | bytes 25165824 | tf_op jit(solution)/shard_map/convert.3
  405.7 10.4 %copy.35 = bf16[32,8,32,512]{3,2,1,0:T(8,128)(2,1)} copy(bf16[32,8,32,512]{3,1,2,0:T(8,128)(2,1)} %bitcast.80) | data formatting | bytes 16777216
  416.1 148.6 %while.52 = (s32[]{:T(128)}, f32[256,16384]{1,0:T(8,128)}, s32[]{:T(128)}, bf16[2,8,544,512]{2,1,0,3:T(8,128)(2,1)}, f32[32,544]{1,0:T(8,128)S(1)}, /*index=5*/s...) while((s32[]{:T(128)}, f32[256,16384]{1,0:T(8,128)}, s32[]{:T(128)}, ...), condition=%wide.region_5.6_spmd.clone, body=%wide.region_4.5_spmd.clone.sunk | while | flops 1158414464 | bytes 84768968 | solution.py:75
  421.9 8.6 copy.40
  443.3 7.3 convolution_add_fusion.4
  456.5 8.6 copy.40
  477.9 10.7 %convolution_add_fusion.4 = f32[256,16384]{1,0:T(8,128)} fusion(bf16[128,16384]{0,1:T(8,128)(2,1)S(1)} %bitcast.79, f32[256,16384]{1,0:T(8,128)} %get-tuple-element.628, pred[]{:T(512)S(6)} %compare.11, s32[128]{0:T(128)S(1)} %iota_add_fusion.4), kind=kOutput, calls=%fused_computation.2.clone.1 | convolution fusion | flops 1082654720 | bytes 37749248 | tf_op jit(solution)/shard_map/while/body/eval_jaxpr/dot_general | solution.py:73
  494.5 8.6 copy.40
  515.9 10.7 %convolution_add_fusion.4 = f32[256,16384]{1,0:T(8,128)} fusion(bf16[128,16384]{0,1:T(8,128)(2,1)S(1)} %bitcast.79, f32[256,16384]{1,0:T(8,128)} %get-tuple-element.628, pred[]{:T(512)S(6)} %compare.11, s32[128]{0:T(128)S(1)} %iota_add_fusion.4), kind=kOutput, calls=%fused_computation.2.clone.1 | convolution fusion | flops 1082654720 | bytes 37749248 | tf_op jit(solution)/shard_map/while/body/eval_jaxpr/dot_general | solution.py:73
  532.5 8.6 copy.40
  553.9 10.7 %convolution_add_fusion.4 = f32[256,16384]{1,0:T(8,128)} fusion(bf16[128,16384]{0,1:T(8,128)(2,1)S(1)} %bitcast.79, f32[256,16384]{1,0:T(8,128)} %get-tuple-element.628, pred[]{:T(512)S(6)} %compare.11, s32[128]{0:T(128)S(1)} %iota_add_fusion.4), kind=kOutput, calls=%fused_computation.2.clone.1 | convolution fusion | flops 1082654720 | bytes 37749248 | tf_op jit(solution)/shard_map/while/body/eval_jaxpr/dot_general | solution.py:73
  564.7 8.9 %convert.9 = bf16[256,16384]{1,0:T(8,128)(2,1)} convert(f32[256,16384]{1,0:T(8,128)} %get-tuple-element.370) | non-fusion elementwise | flops 4194304 | bytes 25165824 | tf_op jit(solution)/shard_map/convert.4
  573.5 10.4 %copy.34 = bf16[32,8,32,512]{3,2,1,0:T(8,128)(2,1)} copy(bf16[32,8,32,512]{3,1,2,0:T(8,128)(2,1)} %bitcast.81) | data formatting | bytes 16777216
  583.9 13.7 %pad_maximum_fusion = bf16[2,256,32,512]{3,2,1,0:T(8,128)(2,1)} fusion(bf16[1,256,32,512]{3,2,1,0:T(8,128)(2,1)} %bitcast.82, bf16[1,256,32,512]{3,2,1,0:T(8,128)(2,1)} %bitcast.83), kind=kLoop, calls=%fused_computation.68 | loop fusion | flops 8388608 | bytes 33554432 | tf_op jit(solution)/shard_map/stack | solution.py:136
  597.7 258.2 %reduce-scatter.2.cloned.1.call-done = bf16[1,256,32,512]{3,2,1,0:T(8,128)(2,1)} async-done(((bf16[2,256,32,512]{3,2,1,0:T(8,128)(2,1)}), bf16[1,256,32,512]{3,2,1,0:T(8,128)(2,1)}) %reduce-scatter.2.cloned.1.call-update) | async-done | bytes 8388624 | tf_op jit(solution)/shard_map/reduce_scatter | solution.py:135
  (209 shorter events, 326.2 us)
Async XLA Ops:
  6.5 849.4 %reduce-scatter.2.cloned.1.call-start = ((), (), s32[]{:S(2)}) async-start(), calls=%async_computation.1 | async-start | bytes 25165824 | tf_op jit(solution)/shard_map/reduce_scatter | solution.py:135
  33.4 12.0 %collective-permute-start = (bf16[2,8,32,512]{3,2,1,0:T(8,128)(2,1)S(1)}, bf16[2,8,32,512]{3,2,1,0:T(8,128)(2,1)S(1)}, u32[]{:S(2)}, u32[]{:S(2)}) collective-permute-start(bf16[2,8,32,512]{3,2,1,0:T(8,128)(2,1)S(1)} %get-tuple-element.575), channel_id=1, source_target_pairs={{2,0},{4,2},{6,4},{8,6},{10,8},{12,10},{14,12},{16,14},{18,16},{20... | collective-permute-start | bytes 1572872 | tf_op jit(solution)/shard_map/while/body/eval_jaxpr/ppermute | solution.py:38
  46.3 10.5 %collective-permute-start = (bf16[2,8,32,512]{3,2,1,0:T(8,128)(2,1)S(1)}, bf16[2,8,32,512]{3,2,1,0:T(8,128)(2,1)S(1)}, u32[]{:S(2)}, u32[]{:S(2)}) collective-permute-start(bf16[2,8,32,512]{3,2,1,0:T(8,128)(2,1)S(1)} %get-tuple-element.575), channel_id=1, source_target_pairs={{2,0},{4,2},{6,4},{8,6},{10,8},{12,10},{14,12},{16,14},{18,16},{20... | collective-permute-start | bytes 1572872 | tf_op jit(solution)/shard_map/while/body/eval_jaxpr/ppermute | solution.py:38
  48.2 8.6 collective-permute-start.1
  57.7 10.5 %collective-permute-start = (bf16[2,8,32,512]{3,2,1,0:T(8,128)(2,1)S(1)}, bf16[2,8,32,512]{3,2,1,0:T(8,128)(2,1)S(1)}, u32[]{:S(2)}, u32[]{:S(2)}) collective-permute-start(bf16[2,8,32,512]{3,2,1,0:T(8,128)(2,1)S(1)} %get-tuple-element.575), channel_id=1, source_target_pairs={{2,0},{4,2},{6,4},{8,6},{10,8},{12,10},{14,12},{16,14},{18,16},{20... | collective-permute-start | bytes 1572872 | tf_op jit(solution)/shard_map/while/body/eval_jaxpr/ppermute | solution.py:38
  59.6 8.6 collective-permute-start.1
  69.1 10.5 %collective-permute-start = (bf16[2,8,32,512]{3,2,1,0:T(8,128)(2,1)S(1)}, bf16[2,8,32,512]{3,2,1,0:T(8,128)(2,1)S(1)}, u32[]{:S(2)}, u32[]{:S(2)}) collective-permute-start(bf16[2,8,32,512]{3,2,1,0:T(8,128)(2,1)S(1)} %get-tuple-element.575), channel_id=1, source_target_pairs={{2,0},{4,2},{6,4},{8,6},{10,8},{12,10},{14,12},{16,14},{18,16},{20... | collective-permute-start | bytes 1572872 | tf_op jit(solution)/shard_map/while/body/eval_jaxpr/ppermute | solution.py:38
  71.1 8.6 collective-permute-start.1
  80.6 10.5 %collective-permute-start = (bf16[2,8,32,512]{3,2,1,0:T(8,128)(2,1)S(1)}, bf16[2,8,32,512]{3,2,1,0:T(8,128)(2,1)S(1)}, u32[]{:S(2)}, u32[]{:S(2)}) collective-permute-start(bf16[2,8,32,512]{3,2,1,0:T(8,128)(2,1)S(1)} %get-tuple-element.575), channel_id=1, source_target_pairs={{2,0},{4,2},{6,4},{8,6},{10,8},{12,10},{14,12},{16,14},{18,16},{20... | collective-permute-start | bytes 1572872 | tf_op jit(solution)/shard_map/while/body/eval_jaxpr/ppermute | solution.py:38
  82.5 8.6 collective-permute-start.1
  92.0 10.5 %collective-permute-start = (bf16[2,8,32,512]{3,2,1,0:T(8,128)(2,1)S(1)}, bf16[2,8,32,512]{3,2,1,0:T(8,128)(2,1)S(1)}, u32[]{:S(2)}, u32[]{:S(2)}) collective-permute-start(bf16[2,8,32,512]{3,2,1,0:T(8,128)(2,1)S(1)} %get-tuple-element.575), channel_id=1, source_target_pairs={{2,0},{4,2},{6,4},{8,6},{10,8},{12,10},{14,12},{16,14},{18,16},{20... | collective-permute-start | bytes 1572872 | tf_op jit(solution)/shard_map/while/body/eval_jaxpr/ppermute | solution.py:38
  93.9 8.6 collective-permute-start.1
  103.4 10.5 %collective-permute-start = (bf16[2,8,32,512]{3,2,1,0:T(8,128)(2,1)S(1)}, bf16[2,8,32,512]{3,2,1,0:T(8,128)(2,1)S(1)}, u32[]{:S(2)}, u32[]{:S(2)}) collective-permute-start(bf16[2,8,32,512]{3,2,1,0:T(8,128)(2,1)S(1)} %get-tuple-element.575), channel_id=1, source_target_pairs={{2,0},{4,2},{6,4},{8,6},{10,8},{12,10},{14,12},{16,14},{18,16},{20... | collective-permute-start | bytes 1572872 | tf_op jit(solution)/shard_map/while/body/eval_jaxpr/ppermute | solution.py:38
  105.3 8.6 collective-permute-start.1
  114.8 10.5 %collective-permute-start = (bf16[2,8,32,512]{3,2,1,0:T(8,128)(2,1)S(1)}, bf16[2,8,32,512]{3,2,1,0:T(8,128)(2,1)S(1)}, u32[]{:S(2)}, u32[]{:S(2)}) collective-permute-start(bf16[2,8,32,512]{3,2,1,0:T(8,128)(2,1)S(1)} %get-tuple-element.575), channel_id=1, source_target_pairs={{2,0},{4,2},{6,4},{8,6},{10,8},{12,10},{14,12},{16,14},{18,16},{20... | collective-permute-start | bytes 1572872 | tf_op jit(solution)/shard_map/while/body/eval_jaxpr/ppermute | solution.py:38
  116.7 8.6 collective-permute-start.1
  126.2 10.5 %collective-permute-start = (bf16[2,8,32,512]{3,2,1,0:T(8,128)(2,1)S(1)}, bf16[2,8,32,512]{3,2,1,0:T(8,128)(2,1)S(1)}, u32[]{:S(2)}, u32[]{:S(2)}) collective-permute-start(bf16[2,8,32,512]{3,2,1,0:T(8,128)(2,1)S(1)} %get-tuple-element.575), channel_id=1, source_target_pairs={{2,0},{4,2},{6,4},{8,6},{10,8},{12,10},{14,12},{16,14},{18,16},{20... | collective-permute-start | bytes 1572872 | tf_op jit(solution)/shard_map/while/body/eval_jaxpr/ppermute | solution.py:38
  128.1 8.6 collective-permute-start.1
  137.6 10.5 %collective-permute-start = (bf16[2,8,32,512]{3,2,1,0:T(8,128)(2,1)S(1)}, bf16[2,8,32,512]{3,2,1,0:T(8,128)(2,1)S(1)}, u32[]{:S(2)}, u32[]{:S(2)}) collective-permute-start(bf16[2,8,32,512]{3,2,1,0:T(8,128)(2,1)S(1)} %get-tuple-element.575), channel_id=1, source_target_pairs={{2,0},{4,2},{6,4},{8,6},{10,8},{12,10},{14,12},{16,14},{18,16},{20... | collective-permute-start | bytes 1572872 | tf_op jit(solution)/shard_map/while/body/eval_jaxpr/ppermute | solution.py:38
  139.5 8.6 collective-permute-start.1
  149.0 10.5 %collective-permute-start = (bf16[2,8,32,512]{3,2,1,0:T(8,128)(2,1)S(1)}, bf16[2,8,32,512]{3,2,1,0:T(8,128)(2,1)S(1)}, u32[]{:S(2)}, u32[]{:S(2)}) collective-permute-start(bf16[2,8,32,512]{3,2,1,0:T(8,128)(2,1)S(1)} %get-tuple-element.575), channel_id=1, source_target_pairs={{2,0},{4,2},{6,4},{8,6},{10,8},{12,10},{14,12},{16,14},{18,16},{20... | collective-permute-start | bytes 1572872 | tf_op jit(solution)/shard_map/while/body/eval_jaxpr/ppermute | solution.py:38
  151.0 8.6 collective-permute-start.1
  160.5 10.5 %collective-permute-start = (bf16[2,8,32,512]{3,2,1,0:T(8,128)(2,1)S(1)}, bf16[2,8,32,512]{3,2,1,0:T(8,128)(2,1)S(1)}, u32[]{:S(2)}, u32[]{:S(2)}) collective-permute-start(bf16[2,8,32,512]{3,2,1,0:T(8,128)(2,1)S(1)} %get-tuple-element.575), channel_id=1, source_target_pairs={{2,0},{4,2},{6,4},{8,6},{10,8},{12,10},{14,12},{16,14},{18,16},{20... | collective-permute-start | bytes 1572872 | tf_op jit(solution)/shard_map/while/body/eval_jaxpr/ppermute | solution.py:38
  162.4 8.6 collective-permute-start.1
  171.9 10.5 %collective-permute-start = (bf16[2,8,32,512]{3,2,1,0:T(8,128)(2,1)S(1)}, bf16[2,8,32,512]{3,2,1,0:T(8,128)(2,1)S(1)}, u32[]{:S(2)}, u32[]{:S(2)}) collective-permute-start(bf16[2,8,32,512]{3,2,1,0:T(8,128)(2,1)S(1)} %get-tuple-element.575), channel_id=1, source_target_pairs={{2,0},{4,2},{6,4},{8,6},{10,8},{12,10},{14,12},{16,14},{18,16},{20... | collective-permute-start | bytes 1572872 | tf_op jit(solution)/shard_map/while/body/eval_jaxpr/ppermute | solution.py:38
  173.8 8.6 collective-permute-start.1
  183.3 10.5 %collective-permute-start = (bf16[2,8,32,512]{3,2,1,0:T(8,128)(2,1)S(1)}, bf16[2,8,32,512]{3,2,1,0:T(8,128)(2,1)S(1)}, u32[]{:S(2)}, u32[]{:S(2)}) collective-permute-start(bf16[2,8,32,512]{3,2,1,0:T(8,128)(2,1)S(1)} %get-tuple-element.575), channel_id=1, source_target_pairs={{2,0},{4,2},{6,4},{8,6},{10,8},{12,10},{14,12},{16,14},{18,16},{20... | collective-permute-start | bytes 1572872 | tf_op jit(solution)/shard_map/while/body/eval_jaxpr/ppermute | solution.py:38
  185.2 8.6 collective-permute-start.1
  194.7 10.5 %collective-permute-start = (bf16[2,8,32,512]{3,2,1,0:T(8,128)(2,1)S(1)}, bf16[2,8,32,512]{3,2,1,0:T(8,128)(2,1)S(1)}, u32[]{:S(2)}, u32[]{:S(2)}) collective-permute-start(bf16[2,8,32,512]{3,2,1,0:T(8,128)(2,1)S(1)} %get-tuple-element.575), channel_id=1, source_target_pairs={{2,0},{4,2},{6,4},{8,6},{10,8},{12,10},{14,12},{16,14},{18,16},{20... | collective-permute-start | bytes 1572872 | tf_op jit(solution)/shard_map/while/body/eval_jaxpr/ppermute | solution.py:38
  196.6 8.6 collective-permute-start.1
  206.1 11.4 %collective-permute-start = (bf16[2,8,32,512]{3,2,1,0:T(8,128)(2,1)S(1)}, bf16[2,8,32,512]{3,2,1,0:T(8,128)(2,1)S(1)}, u32[]{:S(2)}, u32[]{:S(2)}) collective-permute-start(bf16[2,8,32,512]{3,2,1,0:T(8,128)(2,1)S(1)} %get-tuple-element.575), channel_id=1, source_target_pairs={{2,0},{4,2},{6,4},{8,6},{10,8},{12,10},{14,12},{16,14},{18,16},{20... | collective-permute-start | bytes 1572872 | tf_op jit(solution)/shard_map/while/body/eval_jaxpr/ppermute | solution.py:38
  208.0 9.4 %collective-permute-start.1 = (bf16[32,8]{0,1:T(8,128)(2,1)S(1)}, bf16[32,8]{0,1:T(8,128)(2,1)S(1)}, u32[]{:S(2)}, u32[]{:S(2)}) collective-permute-start(bf16[32,8]{0,1:T(8,128)(2,1)S(1)} %get-tuple-element.576), channel_id=1, source_target_pairs={{2,0},{4,2},{6,4},{8,6},{10,8},{12,10},{14,12},{16,14},{18,16},{20... | collective-permute-start | bytes 1544 | tf_op jit(solution)/shard_map/while/body/eval_jaxpr/ppermute | solution.py:38
  (13 other events, 74.0 us)
Sparse Core Ops, SparseCore 0:
  597.8 258.0 reduce-scatter.1
where the time goes:
time: 868 us; the launch traced here: 863 us
  waiting for transfers between devices  370 us (43%)
  local copies, waits for them, and re-layouts  225 us (26%)
  matrix products  123 us (14%)
  starting transfers between devices  70.3 us (8%)
  other arithmetic  61.5 us (7%)
  between operations  13.6 us (2%)
    reduce_scatter x1, waiting for transfers between devices, local(): lax.psum_scatter(jnp.stack(results).astype(jnp.bfloat16), 'freq', scatter...  258 us
    ppermute x32, waiting for transfers between devices, passed_along(): return lax.ppermute(value, axis, pairs)  107 us
    dot_general x8, matrix products, add_block(): jnp.dot(weights, spectrum, preferred_element_type=jnp.float32)  79 us
    convert_element_type x8, local copies, waits for them, and re-layouts, add_block(): scaled = (product * inverse[None]).astype(jnp.bfloat16)  68.7 us
    ppermute x32, starting transfers between devices, passed_along(): return lax.ppermute(value, axis, pairs)  63.4 us
    dot_general x8, matrix products, add_block(): jnp.einsum('ksCf,ksWf->fCW', source, partner, preferred_element_type=jnp....  43.4 us
    reshape x8, local copies, waits for them, and re-layouts, band_rows(): return padded.reshape(leading + (height, breadth + 1))[..., :band]  42.9 us
    pad x8, local copies, waits for them, and re-layouts, band_rows(): padded = jnp.pad(flattened, [(0, 0)] * len(leading) + [(0, height)])  42.1 us
  transfers between devices with their start and end apart: 35, of which 18 were waited for; matrix products, arithmetic and copies ran while one was open for 0% of the time, Pallas kernels for 0%

commit v1 on v0

v1 whole, which is shorter than its diff:
```python
import math

import jax
import jax.numpy as jnp
import ml_dtypes
import numpy as np
from jax import lax
from jax.experimental import pallas as pl
from jax.experimental.pallas import tpu as pltpu
from jax.sharding import PartitionSpec as P

BAND = 512
FBINS = 1024
HALF = 64
LAGS = 256
NFFT = 2048
EPSILON = 1e-06
SEGMENTS = 8
CH = 32
BINS = 512
GROUP = 16
GROUPS = BINS // GROUP
DEPTH = 2 * SEGMENTS * GROUP
STEP = 4
ROWS = 2
LINE = 4
CSTEP = 4
AXES = ("chan", "freq")
VMEM = 60 * 1024 * 1024
INTERPRET = False


def moved(value, back=(0, 0, 0), core=0, freq=0):
    count, halves = lax.axis_size("chan"), lax.axis_size("freq")
    planes = count // (ROWS * LINE * 2)
    pairs = []
    for index in range(count * halves):
        rest, f = divmod(index, halves)
        rest, k = divmod(rest, 2)
        rest, x = divmod(rest, LINE)
        z, y = divmod(rest, ROWS)
        z, y, x = (z - back[0]) % planes, (y - back[1]) % ROWS, (x - back[2]) % LINE
        pairs.append((index, (((z * ROWS + y) * LINE + x) * 2 + (k ^ core)) * halves + (f ^ freq)))
    return lax.ppermute(value, AXES, pairs)


def whiten_kernel(rank_ref, spectra_ref, rim_ref, mask_ref, out_ref):
    rank = rank_ref[0]
    real = spectra_ref[0].astype(jnp.float32)
    imag = spectra_ref[1].astype(jnp.float32)
    magnitude = jnp.sqrt(real * real + imag * imag).reshape(SEGMENTS * CH, BINS)
    rim_real = rim_ref[0].astype(jnp.float32)
    rim_imag = rim_ref[1].astype(jnp.float32)
    rim = jnp.sqrt(rim_real * rim_real + rim_imag * rim_imag).reshape(SEGMENTS * CH, 128)

    def window_sum(values, positions):
        target = lax.broadcasted_iota(jnp.int32, (values.shape[1], BINS), 1)
        near = jnp.abs(positions - target) <= HALF
        table = jnp.where(near, 1.0, 0.0).astype(jnp.bfloat16)
        high = values.astype(jnp.bfloat16)
        low = (values - high.astype(jnp.float32)).astype(jnp.bfloat16)
        return jnp.dot(high, table, preferred_element_type=jnp.float32) + jnp.dot(
            low, table, preferred_element_type=jnp.float32
        )

    inner = lax.broadcasted_iota(jnp.int32, (BINS, BINS), 0)
    outer = lax.broadcasted_iota(jnp.int32, (128, BINS), 0) + jnp.where(rank == 0, BINS, -128)
    summed = window_sum(magnitude, inner) + window_sum(rim, outer)
    bin_index = rank * BINS + lax.broadcasted_iota(jnp.int32, (1, BINS), 1)
    counted = (
        jnp.minimum(bin_index + HALF, FBINS - 1) - jnp.maximum(bin_index - HALF, 0) + 1
    ).astype(jnp.float32)
    levels = summed / counted + EPSILON
    scale = (1.0 / levels).reshape(SEGMENTS, CH, BINS)
    valid = mask_ref[...].astype(jnp.float32)
    out_ref[GROUPS] = jnp.concatenate(
        [valid, jnp.zeros((CH, DEPTH - SEGMENTS), jnp.float32)], 1
    ).astype(jnp.bfloat16)
    lane = lax.broadcasted_iota(jnp.int32, (CH, 128), 1)
    for p, part in enumerate((real, imag)):
        for tile in range(BINS // 128):
            cut = slice(tile * 128, tile * 128 + 128)
            rows = [
                part[s, :, cut] * scale[s, :, cut] * valid[:, s : s + 1] for s in range(SEGMENTS)
            ]
            for bit in (1, 2, 4):
                upper = (lane // GROUP) & bit != 0
                for i in range(SEGMENTS):
                    if i & bit:
                        continue
                    a, b = rows[i], rows[i + bit]
                    rows[i] = jnp.where(upper, pltpu.roll(b, bit * GROUP, 1), a)
                    rows[i + bit] = jnp.where(upper, b, pltpu.roll(a, 128 - bit * GROUP, 1))
            for g in range(SEGMENTS):
                out_ref[tile * SEGMENTS + g, :, p * 128 : p * 128 + 128] = rows[g].astype(
                    jnp.bfloat16
                )


def whiten(rank, spectra, rim, mask):
    return pl.pallas_call(
        whiten_kernel,
        out_shape=jax.ShapeDtypeStruct((GROUPS + 1, CH, DEPTH), jnp.bfloat16),
        in_specs=[pl.BlockSpec(memory_space=pltpu.SMEM)]
        + [pl.BlockSpec(memory_space=pltpu.VMEM)] * 3,
        out_specs=pl.BlockSpec(memory_space=pltpu.VMEM),
        compiler_params=pltpu.CompilerParams(vmem_limit_bytes=VMEM),
        name="whiten",
    )(rank, spectra, rim, mask)


def piece_kernel(steps, units, final, place_ref, *refs):
    arrays = sorted({unit[0] for unit in units.values()})
    own_ref, source_refs, refs = refs[0], refs[1:3], refs[3:]
    array_refs = dict(zip(arrays, refs[: len(arrays)]))
    table_ref, refs = refs[len(arrays)], refs[len(arrays) + 1 :]
    closing = 0 in steps
    earlier = [j for j in range(LINE) if j not in steps] if final else []
    earlier_refs, refs = refs[: len(earlier)], refs[len(earlier) :]
    if final:
        result_ref, refs = refs[-1], refs[:-1]
    out_ref, rows_ref, flags_ref, diagonal_ref, product_ref, inverse_ref, weights_ref, sems = refs
    core, x, chip, chips = place_ref[0], place_ref[1], place_ref[2], place_ref[3]
    rank = place_ref[4]
    step = pl.program_id(0)
    width = 128 * len(steps)
    blocks = 8 * len(steps) + 4 * closing
    corr_steps = GROUPS // STEP

    def unit_at(j, kind, half, layer):
        if isinstance(kind, int) and kind == 2:
            return blocks - 4 + 2 * half + layer
        return ((steps.index(j) * 2 + kind) * 2 + half) * 2 + layer

    def columns(load):
        listed = []
        for j in steps:
            wraps = jnp.where(x + j >= LINE, 1, 0)
            for upper in (wraps, 1 - wraps):
                for layer in (core, 1 - core):
                    listed.append(load(j, upper, layer))
        if closing:
            listed += [load(0, 2, core), load(0, 2, 1 - core)]
        return jnp.concatenate(listed, 0)

    def fetch(number):
        slot = number % 2
        for key, (name, index) in units.items():
            pltpu.make_async_copy(
                array_refs[name].at[index, pl.ds(number * STEP, STEP)],
                rows_ref.at[slot, unit_at(*key)],
                sems.at[slot],
            ).start()

    @pl.when(step == 0)
    def begin():
        fetch(0)
        pltpu.make_async_copy(table_ref.at[rank], weights_ref, sems.at[3]).start()
        for (j, kind, half, layer), (name, index) in units.items():
            if half == 0:
                pltpu.make_async_copy(
                    array_refs[name].at[index, GROUPS],
                    flags_ref.at[unit_at(j, kind, 0, layer) // 4 * 2 + layer],
                    sems.at[2],
                ).start()
        pltpu.make_async_copy(flags_ref, flags_ref, sems.at[2]).wait()
        counts = lax.dot_general(
            own_ref[0],
            columns(lambda j, kind, layer: flags_ref[unit_at(j, kind, 0, layer) // 4 * 2 + layer]),
            (((1,), (1,)), ((), ())),
            preferred_element_type=jnp.float32,
        )
        inverse = 1.0 / jnp.maximum(counts, 1.0)
        column = lax.broadcasted_iota(jnp.int32, (CH, 64), 1)
        channel = lax.broadcasted_iota(jnp.int32, (CH, 64), 0)
        parts = []
        for n in range(2 * len(steps)):
            offset = steps[n // 2] + 4 * (n % 2)
            part = jnp.where(chip + offset < chips, inverse[:, 64 * n : 64 * n + 64], 0.0)
            if offset == 0:
                after = jnp.where(chip + 8 < chips, inverse[:, width : width + 64], 0.0)
                part = jnp.where(column >= 32 * core + channel, part, after)
            parts.append(part)
        whole = jnp.concatenate(parts, 1)
        for c in range(CH):
            inverse_ref[c] = whole[c : c + 1]

    @pl.when(step < corr_steps)
    def correlate():
        @pl.when(step + 1 < corr_steps)
        def ahead():
            fetch(step + 1)

        slot = step % 2
        pltpu.make_async_copy(rows_ref.at[slot], rows_ref.at[slot], sems.at[slot]).wait()
        lane_bin = lax.broadcasted_iota(jnp.int32, (GROUP, DEPTH), 1) % GROUP
        own_bin = lane_bin == lax.broadcasted_iota(jnp.int32, (GROUP, DEPTH), 0)
        column = lax.broadcasted_iota(jnp.int32, (GROUP, 128), 1)

        def one_group(index, carry):
            for half in range(2):
                source = source_refs[half][index].astype(jnp.float32)
                real, imag = source[:, : DEPTH // 2], source[:, DEPTH // 2 :]
                source = jnp.concatenate(
                    [jnp.where(rank == 0, real, -imag), jnp.where(rank == 0, imag, real)], 1
                )
                for c in range(CH):
                    spread = jnp.broadcast_to(source[c : c + 1, :], (GROUP, DEPTH))
                    diagonal_ref[half, c * GROUP : (c + 1) * GROUP, :] = jnp.where(
                        own_bin, spread, 0.0
                    ).astype(jnp.bfloat16)
                product = lax.dot_general(
                    diagonal_ref[half],
                    columns(
                        lambda j, kind, layer: rows_ref[
                            slot, unit_at(j, kind, half, layer), index
                        ]
                    ),
                    (((1,), (1,)), ((), ())),
                    preferred_element_type=jnp.float32,
                )
                first_bin = pl.multiple_of(half * BINS + (step * STEP + index) * GROUP, GROUP)
                for c in range(CH):
                    part = product[c * GROUP : (c + 1) * GROUP]
                    here = pl.ds(c * FBINS + first_bin, GROUP)
                    if closing:
                        at = width - 128
                        tail = jnp.concatenate(
                            [part[:, width : width + 64], part[:, 64:128]], 1
                        )
                        head = jnp.where(column >= 32 * core + c, part[:, :128], tail)
                        part = jnp.concatenate([head, part[:, 128:width]], 1) if at else head
                    product_ref[here, :] = part.astype(jnp.bfloat16)
            return carry

        lax.fori_loop(0, STEP, one_group, 0, unroll=4)

    @pl.when(step >= corr_steps)
    def transform():
        lag_step = step - corr_steps

        @pl.when(lag_step == 0)
        def table_there():
            pltpu.make_async_copy(table_ref.at[rank], weights_ref, sems.at[3]).wait()

        def one_channel(index, carry):
            c = lag_step * CSTEP + index
            lags = jnp.dot(
                weights_ref[...],
                product_ref[pl.ds(pl.multiple_of(c * FBINS, FBINS), FBINS), :],
                preferred_element_type=jnp.float32,
            )
            lags = lags * inverse_ref[c]
            if not final:
                for n in range(len(steps)):
                    out_ref[n, index] = lags[:, 128 * n : 128 * n + 128].astype(jnp.bfloat16)
                return carry
            tiles = {j: lags[:, 128 * n : 128 * n + 128] for n, j in enumerate(steps)}
            for n, j in enumerate(earlier):
                tiles[j] = earlier_refs[n][0, index].astype(jnp.float32)
            shift = 32 * core + c
            low = [pltpu.roll(tiles[j], (128 - shift) % 128, 1) for j in range(LINE)]
            high = [pltpu.roll(tiles[j], 64 - shift, 1) for j in range(LINE)]
            lane = lax.broadcasted_iota(jnp.int32, (LAGS, 128), 1)
            first, second = lane < 64 - shift, lane < 128 - shift
            slot = c % 16
            for u, (one, two, three) in enumerate(
                (
                    (low[0], high[1], low[2]),
                    (low[2], high[3], high[0]),
                    (high[0], low[1], high[2]),
                    (high[2], low[3], low[0]),
                )
            ):
                value = jnp.where(first, one, jnp.where(second, two, three))
                result_ref[u, pl.ds(pl.multiple_of(slot * LAGS, LAGS), LAGS), :] = value
            return carry

        lax.fori_loop(0, CSTEP, one_channel, 0, unroll=4)
        if final:

            @pl.when(lag_step % (16 // CSTEP) == 16 // CSTEP - 1)
            def flush():
                for u in range(4):

                    def some_lags(number, carry, u=u):
                        at = pl.multiple_of(number * 8, 8)
                        block = jnp.stack(
                            [result_ref[u, pl.ds(n * LAGS + at, 8), :] for n in range(16)]
                        )
                        out_ref[pl.ds(at, 8), :, u * 128 : u * 128 + 128] = jnp.swapaxes(
                            block, 0, 1
                        ).astype(jnp.bfloat16)
                        return carry

                    lax.fori_loop(0, LAGS // 8, some_lags, 0, unroll=4)


def piece(place, own, sources, steps, arrays, units, weights, earlier=None):
    final = earlier is not None
    width = 128 * len(steps)
    rows = width + 64 * (0 in steps)
    corr_steps = GROUPS // STEP
    lag_steps = CH // CSTEP
    names = sorted({unit[0] for unit in units.values()})

    def lag_at(i):
        return jnp.maximum(i - corr_steps, 0)

    source_spec = pl.BlockSpec((STEP, CH, DEPTH), lambda i: (jnp.minimum(i, corr_steps - 1), 0, 0))
    in_specs = [pl.BlockSpec(memory_space=pltpu.SMEM)]
    in_specs += [pl.BlockSpec((1, CH, DEPTH), lambda i: (GROUPS, 0, 0))]
    in_specs += [source_spec] * 2
    in_specs += [pl.BlockSpec(memory_space=pl.ANY)] * len(names)
    in_specs += [pl.BlockSpec(memory_space=pl.ANY)]
    scratch = [
        pltpu.VMEM((2, rows // 16, STEP, CH, DEPTH), jnp.bfloat16),
        pltpu.VMEM((rows // 32, CH, DEPTH), jnp.bfloat16),
        pltpu.VMEM((2, CH * GROUP, DEPTH), jnp.bfloat16),
        pltpu.VMEM((CH * FBINS, width), jnp.bfloat16),
        pltpu.VMEM((CH, 1, width), jnp.float32),
        pltpu.VMEM((LAGS, FBINS), jnp.bfloat16),
        pltpu.SemaphoreType.DMA((4,)),
    ]
    operands = [place, own, *sources, *(arrays[name] for name in names), weights]
    if final:
        for j in range(LINE):
            if j not in steps:
                array, index = earlier[j]
                operands.append(array)
                in_specs.append(
                    pl.BlockSpec(
                        (1, CSTEP, LAGS, 128), lambda i, index=index: (index, lag_at(i), 0, 0)
                    )
                )
        scratch += [pltpu.VMEM((4, LAGS * 16, 128), jnp.float32)]
        out_shape = jax.ShapeDtypeStruct((LAGS, CH, BAND), jnp.bfloat16)
        out_specs = pl.BlockSpec((LAGS, 16, BAND), lambda i: (0, lag_at(i) * CSTEP // 16, 0))
    else:
        out_shape = jax.ShapeDtypeStruct((len(steps), CH, LAGS, 128), jnp.bfloat16)
        out_specs = pl.BlockSpec((len(steps), CSTEP, LAGS, 128), lambda i: (0, lag_at(i), 0, 0))
    flops = 2 * CH * FBINS * rows * (DEPTH + LAGS)
    moved_bytes = 4 * rows * BINS * DEPTH // GROUP + 2 * CH * LAGS * width
    return pl.pallas_call(
        lambda *refs: piece_kernel(steps, units, final, *refs),
        grid=(corr_steps + lag_steps,),
        out_shape=out_shape,
        in_specs=in_specs,
        out_specs=out_specs,
        scratch_shapes=scratch,
        compiler_params=pltpu.CompilerParams(
            vmem_limit_bytes=VMEM, dimension_semantics=("arbitrary",)
        ),
        cost_estimate=pl.CostEstimate(flops=flops, bytes_accessed=moved_bytes, transcendentals=0),
        name="piece_" + "_".join(map(str, steps)),
    )(*operands)


def lag_table():
    lag_index = np.arange(LAGS, dtype=np.int64)
    tables = []
    for rank in range(2):
        freq_index = (np.arange(FBINS, dtype=np.int64) + rank * BINS) % FBINS
        angles = (lag_index[:, None] * freq_index[None, :] % NFFT) * (2.0 * math.pi / NFFT)
        values = -np.sin(angles) if rank else np.cos(angles)
        tables.append((values * FBINS ** (-0.5)).astype(np.float32).astype(ml_dtypes.bfloat16))
    return np.stack(tables)


BARRIERS = ()
PIECES = ((0, 1, 2, 3),)
SWAPS = "stack"


def held_back(number, *values):
    return lax.optimization_barrier(values) if number in BARRIERS else values


def local(spectra, seg_mask):
    chan = lax.axis_index("chan")
    rank = lax.axis_index("freq")
    core, x, row = chan % 2, chan // 2 % LINE, chan // (2 * LINE) % ROWS
    place = jnp.stack([core, x, chan // 2, jnp.int32(lax.axis_size("chan") // 2), rank]).astype(jnp.int32)
    edge = jnp.where(rank == 0, spectra[..., BINS - 128 :], spectra[..., :128])
    rim = moved(edge, freq=1)
    own = whiten(rank.astype(jnp.int32).reshape(1), spectra, rim, seg_mask)

    other = {}

    def swap(blocks):
        if SWAPS == "stack":
            both = moved(jnp.stack(list(blocks.values())), core=1)
            for n, key in enumerate(blocks):
                other[key] = (both, n)
        else:
            for key, block in blocks.items():
                other[key] = (moved(block, core=1)[None], 0)

    after = moved(own, (1, 0, 0))
    flip = moved(own, freq=1)
    own_, after, flip = held_back(0, own, after, flip)
    along = {j: moved(jnp.where(x >= j, own_, after), (0, 0, j)) for j in (1, 3, 2)}
    crossing = jnp.where(row == 1, own_, after)
    cross = {0: moved(crossing, (0, 1, 0))}
    cross_flip = {0: moved(crossing, (0, 1, 0), freq=1)}
    after_flip = moved(flip, (1, 0, 0))
    (along, cross, cross_flip, after_flip) = held_back(1, along, cross, cross_flip, after_flip)
    along[0] = own
    along_flip = {0: flip}
    swap(
        {
            (0, 0, 0): own,
            (0, 0, 1): flip,
            (0, 1, 0): cross[0],
            (0, 1, 1): cross_flip[0],
            (0, 2, 0): after,
            (0, 2, 1): after_flip,
        }
    )
    for j in (1, 3):
        cross[j] = moved(cross[0], (0, 0, j))
        cross_flip[j] = moved(cross_flip[0], (0, 0, j))
        along_flip[j] = moved(along[j], freq=1)
    kept = {key: array for key, (array, index) in other.items()}
    cross, cross_flip, along_flip, kept = held_back(2, cross, cross_flip, along_flip, kept)
    for key, array in kept.items():
        other[key] = (array, other[key][1])
    swap(
        {
            (j, kind, half): blocks[j]
            for j in (1, 3)
            for kind, half, blocks in (
                (0, 0, along),
                (0, 1, along_flip),
                (1, 0, cross),
                (1, 1, cross_flip),
            )
        }
    )
    cross[2] = moved(cross[1], (0, 0, 1))
    cross_flip[2] = moved(cross_flip[3], (0, 0, 3))
    along_flip[2] = moved(along[2], freq=1)
    swap(
        {
            (2, 0, 0): along[2],
            (2, 0, 1): along_flip[2],
            (2, 1, 0): cross[2],
            (2, 1, 1): cross_flip[2],
        }
    )
    weights = jnp.asarray(lag_table())
    sources = [own, flip]
    mine = {(0, 2, 0): after, (0, 2, 1): after_flip}
    for j in range(LINE):
        mine[j, 0, 0], mine[j, 0, 1] = along[j], along_flip[j]
        mine[j, 1, 0], mine[j, 1, 1] = cross[j], cross_flip[j]

    def part(steps, earlier=None):
        arrays, units, known = {}, {}, {}
        for key in mine:
            if key[0] not in steps:
                continue
            for layer, (array, index) in enumerate(((mine[key][None], 0), other[key])):
                name = known.setdefault(id(array) if layer else key, len(known))
                arrays[name] = array
                units[(*key, layer)] = (name, index)
        return piece(place, own, sources, steps, arrays, units, weights, earlier)

    earlier = {}
    for steps in PIECES[:-1]:
        array = part(steps)
        for n, j in enumerate(steps):
            earlier[j] = (array, n)
    return part(PIECES[-1], earlier)[None]


def solution(mesh):
    placed = (P(None, None, "chan", "freq"), P("chan", None))
    return jax.shard_map(
        local, mesh=mesh, in_specs=placed, out_specs=P("freq", None, "chan", None), check_vma=False
    )
```

time: 868 us -> 172 us (0.20)
  waiting for transfers between devices: 370 us -> 75 us
  local copies, waits for them, and re-layouts: 225 us -> 15.7 us
  matrix products: 123 us -> 0 us
  other arithmetic: 61.5 us -> 2.64 us
  Pallas kernels: 0 us -> 41.6 us
  starting transfers between devices: 70.3 us -> 36.7 us
  between operations: 13.6 us -> 0.27 us
    reduce_scatter x1 -> x0, waiting for transfers between devices: 258 us -> none  [local(): lax.psum_scatter(jnp.stack(results).astype(jnp.bfloat16), 'freq', scatter...]
    dot_general x17 -> x0, matrix products: 123 us -> none  [the longest x8 79 us: add_block(): jnp.dot(weights, spectrum, preferred_element_type=jnp.float32)]
    convert_element_type x8 -> x0, local copies, waits for them, and re-layouts: 68.7 us -> none  [add_block(): scaled = (product * inverse[None]).astype(jnp.bfloat16)]
    another operation x6 -> x1, other arithmetic: 43.4 us -> 0.27 us  [swap(): both = moved(jnp.stack(list(blocks.values())), core=1)]
    reshape x9 -> x0, local copies, waits for them, and re-layouts: 43 us -> none  [the longest x8 42.9 us: band_rows(): return padded.reshape(leading + (height, breadth + 1))[..., :band]]
    pad x8 -> x0, local copies, waits for them, and re-layouts: 42.1 us -> none  [band_rows(): padded = jnp.pad(flattened, [(0, 0)] * len(leading) + [(0, height)])]
    pallas_call x0 -> x2, Pallas kernels: none -> 41.6 us  [the longest x1 38.5 us: piece(): pl.pallas_call(lambda *refs: piece_kernel(steps, units, final, *refs), gr...]
    ppermute x34 -> x21, waiting for transfers between devices: 111 us -> 75 us  [moved(): return lax.ppermute(value, AXES, pairs)]
  transfers between devices with their start and end apart: 35 -> 21, of which waited for: 18 -> 9; matrix products, arithmetic and copies ran while one was open for 0% -> 8% of each run, Pallas kernels for 0% -> 0%
where the time goes in v1:
time: 172 us
  waiting for transfers between devices  75 us (44%)
  Pallas kernels  41.6 us (24%)
  starting transfers between devices  36.7 us (21%)
  local copies, waits for them, and re-layouts  15.7 us (9%)
  other arithmetic  2.64 us (2%)
    ppermute x21, waiting for transfers between devices, moved(): return lax.ppermute(value, AXES, pairs)  75 us
    pallas_call x1, Pallas kernels, piece(): pl.pallas_call(lambda *refs: piece_kernel(steps, units, final, *refs), gr...  38.5 us
    ppermute x21, starting transfers between devices, moved(): return lax.ppermute(value, AXES, pairs)  36.7 us
    unnamed x51, local copies, waits for them, and re-layouts  13.3 us
  transfers between devices with their start and end apart: 21, of which 9 were waited for; matrix products, arithmetic and copies ran while one was open for 8% of the time, Pallas kernels for 0%

profile of v1, /device:TPU:1, one launch (start us, length us, event | category | flops | bytes accessed | tf_op | source)
XLA Modules:
  0.0 172.0 jit_solution(9418153847977714973)
XLA Ops:
  0.0 1.0 slice_select_fusion
  1.0 3.8 %collective-permute-start = (bf16[2,8,32,128]{3,2,1,0:T(8,128)(2,1)S(1)}, bf16[2,8,32,128]{3,2,1,0:T(8,128)(2,1)S(1)}, u32[]{:S(2)}, u32[]{:S(2)}) collective-permute-start(bf16[2,8,32,128]{3,2,1,0:T(8,128)(2,1)S(1)} %slice_select_fusion), channel_id=1, source_target_pairs={{0,1},{1,0},{2,3},{3,2},{4,5},{5,4},{6,7},{7,6},{8,9},{9,8},{10,11... | collective-permute-start | bytes 393224 | tf_op jit(solution)/shard_map/ppermute | solution.py:44
  4.8 1.4 copy.4.mask_ref
  6.2 1.0 collective-permute-done.rim_ref
  7.8 3.1 %whiten.1.refs_1_.refs_2_ = bf16[33,32,256]{2,1,0:T(8,128)(2,1)} custom-call(s32[1]{0:T(128)} %bitcast.3.rank_ref, bf16[2,8,32,512]{3,2,1,0:T(8,128)(2,1)} %spectra_ref.1, bf16[2,8,32,128]{3,2,1,0:T(8,128)(2,1)} %copy-done.18, s32[32,8]{1,0:T(8,128)} %copy.4.mask_ref), custom_call_target="tpu_custom_call" | custom-call | tf_op jit(solution)/shard_map/whiten/pallas_call | solution.py:101
  11.0 6.2 %collective-permute-start.2 = (bf16[33,32,256]{2,1,0:T(8,128)(2,1)}, bf16[33,32,256]{2,1,0:T(8,128)(2,1)S(1)}, u32[]{:S(2)}, u32[]{:S(2)}) collective-permute-start(bf16[33,32,256]{2,1,0:T(8,128)(2,1)} %whiten.1.refs_1_.refs_2_), channel_id=1, source_target_pairs={{0,224},{1,225},{2,226},{3,227},{4,228},{5,229},{6,230},{7,231},{8... | collective-permute-start | bytes 1622024 | tf_op jit(solution)/shard_map/ppermute | solution.py:44
  17.2 10.3 %collective-permute-done.2 = bf16[33,32,256]{2,1,0:T(8,128)(2,1)S(1)} collective-permute-done((bf16[33,32,256]{2,1,0:T(8,128)(2,1)}, bf16[33,32,256]{2,1,0:T(8,128)(2,1)S(1)}, u32[]{:S(2)}, u32[]{:S(2)}) %collective-permute-start.2) | collective-permute-done | bytes 540704 | tf_op jit(solution)/shard_map/ppermute | solution.py:44
  27.5 1.4 broadcast_select_fusion
  28.9 2.6 %collective-permute-start.7 = (bf16[33,32,256]{2,1,0:T(8,128)(2,1)S(1)}, bf16[33,32,256]{2,1,0:T(8,128)(2,1)S(1)}, u32[]{:S(2)}, u32[]{:S(2)}) collective-permute-start(bf16[33,32,256]{2,1,0:T(8,128)(2,1)S(1)} %get-tuple-element.7), channel_id=1, source_target_pairs={{0,12},{1,13},{2,14},{3,15},{4,0},{5,1},{6,2},{7,3},{8,4},{9,5},{1... | collective-permute-start | bytes 1622024 | tf_op jit(solution)/shard_map/ppermute | solution.py:44
  31.4 1.3 collective-permute-start.3
  32.7 1.9 %collective-permute-start.4 = (bf16[33,32,256]{2,1,0:T(8,128)(2,1)S(1)}, bf16[33,32,256]{2,1,0:T(8,128)(2,1)S(1)}, u32[]{:S(2)}, u32[]{:S(2)}) collective-permute-start(bf16[33,32,256]{2,1,0:T(8,128)(2,1)S(1)} %get-tuple-element.8), channel_id=1, source_target_pairs={{0,17},{1,16},{2,19},{3,18},{4,21},{5,20},{6,23},{7,22},{8,25},{9,... | collective-permute-start | bytes 1622024 | tf_op jit(solution)/shard_map/ppermute | solution.py:44
  35.4 5.2 %collective-permute-done.7 = bf16[33,32,256]{2,1,0:T(8,128)(2,1)S(1)} collective-permute-done((bf16[33,32,256]{2,1,0:T(8,128)(2,1)S(1)}, bf16[33,32,256]{2,1,0:T(8,128)(2,1)S(1)}, u32[]{:S(2)}, u32[]{:S(2)}) %collective-permute-start.7) | collective-permute-done | bytes 540704 | tf_op jit(solution)/shard_map/ppermute | solution.py:44
  40.5 2.9 %collective-permute-start.8 = (bf16[33,32,256]{2,1,0:T(8,128)(2,1)S(1)}, bf16[33,32,256]{2,1,0:T(8,128)(2,1)S(1)}, u32[]{:S(2)}, u32[]{:S(2)}) collective-permute-start(bf16[33,32,256]{2,1,0:T(8,128)(2,1)S(1)} %collective-permute-done.7), channel_id=1, source_target_pairs={{0,1},{1,0},{2,3},{3,2},{4,5},{5,4},{6,7},{7,6},{8,9},{9,8},{10,11... | collective-permute-start | bytes 1622024 | tf_op jit(solution)/shard_map/ppermute | solution.py:44
  43.4 0.9 collective-permute-start.11
  44.4 2.6 %collective-permute-start.9 = (bf16[33,32,256]{2,1,0:T(8,128)(2,1)S(1)}, bf16[33,32,256]{2,1,0:T(8,128)(2,1)S(1)}, u32[]{:S(2)}, u32[]{:S(2)}) collective-permute-start(bf16[33,32,256]{2,1,0:T(8,128)(2,1)S(1)} %collective-permute-done.3), channel_id=1, source_target_pairs={{0,12},{1,13},{2,14},{3,15},{4,0},{5,1},{6,2},{7,3},{8,4},{9,5},{1... | collective-permute-start | bytes 1622024 | tf_op jit(solution)/shard_map/ppermute | solution.py:44
  46.9 0.9 constant_dynamic-update-slice_fusion.5
  47.8 1.4 collective-permute-start.10
  50.1 6.4 %collective-permute-done.1.refs_3_ = bf16[33,32,256]{2,1,0:T(8,128)(2,1)S(1)} collective-permute-done((bf16[33,32,256]{2,1,0:T(8,128)(2,1)S(1)}, bf16[33,32,256]{2,1,0:T(8,128)(2,1)S(1)}, u32[]{:S(2)}, u32[]{:S(2)}) %collective-permute-start.1) | collective-permute-done | bytes 540704 | tf_op jit(solution)/shard_map/ppermute | solution.py:44
  57.0 11.1 %collective-permute-done.8 = bf16[33,32,256]{2,1,0:T(8,128)(2,1)S(1)} collective-permute-done((bf16[33,32,256]{2,1,0:T(8,128)(2,1)S(1)}, bf16[33,32,256]{2,1,0:T(8,128)(2,1)S(1)}, u32[]{:S(2)}, u32[]{:S(2)}) %collective-permute-start.8) | collective-permute-done | bytes 540704 | tf_op jit(solution)/shard_map/ppermute | solution.py:44
  68.1 3.3 %collective-permute-start.5 = (bf16[33,32,256]{2,1,0:T(8,128)(2,1)S(1)}, bf16[33,32,256]{2,1,0:T(8,128)(2,1)S(1)}, u32[]{:S(2)}, u32[]{:S(2)}) collective-permute-start(bf16[33,32,256]{2,1,0:T(8,128)(2,1)S(1)} %collective-permute-done.1.refs_3_), channel_id=1, source_target_pairs={{0,224},{1,225},{2,226},{3,227},{4,228},{5,229},{6,230},{7,231},{8... | collective-permute-start | bytes 1622024 | tf_op jit(solution)/shard_map/ppermute | solution.py:44
  75.4 7.0 %collective-permute-done.12 = bf16[33,32,256]{2,1,0:T(8,128)(2,1)S(1)} collective-permute-done((bf16[33,32,256]{2,1,0:T(8,128)(2,1)S(1)}, bf16[33,32,256]{2,1,0:T(8,128)(2,1)S(1)}, u32[]{:S(2)}, u32[]{:S(2)}) %collective-permute-start.12) | collective-permute-done | bytes 540704 | tf_op jit(solution)/shard_map/ppermute | solution.py:44
  82.3 0.9 constant_dynamic-update-slice_fusion.8
  83.3 18.9 %collective-permute-done.13 = bf16[33,32,256]{2,1,0:T(8,128)(2,1)S(1)} collective-permute-done((bf16[33,32,256]{2,1,0:T(8,128)(2,1)S(1)}, bf16[33,32,256]{2,1,0:T(8,128)(2,1)S(1)}, u32[]{:S(2)}, u32[]{:S(2)}) %collective-permute-start.13) | collective-permute-done | bytes 540704 | tf_op jit(solution)/shard_map/ppermute | solution.py:44
  102.1 0.9 constant_dynamic-update-slice_fusion.7
  103.9 3.4 %collective-permute-start.15 = (bf16[8,33,32,256]{3,2,1,0:T(8,128)(2,1)}, bf16[8,33,32,256]{3,2,1,0:T(8,128)(2,1)}, u32[]{:S(2)}, u32[]{:S(2)}) collective-permute-start(bf16[8,33,32,256]{3,2,1,0:T(8,128)(2,1)} %constant_dynamic-update-slice_fusion.6), channel_id=1, source_target_pairs={{0,2},{1,3},{2,0},{3,1},{4,6},{5,7},{6,4},{7,5},{8,10},{9,11},{10,... | collective-permute-start | bytes 12976136 | tf_op jit(solution)/shard_map/ppermute | solution.py:44
  107.3 0.9 constant_dynamic-update-slice_fusion.4
  110.8 0.9 constant_dynamic-update-slice_fusion
  112.2 2.7 %collective-permute-start.18 = (bf16[33,32,256]{2,1,0:T(8,128)(2,1)S(1)}, bf16[33,32,256]{2,1,0:T(8,128)(2,1)S(1)}, u32[]{:S(2)}, u32[]{:S(2)}) collective-permute-start(bf16[33,32,256]{2,1,0:T(8,128)(2,1)S(1)} %collective-permute-done.9), channel_id=1, source_target_pairs={{0,12},{1,13},{2,14},{3,15},{4,0},{5,1},{6,2},{7,3},{8,4},{9,5},{1... | collective-permute-start | bytes 1622024 | tf_op jit(solution)/shard_map/ppermute | solution.py:44
  114.9 11.9 %collective-permute-done.17 = bf16[33,32,256]{2,1,0:T(8,128)(2,1)S(1)} collective-permute-done((bf16[33,32,256]{2,1,0:T(8,128)(2,1)S(1)}, bf16[33,32,256]{2,1,0:T(8,128)(2,1)S(1)}, u32[]{:S(2)}, u32[]{:S(2)}) %collective-permute-start.17) | collective-permute-done | bytes 540704 | tf_op jit(solution)/shard_map/ppermute | solution.py:44
  127.9 1.5 collective-permute-start.20
  130.0 3.3 %collective-permute-done.20.refs_17_ = bf16[4,33,32,256]{3,2,1,0:T(8,128)(2,1)} collective-permute-done((bf16[4,33,32,256]{3,2,1,0:T(8,128)(2,1)S(1)}, bf16[4,33,32,256]{3,2,1,0:T(8,128)(2,1)}, u32[]{:S(2)}, u32[]{:S(2)}) %collective-permute-start.20) | collective-permute-done | bytes 2162720 | tf_op jit(solution)/shard_map/ppermute | solution.py:44
  133.4 38.5 %piece_0_1_2_3.1 = bf16[256,32,512]{2,1,0:T(8,128)(2,1)} custom-call(s32[5]{0:T(128)} %stack.76.refs_0_, bf16[33,32,256]{2,1,0:T(8,128)(2,1)} %whiten.1.refs_1_.refs_2_, bf16[33,32,256]{2,1,0:T(8,128)(2,1)} %whiten.1.refs_1_.refs_2_, bf16[33,32,256]{2,1,0:T(8,128)(2,1)} %copy-done.9, bf16[1,33,32,256]{3,2,1,0:T(8,128)(2,1)} %bitcast.38, ...), custom_call_target="tpu_custom_call" | custom-call | flops 19327352832 | bytes 27262976 | tf_op jit(solution)/shard_map/piece_0_1_2_3/pallas_call | solution.py:344
  (69 shorter events, 12.5 us)
Async XLA Ops:
  1.0 6.2 %collective-permute-start = (bf16[2,8,32,128]{3,2,1,0:T(8,128)(2,1)S(1)}, bf16[2,8,32,128]{3,2,1,0:T(8,128)(2,1)S(1)}, u32[]{:S(2)}, u32[]{:S(2)}) collective-permute-start(bf16[2,8,32,128]{3,2,1,0:T(8,128)(2,1)S(1)} %slice_select_fusion), channel_id=1, source_target_pairs={{0,1},{1,0},{2,3},{3,2},{4,5},{5,4},{6,7},{7,6},{8,9},{9,8},{10,11... | collective-permute-start | bytes 393224 | tf_op jit(solution)/shard_map/ppermute | solution.py:44
  11.0 23.7 %copy-start = (bf16[33,32,256]{2,1,0:T(8,128)(2,1)S(1)}, bf16[33,32,256]{2,1,0:T(8,128)(2,1)}, u32[]{:S(2)}) copy-start(bf16[33,32,256]{2,1,0:T(8,128)(2,1)} %whiten.1.refs_1_.refs_2_) | copy-start | bytes 1622020
  11.0 16.5 %collective-permute-start.2 = (bf16[33,32,256]{2,1,0:T(8,128)(2,1)}, bf16[33,32,256]{2,1,0:T(8,128)(2,1)S(1)}, u32[]{:S(2)}, u32[]{:S(2)}) collective-permute-start(bf16[33,32,256]{2,1,0:T(8,128)(2,1)} %whiten.1.refs_1_.refs_2_), channel_id=1, source_target_pairs={{0,224},{1,225},{2,226},{3,227},{4,228},{5,229},{6,230},{7,231},{8... | collective-permute-start | bytes 1622024 | tf_op jit(solution)/shard_map/ppermute | solution.py:44
  27.5 82.4 %copy-start.1 = (bf16[33,32,256]{2,1,0:T(8,128)(2,1)}, bf16[33,32,256]{2,1,0:T(8,128)(2,1)S(1)}, u32[]{:S(2)}) copy-start(bf16[33,32,256]{2,1,0:T(8,128)(2,1)S(1)} %collective-permute-done.2) | copy-start | bytes 1622020
  28.9 11.7 %collective-permute-start.7 = (bf16[33,32,256]{2,1,0:T(8,128)(2,1)S(1)}, bf16[33,32,256]{2,1,0:T(8,128)(2,1)S(1)}, u32[]{:S(2)}, u32[]{:S(2)}) collective-permute-start(bf16[33,32,256]{2,1,0:T(8,128)(2,1)S(1)} %get-tuple-element.7), channel_id=1, source_target_pairs={{0,12},{1,13},{2,14},{3,15},{4,0},{5,1},{6,2},{7,3},{8,4},{9,5},{1... | collective-permute-start | bytes 1622024 | tf_op jit(solution)/shard_map/ppermute | solution.py:44
  31.4 12.9 %collective-permute-start.3 = (bf16[33,32,256]{2,1,0:T(8,128)(2,1)S(1)}, bf16[33,32,256]{2,1,0:T(8,128)(2,1)S(1)}, u32[]{:S(2)}, u32[]{:S(2)}) collective-permute-start(bf16[33,32,256]{2,1,0:T(8,128)(2,1)S(1)} %get-tuple-element.8), channel_id=1, source_target_pairs={{0,16},{1,17},{2,18},{3,19},{4,20},{5,21},{6,22},{7,23},{8,24},{9,... | collective-permute-start | bytes 1622024 | tf_op jit(solution)/shard_map/ppermute | solution.py:44
  32.7 15.1 %collective-permute-start.4 = (bf16[33,32,256]{2,1,0:T(8,128)(2,1)S(1)}, bf16[33,32,256]{2,1,0:T(8,128)(2,1)S(1)}, u32[]{:S(2)}, u32[]{:S(2)}) collective-permute-start(bf16[33,32,256]{2,1,0:T(8,128)(2,1)S(1)} %get-tuple-element.8), channel_id=1, source_target_pairs={{0,17},{1,16},{2,19},{3,18},{4,21},{5,20},{6,23},{7,22},{8,25},{9,... | collective-permute-start | bytes 1622024 | tf_op jit(solution)/shard_map/ppermute | solution.py:44
  34.6 21.9 %collective-permute-start.1 = (bf16[33,32,256]{2,1,0:T(8,128)(2,1)S(1)}, bf16[33,32,256]{2,1,0:T(8,128)(2,1)S(1)}, u32[]{:S(2)}, u32[]{:S(2)}) collective-permute-start(bf16[33,32,256]{2,1,0:T(8,128)(2,1)S(1)} %copy-done), channel_id=1, source_target_pairs={{0,1},{1,0},{2,3},{3,2},{4,5},{5,4},{6,7},{7,6},{8,9},{9,8},{10,11... | collective-permute-start | bytes 1622024 | tf_op jit(solution)/shard_map/ppermute | solution.py:44
  40.5 34.9 %copy-start.6 = (bf16[33,32,256]{2,1,0:T(8,128)(2,1)}, bf16[33,32,256]{2,1,0:T(8,128)(2,1)S(1)}, u32[]{:S(2)}) copy-start(bf16[33,32,256]{2,1,0:T(8,128)(2,1)S(1)} %collective-permute-done.7) | copy-start | bytes 1622020
  40.5 27.6 %collective-permute-start.8 = (bf16[33,32,256]{2,1,0:T(8,128)(2,1)S(1)}, bf16[33,32,256]{2,1,0:T(8,128)(2,1)S(1)}, u32[]{:S(2)}, u32[]{:S(2)}) collective-permute-start(bf16[33,32,256]{2,1,0:T(8,128)(2,1)S(1)} %collective-permute-done.7), channel_id=1, source_target_pairs={{0,1},{1,0},{2,3},{3,2},{4,5},{5,4},{6,7},{7,6},{8,9},{9,8},{10,11... | collective-permute-start | bytes 1622024 | tf_op jit(solution)/shard_map/ppermute | solution.py:44
  43.4 28.8 %collective-permute-start.11 = (bf16[33,32,256]{2,1,0:T(8,128)(2,1)S(1)}, bf16[33,32,256]{2,1,0:T(8,128)(2,1)S(1)}, u32[]{:S(2)}, u32[]{:S(2)}) collective-permute-start(bf16[33,32,256]{2,1,0:T(8,128)(2,1)S(1)} %get-tuple-element.6), channel_id=1, source_target_pairs={{0,4},{1,5},{2,6},{3,7},{4,8},{5,9},{6,10},{7,11},{8,12},{9,13},{1... | collective-permute-start | bytes 1622024 | tf_op jit(solution)/shard_map/ppermute | solution.py:44
  44.4 63.8 %copy-start.7 = (bf16[33,32,256]{2,1,0:T(8,128)(2,1)}, bf16[33,32,256]{2,1,0:T(8,128)(2,1)S(1)}, u32[]{:S(2)}) copy-start(bf16[33,32,256]{2,1,0:T(8,128)(2,1)S(1)} %collective-permute-done.3) | copy-start | bytes 1622020
  44.4 27.9 %collective-permute-start.9 = (bf16[33,32,256]{2,1,0:T(8,128)(2,1)S(1)}, bf16[33,32,256]{2,1,0:T(8,128)(2,1)S(1)}, u32[]{:S(2)}, u32[]{:S(2)}) collective-permute-start(bf16[33,32,256]{2,1,0:T(8,128)(2,1)S(1)} %collective-permute-done.3), channel_id=1, source_target_pairs={{0,12},{1,13},{2,14},{3,15},{4,0},{5,1},{6,2},{7,3},{8,4},{9,5},{1... | collective-permute-start | bytes 1622024 | tf_op jit(solution)/shard_map/ppermute | solution.py:44
  47.8 61.2 %copy-start.8 = (bf16[33,32,256]{2,1,0:T(8,128)(2,1)}, bf16[33,32,256]{2,1,0:T(8,128)(2,1)S(1)}, u32[]{:S(2)}) copy-start(bf16[33,32,256]{2,1,0:T(8,128)(2,1)S(1)} %collective-permute-done.4) | copy-start | bytes 1622020
  47.8 25.7 %collective-permute-start.10 = (bf16[33,32,256]{2,1,0:T(8,128)(2,1)S(1)}, bf16[33,32,256]{2,1,0:T(8,128)(2,1)S(1)}, u32[]{:S(2)}, u32[]{:S(2)}) collective-permute-start(bf16[33,32,256]{2,1,0:T(8,128)(2,1)S(1)} %collective-permute-done.4), channel_id=1, source_target_pairs={{0,12},{1,13},{2,14},{3,15},{4,0},{5,1},{6,2},{7,3},{8,4},{9,5},{1... | collective-permute-start | bytes 1622024 | tf_op jit(solution)/shard_map/ppermute | solution.py:44
  56.5 50.8 %copy-start.9 = (bf16[33,32,256]{2,1,0:T(8,128)(2,1)}, bf16[33,32,256]{2,1,0:T(8,128)(2,1)S(1)}, u32[]{:S(2)}) copy-start(bf16[33,32,256]{2,1,0:T(8,128)(2,1)S(1)} %collective-permute-done.1.refs_3_) | copy-start | bytes 1622020
  56.5 55.2 %collective-permute-start.16 = (bf16[33,32,256]{2,1,0:T(8,128)(2,1)S(1)}, bf16[33,32,256]{2,1,0:T(8,128)(2,1)S(1)}, u32[]{:S(2)}, u32[]{:S(2)}) collective-permute-start(bf16[33,32,256]{2,1,0:T(8,128)(2,1)S(1)} %get-tuple-element.5), channel_id=1, source_target_pairs={{0,8},{1,9},{2,10},{3,11},{4,12},{5,13},{6,14},{7,15},{8,0},{9,1},... | collective-permute-start | bytes 1622024 | tf_op jit(solution)/shard_map/ppermute | solution.py:44
  68.1 35.0 %copy-start.10 = (bf16[33,32,256]{2,1,0:T(8,128)(2,1)}, bf16[33,32,256]{2,1,0:T(8,128)(2,1)S(1)}, u32[]{:S(2)}) copy-start(bf16[33,32,256]{2,1,0:T(8,128)(2,1)S(1)} %collective-permute-done.8) | copy-start | bytes 1622020
  68.1 42.7 %collective-permute-start.5 = (bf16[33,32,256]{2,1,0:T(8,128)(2,1)S(1)}, bf16[33,32,256]{2,1,0:T(8,128)(2,1)S(1)}, u32[]{:S(2)}, u32[]{:S(2)}) collective-permute-start(bf16[33,32,256]{2,1,0:T(8,128)(2,1)S(1)} %collective-permute-done.1.refs_3_), channel_id=1, source_target_pairs={{0,224},{1,225},{2,226},{3,227},{4,228},{5,229},{6,230},{7,231},{8... | collective-permute-start | bytes 1622024 | tf_op jit(solution)/shard_map/ppermute | solution.py:44
  72.2 31.7 %copy-start.11 = (bf16[33,32,256]{2,1,0:T(8,128)(2,1)}, bf16[33,32,256]{2,1,0:T(8,128)(2,1)S(1)}, u32[]{:S(2)}) copy-start(bf16[33,32,256]{2,1,0:T(8,128)(2,1)S(1)} %collective-permute-done.11) | copy-start | bytes 1622020
  72.2 30.8 %collective-permute-start.14 = (bf16[33,32,256]{2,1,0:T(8,128)(2,1)S(1)}, bf16[33,32,256]{2,1,0:T(8,128)(2,1)S(1)}, u32[]{:S(2)}, u32[]{:S(2)}) collective-permute-start(bf16[33,32,256]{2,1,0:T(8,128)(2,1)S(1)} %collective-permute-done.4), channel_id=1, source_target_pairs={{0,4},{1,5},{2,6},{3,7},{4,8},{5,9},{6,10},{7,11},{8,12},{9,13},{1... | collective-permute-start | bytes 1622024 | tf_op jit(solution)/shard_map/ppermute | solution.py:44
  72.2 40.0 %copy-start.12 = (bf16[33,32,256]{2,1,0:T(8,128)(2,1)}, bf16[33,32,256]{2,1,0:T(8,128)(2,1)S(1)}, u32[]{:S(2)}) copy-start(bf16[33,32,256]{2,1,0:T(8,128)(2,1)S(1)} %collective-permute-done.9) | copy-start | bytes 1622020
  72.3 10.1 %collective-permute-start.12 = (bf16[33,32,256]{2,1,0:T(8,128)(2,1)S(1)}, bf16[33,32,256]{2,1,0:T(8,128)(2,1)S(1)}, u32[]{:S(2)}, u32[]{:S(2)}) collective-permute-start(bf16[33,32,256]{2,1,0:T(8,128)(2,1)S(1)} %collective-permute-done.11), channel_id=1, source_target_pairs={{0,1},{1,0},{2,3},{3,2},{4,5},{5,4},{6,7},{7,6},{8,9},{9,8},{10,11... | collective-permute-start | bytes 1622024 | tf_op jit(solution)/shard_map/ppermute | solution.py:44
  73.6 34.6 %copy-start.13 = (bf16[33,32,256]{2,1,0:T(8,128)(2,1)}, bf16[33,32,256]{2,1,0:T(8,128)(2,1)S(1)}, u32[]{:S(2)}) copy-start(bf16[33,32,256]{2,1,0:T(8,128)(2,1)S(1)} %collective-permute-done.10) | copy-start | bytes 1622020
  73.6 28.6 %collective-permute-start.13 = (bf16[33,32,256]{2,1,0:T(8,128)(2,1)S(1)}, bf16[33,32,256]{2,1,0:T(8,128)(2,1)S(1)}, u32[]{:S(2)}, u32[]{:S(2)}) collective-permute-start(bf16[33,32,256]{2,1,0:T(8,128)(2,1)S(1)} %collective-permute-done.3), channel_id=1, source_target_pairs={{0,4},{1,5},{2,6},{3,7},{4,8},{5,9},{6,10},{7,11},{8,12},{9,13},{1... | collective-permute-start | bytes 1622024 | tf_op jit(solution)/shard_map/ppermute | solution.py:44
  82.3 27.6 %copy-start.16 = (bf16[33,32,256]{2,1,0:T(8,128)(2,1)}, bf16[33,32,256]{2,1,0:T(8,128)(2,1)S(1)}, u32[]{:S(2)}) copy-start(bf16[33,32,256]{2,1,0:T(8,128)(2,1)S(1)} %collective-permute-done.12) | copy-start | bytes 1622020
  103.9 29.4 %collective-permute-start.15 = (bf16[8,33,32,256]{3,2,1,0:T(8,128)(2,1)}, bf16[8,33,32,256]{3,2,1,0:T(8,128)(2,1)}, u32[]{:S(2)}, u32[]{:S(2)}) collective-permute-start(bf16[8,33,32,256]{3,2,1,0:T(8,128)(2,1)} %constant_dynamic-update-slice_fusion.6), channel_id=1, source_target_pairs={{0,2},{1,3},{2,0},{3,1},{4,6},{5,7},{6,4},{7,5},{8,10},{9,11},{10,... | collective-permute-start | bytes 12976136 | tf_op jit(solution)/shard_map/ppermute | solution.py:44
  111.7 18.3 %collective-permute-start.6 = (bf16[6,33,32,256]{3,2,1,0:T(8,128)(2,1)}, bf16[6,33,32,256]{3,2,1,0:T(8,128)(2,1)}, u32[]{:S(2)}, u32[]{:S(2)}) collective-permute-start(bf16[6,33,32,256]{3,2,1,0:T(8,128)(2,1)} %constant_dynamic-update-slice_fusion), channel_id=1, source_target_pairs={{0,2},{1,3},{2,0},{3,1},{4,6},{5,7},{6,4},{7,5},{8,10},{9,11},{10,... | collective-permute-start | bytes 9732104 | tf_op jit(solution)/shard_map/ppermute | solution.py:44
  111.7 15.0 %collective-permute-start.17 = (bf16[33,32,256]{2,1,0:T(8,128)(2,1)S(1)}, bf16[33,32,256]{2,1,0:T(8,128)(2,1)S(1)}, u32[]{:S(2)}, u32[]{:S(2)}) collective-permute-start(bf16[33,32,256]{2,1,0:T(8,128)(2,1)S(1)} %collective-permute-done.16), channel_id=1, source_target_pairs={{0,1},{1,0},{2,3},{3,2},{4,5},{5,4},{6,7},{7,6},{8,9},{9,8},{10,11... | collective-permute-start | bytes 1622024 | tf_op jit(solution)/shard_map/ppermute | solution.py:44
  112.2 14.5 %collective-permute-start.19 = (bf16[33,32,256]{2,1,0:T(8,128)(2,1)S(1)}, bf16[33,32,256]{2,1,0:T(8,128)(2,1)S(1)}, u32[]{:S(2)}, u32[]{:S(2)}) collective-permute-start(bf16[33,32,256]{2,1,0:T(8,128)(2,1)S(1)} %collective-permute-done.14), channel_id=1, source_target_pairs={{0,4},{1,5},{2,6},{3,7},{4,8},{5,9},{6,10},{7,11},{8,12},{9,13},{1... | collective-permute-start | bytes 1622024 | tf_op jit(solution)/shard_map/ppermute | solution.py:44
  112.2 14.5 %collective-permute-start.18 = (bf16[33,32,256]{2,1,0:T(8,128)(2,1)S(1)}, bf16[33,32,256]{2,1,0:T(8,128)(2,1)S(1)}, u32[]{:S(2)}, u32[]{:S(2)}) collective-permute-start(bf16[33,32,256]{2,1,0:T(8,128)(2,1)S(1)} %collective-permute-done.9), channel_id=1, source_target_pairs={{0,12},{1,13},{2,14},{3,15},{4,0},{5,1},{6,2},{7,3},{8,4},{9,5},{1... | collective-permute-start | bytes 1622024 | tf_op jit(solution)/shard_map/ppermute | solution.py:44
  127.9 5.5 %collective-permute-start.20 = (bf16[4,33,32,256]{3,2,1,0:T(8,128)(2,1)S(1)}, bf16[4,33,32,256]{3,2,1,0:T(8,128)(2,1)}, u32[]{:S(2)}, u32[]{:S(2)}) collective-permute-start(bf16[4,33,32,256]{3,2,1,0:T(8,128)(2,1)S(1)} %pad_maximum_fusion), channel_id=1, source_target_pairs={{0,2},{1,3},{2,0},{3,1},{4,6},{5,7},{6,4},{7,5},{8,10},{9,11},{10,... | collective-permute-start | bytes 6488072 | tf_op jit(solution)/shard_map/ppermute | solution.py:44
  (8 other events, 64.7 us)

commit v2 on v0

v2 whole, which is shorter than its diff:
```python
import math

import jax
import jax.numpy as jnp
import ml_dtypes
import numpy as np
from jax import lax
from jax.experimental import pallas as pl
from jax.experimental.pallas import tpu as pltpu
from jax.sharding import PartitionSpec as P

BAND = 512
FBINS = 1024
HALF = 64
LAGS = 256
NFFT = 2048
EPSILON = 1e-06
SEGMENTS = 8
CH = 32
BINS = 512
GROUP = 16
GROUPS = BINS // GROUP
DEPTH = 2 * SEGMENTS * GROUP
STEP = 8
UNROLL = 8
BATCH = 16
CHUNK = 16
ROWS = 2
LINE = 4
CSTEP = 4
AXES = ("chan", "freq")
VMEM = 60 * 1024 * 1024
INTERPRET = False


def moved(value, back=(0, 0, 0), core=0, freq=0):
    count, halves = lax.axis_size("chan"), lax.axis_size("freq")
    planes = count // (ROWS * LINE * 2)
    pairs = []
    for index in range(count * halves):
        rest, f = divmod(index, halves)
        rest, k = divmod(rest, 2)
        rest, x = divmod(rest, LINE)
        z, y = divmod(rest, ROWS)
        z, y, x = (z - back[0]) % planes, (y - back[1]) % ROWS, (x - back[2]) % LINE
        pairs.append((index, (((z * ROWS + y) * LINE + x) * 2 + (k ^ core)) * halves + (f ^ freq)))
    return lax.ppermute(value, AXES, pairs)


def whiten_kernel(rank_ref, spectra_ref, rim_ref, mask_ref, out_ref):
    rank = rank_ref[0]
    real = spectra_ref[0].astype(jnp.float32)
    imag = spectra_ref[1].astype(jnp.float32)
    magnitude = jnp.sqrt(real * real + imag * imag).reshape(SEGMENTS * CH, BINS)
    rim_real = rim_ref[0].astype(jnp.float32)
    rim_imag = rim_ref[1].astype(jnp.float32)
    rim = jnp.sqrt(rim_real * rim_real + rim_imag * rim_imag).reshape(SEGMENTS * CH, 128)

    def window_sum(values, positions):
        target = lax.broadcasted_iota(jnp.int32, (values.shape[1], BINS), 1)
        near = jnp.abs(positions - target) <= HALF
        table = jnp.where(near, 1.0, 0.0).astype(jnp.bfloat16)
        high = values.astype(jnp.bfloat16)
        low = (values - high.astype(jnp.float32)).astype(jnp.bfloat16)
        return jnp.dot(high, table, preferred_element_type=jnp.float32) + jnp.dot(
            low, table, preferred_element_type=jnp.float32
        )

    inner = lax.broadcasted_iota(jnp.int32, (BINS, BINS), 0)
    outer = lax.broadcasted_iota(jnp.int32, (128, BINS), 0) + jnp.where(rank == 0, BINS, -128)
    summed = window_sum(magnitude, inner) + window_sum(rim, outer)
    bin_index = rank * BINS + lax.broadcasted_iota(jnp.int32, (1, BINS), 1)
    counted = (
        jnp.minimum(bin_index + HALF, FBINS - 1) - jnp.maximum(bin_index - HALF, 0) + 1
    ).astype(jnp.float32)
    levels = summed / counted + EPSILON
    scale = (1.0 / levels).reshape(SEGMENTS, CH, BINS)
    valid = mask_ref[...].astype(jnp.float32)
    out_ref[GROUPS] = jnp.concatenate(
        [valid, jnp.zeros((CH, DEPTH - SEGMENTS), jnp.float32)], 1
    ).astype(jnp.bfloat16)
    lane = lax.broadcasted_iota(jnp.int32, (CH, 128), 1)
    for p, part in enumerate((real, imag)):
        for tile in range(BINS // 128):
            cut = slice(tile * 128, tile * 128 + 128)
            rows = [
                part[s, :, cut] * scale[s, :, cut] * valid[:, s : s + 1] for s in range(SEGMENTS)
            ]
            for bit in (1, 2, 4):
                upper = (lane // GROUP) & bit != 0
                for i in range(SEGMENTS):
                    if i & bit:
                        continue
                    a, b = rows[i], rows[i + bit]
                    rows[i] = jnp.where(upper, pltpu.roll(b, bit * GROUP, 1), a)
                    rows[i + bit] = jnp.where(upper, b, pltpu.roll(a, 128 - bit * GROUP, 1))
            for g in range(SEGMENTS):
                out_ref[tile * SEGMENTS + g, :, p * 128 : p * 128 + 128] = rows[g].astype(
                    jnp.bfloat16
                )


def whiten(rank, spectra, rim, mask):
    return pl.pallas_call(
        whiten_kernel,
        out_shape=jax.ShapeDtypeStruct((GROUPS + 1, CH, DEPTH), jnp.bfloat16),
        in_specs=[pl.BlockSpec(memory_space=pltpu.SMEM)]
        + [pl.BlockSpec(memory_space=pltpu.VMEM)] * 3,
        out_specs=pl.BlockSpec(memory_space=pltpu.VMEM),
        compiler_params=pltpu.CompilerParams(vmem_limit_bytes=VMEM),
        name="whiten",
    )(rank, spectra, rim, mask)


def band_kernel(lies, place_ref, *refs):
    own_ref, source_refs, array_refs = refs[0], refs[1:3], refs[3 : 3 + len(lies)]
    (table_ref, out_ref, rows_ref, flags_ref, diagonal_ref, product_ref, inverse_ref) = refs[
        3 + len(lies) : 10 + len(lies)
    ]
    weights_ref, result_ref, staging_ref, sems, out_sems = refs[10 + len(lies) :]
    core, x, chip, chips, rank = [place_ref[n] for n in range(5)]
    step = pl.program_id(0)
    corr_steps = GROUPS // STEP
    place = {}
    count = 0
    spans = []
    for names in lies:
        spans.append((count, len(names)))
        for name in names:
            place[name] = count
            count += 1

    def order(half):
        listed = []

        def add(kinds, layer):
            listed.append(jnp.where(layer == 0, place[(*kinds, 0)], place[(*kinds, 1)]))

        for j in range(LINE):
            wraps = x + j >= LINE
            for upper in (0, 1):
                for layer in (core, 1 - core):
                    straight = [place[j, upper, half, n] for n in range(2)]
                    turned = [place[j, 1 - upper, half, n] for n in range(2)]
                    listed.append(
                        jnp.where(
                            wraps,
                            jnp.where(layer == 0, turned[0], turned[1]),
                            jnp.where(layer == 0, straight[0], straight[1]),
                        )
                    )
        for layer in (core, 1 - core):
            add((0, 2, half), layer)
        return listed

    def fetch(number):
        slot = number % 2
        for ref, (start, size) in zip(array_refs, spans):
            pltpu.make_async_copy(
                ref.at[:, pl.ds(number * STEP, STEP)],
                rows_ref.at[slot, pl.ds(start, size)],
                sems.at[slot],
            ).start()

    @pl.when(step == 0)
    def begin():
        fetch(0)
        pltpu.make_async_copy(table_ref.at[rank], weights_ref, sems.at[3]).start()
        for ref, (start, size) in zip(array_refs, spans):
            pltpu.make_async_copy(
                ref.at[:, GROUPS], flags_ref.at[pl.ds(start, size)], sems.at[2]
            ).start()

    @pl.when(step < corr_steps)
    def correlate():
        @pl.when(step + 1 < corr_steps)
        def ahead():
            fetch(step + 1)

        slot = step % 2
        pltpu.make_async_copy(rows_ref.at[slot], rows_ref.at[slot], sems.at[slot]).wait()
        lane_bin = lax.broadcasted_iota(jnp.int32, (GROUP, DEPTH), 1) % GROUP
        own_bin = lane_bin == lax.broadcasted_iota(jnp.int32, (GROUP, DEPTH), 0)
        column = lax.broadcasted_iota(jnp.int32, (GROUP, 128), 1)
        orders = [order(half) for half in range(2)]

        def one_group(index, carry):
            for half in range(2):
                source = source_refs[half][index].astype(jnp.float32)
                real, imag = source[:, : DEPTH // 2], source[:, DEPTH // 2 :]
                source = jnp.concatenate(
                    [jnp.where(rank == 0, real, -imag), jnp.where(rank == 0, imag, real)], 1
                )
                for c in range(CH):
                    spread = jnp.broadcast_to(source[c : c + 1, :], (GROUP, DEPTH))
                    diagonal_ref[half, c * GROUP : (c + 1) * GROUP, :] = jnp.where(
                        own_bin, spread, 0.0
                    ).astype(jnp.bfloat16)
                rows = jnp.concatenate([rows_ref[slot, at, index] for at in orders[half]], 0)
                product = lax.dot_general(
                    diagonal_ref[half],
                    rows,
                    (((1,), (1,)), ((), ())),
                    preferred_element_type=jnp.float32,
                )
                first_bin = pl.multiple_of(half * BINS + (step * STEP + index) * GROUP, GROUP)
                for c in range(CH):
                    part = product[c * GROUP : (c + 1) * GROUP]
                    here = pl.ds(c * FBINS + first_bin, GROUP)
                    tail = jnp.concatenate([part[:, BAND:], part[:, 64:128]], 1)
                    head = jnp.where(column >= 32 * core + c, part[:, :128], tail)
                    product_ref[here, :] = jnp.concatenate([head, part[:, 128:BAND]], 1).astype(
                        jnp.bfloat16
                    )
            return carry

        lax.fori_loop(0, STEP, one_group, 0, unroll=UNROLL)

    @pl.when(step == corr_steps)
    def scales():
        pltpu.make_async_copy(table_ref.at[rank], weights_ref, sems.at[3]).wait()
        pltpu.make_async_copy(flags_ref, flags_ref, sems.at[2]).wait()
        counts = lax.dot_general(
            own_ref[0],
            jnp.concatenate([flags_ref[at] for at in order(0)], 0),
            (((1,), (1,)), ((), ())),
            preferred_element_type=jnp.float32,
        )
        inverse = 1.0 / jnp.maximum(counts, 1.0)
        column = lax.broadcasted_iota(jnp.int32, (CH, 64), 1)
        channel = lax.broadcasted_iota(jnp.int32, (CH, 64), 0)
        parts = []
        for n in range(8):
            offset = n // 2 + 4 * (n % 2)
            part = jnp.where(chip + offset < chips, inverse[:, 64 * n : 64 * n + 64], 0.0)
            if offset == 0:
                after = jnp.where(chip + 8 < chips, inverse[:, BAND:], 0.0)
                part = jnp.where(column >= 32 * core + channel, part, after)
            parts.append(part)
        whole = jnp.concatenate(parts, 1)
        for c in range(CH):
            inverse_ref[c] = whole[c : c + 1]

    def one_channel(c):
        lags = jnp.dot(
            weights_ref[...],
            product_ref[pl.ds(pl.multiple_of(c * FBINS, FBINS), FBINS), :],
            preferred_element_type=jnp.float32,
        )
        lags = (lags * inverse_ref[c]).astype(jnp.bfloat16)
        tiles = [lags[:, 128 * j : 128 * j + 128] for j in range(LINE)]
        shift = 32 * core + c
        low = [pltpu.roll(tile, (128 - shift) % 128, 1) for tile in tiles]
        high = [pltpu.roll(tile, 64 - shift, 1) for tile in tiles]
        lane = lax.broadcasted_iota(jnp.int32, (LAGS, 128), 1)
        first, second = lane < 64 - shift, lane < 128 - shift
        rows = pl.ds(pl.multiple_of(c % BATCH * LAGS, LAGS), LAGS)
        for u, (one, two, three) in enumerate(
            (
                (low[0], high[1], low[2]),
                (low[2], high[3], high[0]),
                (high[0], low[1], high[2]),
                (high[2], low[3], low[0]),
            )
        ):
            result_ref[c // BATCH, u, rows, :] = jnp.where(first, one, jnp.where(second, two, three))

    def flush(batch, chunk):
        at = pl.multiple_of(chunk * CHUNK, CHUNK)
        for u in range(4):
            block = jnp.stack(
                [result_ref[batch, u, pl.ds(n * LAGS + at, CHUNK), :] for n in range(BATCH)]
            ).astype(jnp.float32)
            staging_ref[pl.ds(at, CHUNK), :, u * 128 : u * 128 + 128] = jnp.swapaxes(
                block, 0, 1
            ).astype(jnp.bfloat16)

    def leaving(batch, chunk):
        at = pl.multiple_of(chunk * CHUNK, CHUNK)
        return pltpu.make_async_copy(
            staging_ref.at[pl.ds(at, CHUNK)],
            out_ref.at[pl.ds(at, CHUNK), pl.ds(batch * BATCH, BATCH), :],
            out_sems.at[chunk],
        )

    lag_step = step - corr_steps
    batch_steps = BATCH // CSTEP

    @pl.when(jnp.logical_and(step >= corr_steps, lag_step < batch_steps))
    def first_batch():
        lax.fori_loop(0, CSTEP, lambda n, carry: one_channel(lag_step * CSTEP + n), None, unroll=CSTEP)

    @pl.when(lag_step >= batch_steps)
    def second_batch():
        def one(n, carry):
            c = lag_step * CSTEP + n
            one_channel(c)
            flush(0, c - BATCH)
            leaving(0, c - BATCH).start()

        lax.fori_loop(0, CSTEP, one, None, unroll=CSTEP)

    @pl.when(lag_step == 2 * batch_steps - 1)
    def last_flush():
        def one(n, carry):
            leaving(0, n).wait()
            flush(1, n)
            leaving(1, n).start()

        lax.fori_loop(0, LAGS // CHUNK, one, None, unroll=2)
        lax.fori_loop(0, LAGS // CHUNK, lambda n, carry: leaving(1, n).wait(), None)


def band_lags(place, own, sources, arrays, lies, table):
    corr_steps = GROUPS // STEP
    blocks = sum(map(len, lies))
    source_spec = pl.BlockSpec((STEP, CH, DEPTH), lambda i: (jnp.minimum(i, corr_steps - 1), 0, 0))
    flops = 2 * CH * FBINS * BAND * (DEPTH + LAGS)
    moved_bytes = 2 * blocks * CH * DEPTH * GROUPS + 2 * CH * LAGS * BAND
    return pl.pallas_call(
        lambda *refs: band_kernel(lies, *refs),
        grid=(corr_steps + CH // CSTEP,),
        out_shape=jax.ShapeDtypeStruct((LAGS, CH, BAND), jnp.bfloat16),
        in_specs=[
            pl.BlockSpec(memory_space=pltpu.SMEM),
            pl.BlockSpec((1, CH, DEPTH), lambda i: (GROUPS, 0, 0)),
            source_spec,
            source_spec,
        ]
        + [pl.BlockSpec(memory_space=pl.ANY)] * (len(arrays) + 1),
        out_specs=pl.BlockSpec(memory_space=pl.ANY),
        scratch_shapes=[
            pltpu.VMEM((2, blocks, STEP, CH, DEPTH), jnp.bfloat16),
            pltpu.VMEM((blocks, CH, DEPTH), jnp.bfloat16),
            pltpu.VMEM((2, CH * GROUP, DEPTH), jnp.bfloat16),
            pltpu.VMEM((CH * FBINS, BAND), jnp.bfloat16),
            pltpu.VMEM((CH, 1, BAND), jnp.float32),
            pltpu.VMEM((LAGS, FBINS), jnp.bfloat16),
            pltpu.VMEM((2, 4, BATCH * LAGS, 128), jnp.bfloat16),
            pltpu.VMEM((LAGS, BATCH, BAND), jnp.bfloat16),
            pltpu.SemaphoreType.DMA((4,)),
            pltpu.SemaphoreType.DMA((LAGS // CHUNK,)),
        ],
        compiler_params=pltpu.CompilerParams(
            vmem_limit_bytes=VMEM, dimension_semantics=("arbitrary",)
        ),
        cost_estimate=pl.CostEstimate(flops=flops, bytes_accessed=moved_bytes, transcendentals=0),
        name="band_lags",
    )(place, own, *sources, *arrays, table)


def lag_table():
    lag_index = np.arange(LAGS, dtype=np.int64)
    tables = []
    for rank in range(2):
        freq_index = (np.arange(FBINS, dtype=np.int64) + rank * BINS) % FBINS
        angles = (lag_index[:, None] * freq_index[None, :] % NFFT) * (2.0 * math.pi / NFFT)
        values = -np.sin(angles) if rank else np.cos(angles)
        tables.append((values * FBINS ** (-0.5)).astype(np.float32).astype(ml_dtypes.bfloat16))
    return np.stack(tables)


def local(spectra, seg_mask):
    chan = lax.axis_index("chan")
    rank = lax.axis_index("freq")
    core, x, row = chan % 2, chan // 2 % LINE, chan // (2 * LINE) % ROWS
    chips = lax.axis_size("chan") // 2
    place = jnp.stack([core, x, chan // 2, jnp.int32(chips), rank]).astype(jnp.int32)
    edge = jnp.where(rank == 0, spectra[..., BINS - 128 :], spectra[..., :128])
    rim = moved(edge, freq=1)
    own = whiten(rank.astype(jnp.int32).reshape(1), spectra, rim, seg_mask)

    def along(block, j):
        return moved(block, (0, 0, j))

    def flip(block):
        return moved(block, freq=1)

    def swap(block):
        return moved(block, core=1)

    def reached(j):
        return along(jnp.where(x >= j, own, after), j)

    after = moved(own, (1, 0, 0))
    own_flip = flip(own)
    own, after = lax.optimization_barrier((own, after))
    crossing = jnp.where(row == 1, own, after)
    one, three = reached(1), reached(3)
    cross = moved(crossing, (0, 1, 0))
    cross_flip = moved(crossing, (0, 1, 0), freq=1)
    one, three, cross, cross_flip, own_flip = lax.optimization_barrier(
        (one, three, cross, cross_flip, own_flip)
    )
    pairs = {0: jnp.stack([cross, cross_flip])}
    row_pair = jnp.stack([one, three])
    row_flip = flip(row_pair)
    pairs[1], pairs[3] = along(pairs[0], 1), along(pairs[0], 3)
    two = reached(2)
    after_flip = moved(own_flip, (1, 0, 0))
    singles = [own, own_flip, after, after_flip]
    row_flip, row_pair_, pair_, *singles_ = lax.optimization_barrier(
        (row_flip, row_pair, pairs[0], *singles)
    )
    swapped = [swap(block) for block in (*singles_, pair_, row_pair_, row_flip)]
    pairs[1], pairs[3], two = lax.optimization_barrier((pairs[1], pairs[3], two))
    two_flip = flip(two)
    cross_two = along(pairs[1][0], 1)
    cross_two_flip = along(pairs[3][1], 3)
    held = [*singles, pairs[0], row_pair, row_flip, pairs[1], pairs[3]]
    held += [two, two_flip, cross_two, cross_two_flip]
    swapped = [*swapped, *(swap(block) for block in held[7:])]
    names = [[(0, 0, 0)], [(0, 0, 1)], [(0, 2, 0)], [(0, 2, 1)], [(0, 1, 0), (0, 1, 1)]]
    names += [[(1, 0, 0), (3, 0, 0)], [(1, 0, 1), (3, 0, 1)]]
    names += [[(1, 1, 0), (1, 1, 1)], [(3, 1, 0), (3, 1, 1)]]
    names += [[(2, 0, 0)], [(2, 0, 1)], [(2, 1, 0)], [(2, 1, 1)]]
    arrays, lies = [], []
    for layer, blocks in enumerate((held, swapped)):
        for listed, block in zip(names, blocks):
            arrays.append(block if block.ndim == 4 else block[None])
            lies.append([(*name, layer) for name in listed])
    table = jnp.asarray(lag_table())
    return band_lags(place, own, [own, own_flip], arrays, lies, table)[None]


def solution(mesh):
    placed = (P(None, None, "chan", "freq"), P("chan", None))
    return jax.shard_map(
        local, mesh=mesh, in_specs=placed, out_specs=P("freq", None, "chan", None), check_vma=False
    )
```

time: 868 us -> 159 us (0.18)
  waiting for transfers between devices: 370 us -> 63.2 us
  local copies, waits for them, and re-layouts: 225 us -> 7.51 us
  matrix products: 123 us -> 0 us
  other arithmetic: 61.5 us -> 2.57 us
  Pallas kernels: 0 us -> 37 us
  starting transfers between devices: 70.3 us -> 47.6 us
  between operations: 13.6 us -> 0.33 us
    reduce_scatter x1 -> x0, waiting for transfers between devices: 258 us -> none  [local(): lax.psum_scatter(jnp.stack(results).astype(jnp.bfloat16), 'freq', scatter...]
    dot_general x17 -> x0, matrix products: 123 us -> none  [the longest x8 79 us: add_block(): jnp.dot(weights, spectrum, preferred_element_type=jnp.float32)]
    convert_element_type x8 -> x0, local copies, waits for them, and re-layouts: 68.7 us -> none  [add_block(): scaled = (product * inverse[None]).astype(jnp.bfloat16)]
    ppermute x34 -> x28, waiting for transfers between devices: 111 us -> 63.2 us  [moved(): return lax.ppermute(value, AXES, pairs)]
    another operation x6 -> x2, other arithmetic: 43.4 us -> 0.2 us  [the longest x1 0.1 us: local(): row_pair = jnp.stack([one, three])]
    reshape x9 -> x0, local copies, waits for them, and re-layouts: 43 us -> none  [the longest x8 42.9 us: band_rows(): return padded.reshape(leading + (height, breadth + 1))[..., :band]]
    pad x8 -> x0, local copies, waits for them, and re-layouts: 42.1 us -> none  [band_rows(): padded = jnp.pad(flattened, [(0, 0)] * len(leading) + [(0, height)])]
    pallas_call x0 -> x2, Pallas kernels: none -> 37 us  [the longest x1 33.9 us: band_lags(): pl.pallas_call(lambda *refs: band_kernel(lies, *refs), grid=(corr_steps +...]
  transfers between devices with their start and end apart: 35 -> 28, of which waited for: 18 -> 12; matrix products, arithmetic and copies ran while one was open for 0% -> 4% of each run, Pallas kernels for 0% -> 0%
where the time goes in v2:
time: 159 us; the launch traced here: 158 us
  waiting for transfers between devices  63.2 us (40%)
  starting transfers between devices  47.6 us (30%)
  Pallas kernels  37 us (23%)
  local copies, waits for them, and re-layouts  7.51 us (5%)
  other arithmetic  2.57 us (2%)
    ppermute x28, waiting for transfers between devices, moved(): return lax.ppermute(value, AXES, pairs)  63.2 us
    ppermute x28, starting transfers between devices, moved(): return lax.ppermute(value, AXES, pairs)  47.6 us
    pallas_call x1, Pallas kernels, band_lags(): pl.pallas_call(lambda *refs: band_kernel(lies, *refs), grid=(corr_steps +...  33.9 us
    unnamed x41, local copies, waits for them, and re-layouts  4.75 us
  transfers between devices with their start and end apart: 28, of which 12 were waited for; matrix products, arithmetic and copies ran while one was open for 4% of the time, Pallas kernels for 0%

profile of v2, /device:TPU:1, one launch (start us, length us, event | category | flops | bytes accessed | tf_op | source)
XLA Modules:
  0.0 158.2 jit_solution(3867878436791068529)
XLA Ops:
  1.0 3.8 %collective-permute-start = (bf16[2,8,32,128]{3,2,1,0:T(8,128)(2,1)S(1)}, bf16[2,8,32,128]{3,2,1,0:T(8,128)(2,1)S(1)}, u32[]{:S(2)}, u32[]{:S(2)}) collective-permute-start(bf16[2,8,32,128]{3,2,1,0:T(8,128)(2,1)S(1)} %slice_select_fusion), channel_id=1, source_target_pairs={{0,1},{1,0},{2,3},{3,2},{4,5},{5,4},{6,7},{7,6},{8,9},{9,8},{10,11... | collective-permute-start | bytes 393224 | tf_op jit(solution)/shard_map/ppermute | solution.py:47
  4.8 1.4 copy.4.mask_ref
  7.8 3.1 %whiten.1.refs_1_.refs_2_ = bf16[33,32,256]{2,1,0:T(8,128)(2,1)} custom-call(s32[1]{0:T(128)} %bitcast.3.rank_ref, bf16[2,8,32,512]{3,2,1,0:T(8,128)(2,1)} %spectra_ref.1, bf16[2,8,32,128]{3,2,1,0:T(8,128)(2,1)} %copy-done.4, s32[32,8]{1,0:T(8,128)} %copy.4.mask_ref), custom_call_target="tpu_custom_call" | custom-call | tf_op jit(solution)/shard_map/whiten/pallas_call | solution.py:104
  11.0 6.2 %collective-permute-start.1 = (bf16[33,32,256]{2,1,0:T(8,128)(2,1)}, bf16[33,32,256]{2,1,0:T(8,128)(2,1)S(1)}, u32[]{:S(2)}, u32[]{:S(2)}) collective-permute-start(bf16[33,32,256]{2,1,0:T(8,128)(2,1)} %whiten.1.refs_1_.refs_2_), channel_id=1, source_target_pairs={{0,224},{1,225},{2,226},{3,227},{4,228},{5,229},{6,230},{7,231},{8... | collective-permute-start | bytes 1622024 | tf_op jit(solution)/shard_map/ppermute | solution.py:47
  17.1 2.9 %collective-permute-start.6 = (bf16[33,32,256]{2,1,0:T(8,128)(2,1)}, bf16[33,32,256]{2,1,0:T(8,128)(2,1)S(1)}, u32[]{:S(2)}, u32[]{:S(2)}) collective-permute-start(bf16[33,32,256]{2,1,0:T(8,128)(2,1)} %whiten.1.refs_1_.refs_2_), channel_id=1, source_target_pairs={{0,1},{1,0},{2,3},{3,2},{4,5},{5,4},{6,7},{7,6},{8,9},{9,8},{10,11... | collective-permute-start | bytes 1622024 | tf_op jit(solution)/shard_map/ppermute | solution.py:47
  20.0 7.4 %collective-permute-done.1 = bf16[33,32,256]{2,1,0:T(8,128)(2,1)S(1)} collective-permute-done((bf16[33,32,256]{2,1,0:T(8,128)(2,1)}, bf16[33,32,256]{2,1,0:T(8,128)(2,1)S(1)}, u32[]{:S(2)}, u32[]{:S(2)}) %collective-permute-start.1) | collective-permute-done | bytes 540704 | tf_op jit(solution)/shard_map/ppermute | solution.py:47
  27.5 1.4 broadcast_select_fusion
  28.9 1.3 collective-permute-start.3
  30.2 1.5 collective-permute-start.2
  31.6 2.7 %collective-permute-start.5 = (bf16[33,32,256]{2,1,0:T(8,128)(2,1)S(1)}, bf16[33,32,256]{2,1,0:T(8,128)(2,1)S(1)}, u32[]{:S(2)}, u32[]{:S(2)}) collective-permute-start(bf16[33,32,256]{2,1,0:T(8,128)(2,1)S(1)} %get-tuple-element.40), channel_id=1, source_target_pairs={{0,17},{1,16},{2,19},{3,18},{4,21},{5,20},{6,23},{7,22},{8,25},{9,... | collective-permute-start | bytes 1622024 | tf_op jit(solution)/shard_map/ppermute | solution.py:47
  34.4 7.1 %collective-permute-done.3 = bf16[33,32,256]{2,1,0:T(8,128)(2,1)S(1)} collective-permute-done((bf16[33,32,256]{2,1,0:T(8,128)(2,1)S(1)}, bf16[33,32,256]{2,1,0:T(8,128)(2,1)S(1)}, u32[]{:S(2)}, u32[]{:S(2)}) %collective-permute-start.3) | collective-permute-done | bytes 540704 | tf_op jit(solution)/shard_map/ppermute | solution.py:47
  41.4 2.3 %collective-permute-done.5 = bf16[33,32,256]{2,1,0:T(8,128)(2,1)S(1)} collective-permute-done((bf16[33,32,256]{2,1,0:T(8,128)(2,1)S(1)}, bf16[33,32,256]{2,1,0:T(8,128)(2,1)S(1)}, u32[]{:S(2)}, u32[]{:S(2)}) %collective-permute-start.5) | collective-permute-done | bytes 540704 | tf_op jit(solution)/shard_map/ppermute | solution.py:47
  43.7 1.1 collective-permute-done.4
  45.7 2.6 %collective-permute-start.9 = (bf16[2,33,32,256]{3,2,1,0:T(8,128)(2,1)S(1)}, bf16[2,33,32,256]{3,2,1,0:T(8,128)(2,1)}, u32[]{:S(2)}, u32[]{:S(2)}) collective-permute-start(bf16[2,33,32,256]{3,2,1,0:T(8,128)(2,1)S(1)} %pad_maximum_fusion.refs_8_), channel_id=1, source_target_pairs={{0,12},{1,13},{2,14},{3,15},{4,0},{5,1},{6,2},{7,3},{8,4},{9,5},{1... | collective-permute-start | bytes 3244040 | tf_op jit(solution)/shard_map/ppermute | solution.py:47
  48.3 3.3 %collective-permute-start.7 = (bf16[33,32,256]{2,1,0:T(8,128)(2,1)S(1)}, bf16[33,32,256]{2,1,0:T(8,128)(2,1)S(1)}, u32[]{:S(2)}, u32[]{:S(2)}) collective-permute-start(bf16[33,32,256]{2,1,0:T(8,128)(2,1)S(1)} %collective-permute-done.6.refs_3_), channel_id=1, source_target_pairs={{0,224},{1,225},{2,226},{3,227},{4,228},{5,229},{6,230},{7,231},{8... | collective-permute-start | bytes 1622024 | tf_op jit(solution)/shard_map/ppermute | solution.py:47
  52.0 6.3 %collective-permute-done.7 = bf16[33,32,256]{2,1,0:T(8,128)(2,1)S(1)} collective-permute-done((bf16[33,32,256]{2,1,0:T(8,128)(2,1)S(1)}, bf16[33,32,256]{2,1,0:T(8,128)(2,1)S(1)}, u32[]{:S(2)}, u32[]{:S(2)}) %collective-permute-start.7) | collective-permute-done | bytes 540704 | tf_op jit(solution)/shard_map/ppermute | solution.py:47
  58.3 9.1 %collective-permute-done.8.refs_10_ = bf16[2,33,32,256]{3,2,1,0:T(8,128)(2,1)S(1)} collective-permute-done((bf16[2,33,32,256]{3,2,1,0:T(8,128)(2,1)S(1)}, bf16[2,33,32,256]{3,2,1,0:T(8,128)(2,1)S(1)}, u32[]{:S(2)}, u32[]{:S(2)}) %collective-permute-start.8) | collective-permute-done | bytes 1081376 | tf_op jit(solution)/shard_map/ppermute | solution.py:47
  67.4 5.4 %collective-permute-start.15 = (bf16[33,32,256]{2,1,0:T(8,128)(2,1)S(1)}, bf16[33,32,256]{2,1,0:T(8,128)(2,1)S(1)}, u32[]{:S(2)}, u32[]{:S(2)}) collective-permute-start(bf16[33,32,256]{2,1,0:T(8,128)(2,1)S(1)} %copy-done), channel_id=1, source_target_pairs={{0,2},{1,3},{2,0},{3,1},{4,6},{5,7},{6,4},{7,5},{8,10},{9,11},{10,... | collective-permute-start | bytes 1622024 | tf_op jit(solution)/shard_map/ppermute | solution.py:47
  72.9 6.8 %collective-permute-done.11 = bf16[33,32,256]{2,1,0:T(8,128)(2,1)S(1)} collective-permute-done((bf16[33,32,256]{2,1,0:T(8,128)(2,1)S(1)}, bf16[33,32,256]{2,1,0:T(8,128)(2,1)S(1)}, u32[]{:S(2)}, u32[]{:S(2)}) %collective-permute-start.11) | collective-permute-done | bytes 540704 | tf_op jit(solution)/shard_map/ppermute | solution.py:47
  79.7 5.1 %collective-permute-start.17 = (bf16[33,32,256]{2,1,0:T(8,128)(2,1)S(1)}, bf16[33,32,256]{2,1,0:T(8,128)(2,1)}, u32[]{:S(2)}, u32[]{:S(2)}) collective-permute-start(bf16[33,32,256]{2,1,0:T(8,128)(2,1)S(1)} %collective-permute-done.1), channel_id=1, source_target_pairs={{0,2},{1,3},{2,0},{3,1},{4,6},{5,7},{6,4},{7,5},{8,10},{9,11},{10,... | collective-permute-start | bytes 1622024 | tf_op jit(solution)/shard_map/ppermute | solution.py:47
  84.9 1.1 slice_bitcast_fusion
  85.9 1.1 collective-permute-start.14
  87.1 1.1 slice_bitcast_fusion.1
  88.2 1.9 %collective-permute-start.13 = (bf16[33,32,256]{2,1,0:T(8,128)(2,1)S(1)}, bf16[33,32,256]{2,1,0:T(8,128)(2,1)S(1)}, u32[]{:S(2)}, u32[]{:S(2)}) collective-permute-start(bf16[33,32,256]{2,1,0:T(8,128)(2,1)S(1)} %slice_bitcast_fusion.1), channel_id=1, source_target_pairs={{0,12},{1,13},{2,14},{3,15},{4,0},{5,1},{6,2},{7,3},{8,4},{9,5},{1... | collective-permute-start | bytes 1622024 | tf_op jit(solution)/shard_map/ppermute | solution.py:47
  90.1 1.1 collective-permute-start.19
  91.9 9.0 %collective-permute-done.14 = bf16[33,32,256]{2,1,0:T(8,128)(2,1)} collective-permute-done((bf16[33,32,256]{2,1,0:T(8,128)(2,1)S(1)}, bf16[33,32,256]{2,1,0:T(8,128)(2,1)}, u32[]{:S(2)}, u32[]{:S(2)}) %collective-permute-start.14) | collective-permute-done | bytes 540704 | tf_op jit(solution)/shard_map/ppermute | solution.py:47
  101.0 1.2 collective-permute-start.24
  102.2 2.5 %collective-permute-start.12 = (bf16[33,32,256]{2,1,0:T(8,128)(2,1)S(1)}, bf16[33,32,256]{2,1,0:T(8,128)(2,1)}, u32[]{:S(2)}, u32[]{:S(2)}) collective-permute-start(bf16[33,32,256]{2,1,0:T(8,128)(2,1)S(1)} %collective-permute-done.11), channel_id=1, source_target_pairs={{0,1},{1,0},{2,3},{3,2},{4,5},{5,4},{6,7},{7,6},{8,9},{9,8},{10,11... | collective-permute-start | bytes 1622024 | tf_op jit(solution)/shard_map/ppermute | solution.py:47
  105.5 11.4 %collective-permute-done.12 = bf16[33,32,256]{2,1,0:T(8,128)(2,1)} collective-permute-done((bf16[33,32,256]{2,1,0:T(8,128)(2,1)S(1)}, bf16[33,32,256]{2,1,0:T(8,128)(2,1)}, u32[]{:S(2)}, u32[]{:S(2)}) %collective-permute-start.12) | collective-permute-done | bytes 540704 | tf_op jit(solution)/shard_map/ppermute | solution.py:47
  116.9 1.6 %collective-permute-start.23 = (bf16[2,33,32,256]{3,2,1,0:T(8,128)(2,1)}, bf16[2,33,32,256]{3,2,1,0:T(8,128)(2,1)}, u32[]{:S(2)}, u32[]{:S(2)}) collective-permute-start(bf16[2,33,32,256]{3,2,1,0:T(8,128)(2,1)} %collective-permute-done.10.refs_12_), channel_id=1, source_target_pairs={{0,2},{1,3},{2,0},{3,1},{4,6},{5,7},{6,4},{7,5},{8,10},{9,11},{10,... | collective-permute-start | bytes 3244040 | tf_op jit(solution)/shard_map/ppermute | solution.py:47
  119.9 1.1 copy-done.8
  124.2 33.9 %band_lags.1 = bf16[256,32,512]{2,1,0:T(8,128)(2,1)} custom-call(s32[5]{0:T(128)} %stack.37.refs_0_, bf16[33,32,256]{2,1,0:T(8,128)(2,1)} %whiten.1.refs_1_.refs_2_, bf16[33,32,256]{2,1,0:T(8,128)(2,1)} %whiten.1.refs_1_.refs_2_, bf16[33,32,256]{2,1,0:T(8,128)(2,1)} %copy-done.9, bf16[1,33,32,256]{3,2,1,0:T(8,128)(2,1)} %bitcast.29, ...), custom_call_target="tpu_custom_call" | custom-call | flops 17179869184 | bytes 27262976 | tf_op jit(solution)/shard_map/band_lags/pallas_call | solution.py:320
  (74 shorter events, 10.2 us)
Async XLA Ops:
  1.0 6.2 %collective-permute-start = (bf16[2,8,32,128]{3,2,1,0:T(8,128)(2,1)S(1)}, bf16[2,8,32,128]{3,2,1,0:T(8,128)(2,1)S(1)}, u32[]{:S(2)}, u32[]{:S(2)}) collective-permute-start(bf16[2,8,32,128]{3,2,1,0:T(8,128)(2,1)S(1)} %slice_select_fusion), channel_id=1, source_target_pairs={{0,1},{1,0},{2,3},{3,2},{4,5},{5,4},{6,7},{7,6},{8,9},{9,8},{10,11... | collective-permute-start | bytes 393224 | tf_op jit(solution)/shard_map/ppermute | solution.py:47
  11.0 16.5 %collective-permute-start.1 = (bf16[33,32,256]{2,1,0:T(8,128)(2,1)}, bf16[33,32,256]{2,1,0:T(8,128)(2,1)S(1)}, u32[]{:S(2)}, u32[]{:S(2)}) collective-permute-start(bf16[33,32,256]{2,1,0:T(8,128)(2,1)} %whiten.1.refs_1_.refs_2_), channel_id=1, source_target_pairs={{0,224},{1,225},{2,226},{3,227},{4,228},{5,229},{6,230},{7,231},{8... | collective-permute-start | bytes 1622024 | tf_op jit(solution)/shard_map/ppermute | solution.py:47
  17.1 17.2 %collective-permute-start.6 = (bf16[33,32,256]{2,1,0:T(8,128)(2,1)}, bf16[33,32,256]{2,1,0:T(8,128)(2,1)S(1)}, u32[]{:S(2)}, u32[]{:S(2)}) collective-permute-start(bf16[33,32,256]{2,1,0:T(8,128)(2,1)} %whiten.1.refs_1_.refs_2_), channel_id=1, source_target_pairs={{0,1},{1,0},{2,3},{3,2},{4,5},{5,4},{6,7},{7,6},{8,9},{9,8},{10,11... | collective-permute-start | bytes 1622024 | tf_op jit(solution)/shard_map/ppermute | solution.py:47
  27.5 52.2 %copy-start.3 = (bf16[33,32,256]{2,1,0:T(8,128)(2,1)}, bf16[33,32,256]{2,1,0:T(8,128)(2,1)S(1)}, u32[]{:S(2)}) copy-start(bf16[33,32,256]{2,1,0:T(8,128)(2,1)S(1)} %collective-permute-done.1) | copy-start | bytes 1622020
  28.9 12.6 %collective-permute-start.3 = (bf16[33,32,256]{2,1,0:T(8,128)(2,1)S(1)}, bf16[33,32,256]{2,1,0:T(8,128)(2,1)S(1)}, u32[]{:S(2)}, u32[]{:S(2)}) collective-permute-start(bf16[33,32,256]{2,1,0:T(8,128)(2,1)S(1)} %get-tuple-element.41), channel_id=1, source_target_pairs={{0,4},{1,5},{2,6},{3,7},{4,8},{5,9},{6,10},{7,11},{8,12},{9,13},{1... | collective-permute-start | bytes 1622024 | tf_op jit(solution)/shard_map/ppermute | solution.py:47
  30.2 11.3 %collective-permute-start.2 = (bf16[33,32,256]{2,1,0:T(8,128)(2,1)S(1)}, bf16[33,32,256]{2,1,0:T(8,128)(2,1)S(1)}, u32[]{:S(2)}, u32[]{:S(2)}) collective-permute-start(bf16[33,32,256]{2,1,0:T(8,128)(2,1)S(1)} %get-tuple-element.42), channel_id=1, source_target_pairs={{0,12},{1,13},{2,14},{3,15},{4,0},{5,1},{6,2},{7,3},{8,4},{9,5},{1... | collective-permute-start | bytes 1622024 | tf_op jit(solution)/shard_map/ppermute | solution.py:47
  31.6 12.1 %collective-permute-start.5 = (bf16[33,32,256]{2,1,0:T(8,128)(2,1)S(1)}, bf16[33,32,256]{2,1,0:T(8,128)(2,1)S(1)}, u32[]{:S(2)}, u32[]{:S(2)}) collective-permute-start(bf16[33,32,256]{2,1,0:T(8,128)(2,1)S(1)} %get-tuple-element.40), channel_id=1, source_target_pairs={{0,17},{1,16},{2,19},{3,18},{4,21},{5,20},{6,23},{7,22},{8,25},{9,... | collective-permute-start | bytes 1622024 | tf_op jit(solution)/shard_map/ppermute | solution.py:47
  34.4 10.5 %collective-permute-start.4 = (bf16[33,32,256]{2,1,0:T(8,128)(2,1)S(1)}, bf16[33,32,256]{2,1,0:T(8,128)(2,1)S(1)}, u32[]{:S(2)}, u32[]{:S(2)}) collective-permute-start(bf16[33,32,256]{2,1,0:T(8,128)(2,1)S(1)} %get-tuple-element.40), channel_id=1, source_target_pairs={{0,16},{1,17},{2,18},{3,19},{4,20},{5,21},{6,22},{7,23},{8,24},{9,... | collective-permute-start | bytes 1622024 | tf_op jit(solution)/shard_map/ppermute | solution.py:47
  44.9 46.2 %copy-start.1 = (bf16[2,33,32,256]{3,2,1,0:T(8,128)(2,1)}, bf16[2,33,32,256]{3,2,1,0:T(8,128)(2,1)S(1)}, u32[]{:S(2)}) copy-start(bf16[2,33,32,256]{3,2,1,0:T(8,128)(2,1)S(1)} %pad_maximum_fusion.1.refs_9_) | copy-start | bytes 3244036
  44.9 22.5 %collective-permute-start.8 = (bf16[2,33,32,256]{3,2,1,0:T(8,128)(2,1)S(1)}, bf16[2,33,32,256]{3,2,1,0:T(8,128)(2,1)S(1)}, u32[]{:S(2)}, u32[]{:S(2)}) collective-permute-start(bf16[2,33,32,256]{3,2,1,0:T(8,128)(2,1)S(1)} %pad_maximum_fusion.1.refs_9_), channel_id=1, source_target_pairs={{0,1},{1,0},{2,3},{3,2},{4,5},{5,4},{6,7},{7,6},{8,9},{9,8},{10,11... | collective-permute-start | bytes 3244040 | tf_op jit(solution)/shard_map/ppermute | solution.py:47
  45.6 44.5 %copy-start.2 = (bf16[2,33,32,256]{3,2,1,0:T(8,128)(2,1)}, bf16[2,33,32,256]{3,2,1,0:T(8,128)(2,1)S(1)}, u32[]{:S(2)}) copy-start(bf16[2,33,32,256]{3,2,1,0:T(8,128)(2,1)S(1)} %pad_maximum_fusion.refs_8_) | copy-start | bytes 3244036
  45.6 39.2 %collective-permute-start.10 = (bf16[2,33,32,256]{3,2,1,0:T(8,128)(2,1)S(1)}, bf16[2,33,32,256]{3,2,1,0:T(8,128)(2,1)}, u32[]{:S(2)}, u32[]{:S(2)}) collective-permute-start(bf16[2,33,32,256]{3,2,1,0:T(8,128)(2,1)S(1)} %pad_maximum_fusion.refs_8_), channel_id=1, source_target_pairs={{0,4},{1,5},{2,6},{3,7},{4,8},{5,9},{6,10},{7,11},{8,12},{9,13},{1... | collective-permute-start | bytes 3244040 | tf_op jit(solution)/shard_map/ppermute | solution.py:47
  45.7 39.1 %collective-permute-start.9 = (bf16[2,33,32,256]{3,2,1,0:T(8,128)(2,1)S(1)}, bf16[2,33,32,256]{3,2,1,0:T(8,128)(2,1)}, u32[]{:S(2)}, u32[]{:S(2)}) collective-permute-start(bf16[2,33,32,256]{3,2,1,0:T(8,128)(2,1)S(1)} %pad_maximum_fusion.refs_8_), channel_id=1, source_target_pairs={{0,12},{1,13},{2,14},{3,15},{4,0},{5,1},{6,2},{7,3},{8,4},{9,5},{1... | collective-permute-start | bytes 3244040 | tf_op jit(solution)/shard_map/ppermute | solution.py:47
  48.3 9.9 %collective-permute-start.7 = (bf16[33,32,256]{2,1,0:T(8,128)(2,1)S(1)}, bf16[33,32,256]{2,1,0:T(8,128)(2,1)S(1)}, u32[]{:S(2)}, u32[]{:S(2)}) collective-permute-start(bf16[33,32,256]{2,1,0:T(8,128)(2,1)S(1)} %collective-permute-done.6.refs_3_), channel_id=1, source_target_pairs={{0,224},{1,225},{2,226},{3,227},{4,228},{5,229},{6,230},{7,231},{8... | collective-permute-start | bytes 1622024 | tf_op jit(solution)/shard_map/ppermute | solution.py:47
  51.7 28.0 %collective-permute-start.11 = (bf16[33,32,256]{2,1,0:T(8,128)(2,1)S(1)}, bf16[33,32,256]{2,1,0:T(8,128)(2,1)S(1)}, u32[]{:S(2)}, u32[]{:S(2)}) collective-permute-start(bf16[33,32,256]{2,1,0:T(8,128)(2,1)S(1)} %get-tuple-element.39), channel_id=1, source_target_pairs={{0,8},{1,9},{2,10},{3,11},{4,12},{5,13},{6,14},{7,15},{8,0},{9,1},... | collective-permute-start | bytes 1622024 | tf_op jit(solution)/shard_map/ppermute | solution.py:47
  58.3 60.8 %copy-start.10 = (bf16[33,32,256]{2,1,0:T(8,128)(2,1)}, bf16[33,32,256]{2,1,0:T(8,128)(2,1)S(1)}, u32[]{:S(2)}) copy-start(bf16[33,32,256]{2,1,0:T(8,128)(2,1)S(1)} %collective-permute-done.7) | copy-start | bytes 1622020
  67.4 20.8 %collective-permute-start.15 = (bf16[33,32,256]{2,1,0:T(8,128)(2,1)S(1)}, bf16[33,32,256]{2,1,0:T(8,128)(2,1)S(1)}, u32[]{:S(2)}, u32[]{:S(2)}) collective-permute-start(bf16[33,32,256]{2,1,0:T(8,128)(2,1)S(1)} %copy-done), channel_id=1, source_target_pairs={{0,2},{1,3},{2,0},{3,1},{4,6},{5,7},{6,4},{7,5},{8,10},{9,11},{10,... | collective-permute-start | bytes 1622024 | tf_op jit(solution)/shard_map/ppermute | solution.py:47
  72.8 17.3 %collective-permute-start.16 = (bf16[33,32,256]{2,1,0:T(8,128)(2,1)S(1)}, bf16[33,32,256]{2,1,0:T(8,128)(2,1)S(1)}, u32[]{:S(2)}, u32[]{:S(2)}) collective-permute-start(bf16[33,32,256]{2,1,0:T(8,128)(2,1)S(1)} %collective-permute-done.6.refs_3_), channel_id=1, source_target_pairs={{0,2},{1,3},{2,0},{3,1},{4,6},{5,7},{6,4},{7,5},{8,10},{9,11},{10,... | collective-permute-start | bytes 1622024 | tf_op jit(solution)/shard_map/ppermute | solution.py:47
  79.7 11.5 %collective-permute-start.17 = (bf16[33,32,256]{2,1,0:T(8,128)(2,1)S(1)}, bf16[33,32,256]{2,1,0:T(8,128)(2,1)}, u32[]{:S(2)}, u32[]{:S(2)}) collective-permute-start(bf16[33,32,256]{2,1,0:T(8,128)(2,1)S(1)} %collective-permute-done.1), channel_id=1, source_target_pairs={{0,2},{1,3},{2,0},{3,1},{4,6},{5,7},{6,4},{7,5},{8,10},{9,11},{10,... | collective-permute-start | bytes 1622024 | tf_op jit(solution)/shard_map/ppermute | solution.py:47
  84.8 6.5 %collective-permute-start.18 = (bf16[33,32,256]{2,1,0:T(8,128)(2,1)S(1)}, bf16[33,32,256]{2,1,0:T(8,128)(2,1)S(1)}, u32[]{:S(2)}, u32[]{:S(2)}) collective-permute-start(bf16[33,32,256]{2,1,0:T(8,128)(2,1)S(1)} %collective-permute-done.7), channel_id=1, source_target_pairs={{0,2},{1,3},{2,0},{3,1},{4,6},{5,7},{6,4},{7,5},{8,10},{9,11},{10,... | collective-permute-start | bytes 1622024 | tf_op jit(solution)/shard_map/ppermute | solution.py:47
  85.9 15.0 %collective-permute-start.14 = (bf16[33,32,256]{2,1,0:T(8,128)(2,1)S(1)}, bf16[33,32,256]{2,1,0:T(8,128)(2,1)}, u32[]{:S(2)}, u32[]{:S(2)}) collective-permute-start(bf16[33,32,256]{2,1,0:T(8,128)(2,1)S(1)} %slice_bitcast_fusion), channel_id=1, source_target_pairs={{0,4},{1,5},{2,6},{3,7},{4,8},{5,9},{6,10},{7,11},{8,12},{9,13},{1... | collective-permute-start | bytes 1622024 | tf_op jit(solution)/shard_map/ppermute | solution.py:47
  88.2 14.0 %collective-permute-start.13 = (bf16[33,32,256]{2,1,0:T(8,128)(2,1)S(1)}, bf16[33,32,256]{2,1,0:T(8,128)(2,1)S(1)}, u32[]{:S(2)}, u32[]{:S(2)}) collective-permute-start(bf16[33,32,256]{2,1,0:T(8,128)(2,1)S(1)} %slice_bitcast_fusion.1), channel_id=1, source_target_pairs={{0,12},{1,13},{2,14},{3,15},{4,0},{5,1},{6,2},{7,3},{8,4},{9,5},{1... | collective-permute-start | bytes 1622024 | tf_op jit(solution)/shard_map/ppermute | solution.py:47
  90.1 28.4 %collective-permute-start.19 = (bf16[2,33,32,256]{3,2,1,0:T(8,128)(2,1)S(1)}, bf16[2,33,32,256]{3,2,1,0:T(8,128)(2,1)S(1)}, u32[]{:S(2)}, u32[]{:S(2)}) collective-permute-start(bf16[2,33,32,256]{3,2,1,0:T(8,128)(2,1)S(1)} %pad_maximum_fusion.refs_8_), channel_id=1, source_target_pairs={{0,2},{1,3},{2,0},{3,1},{4,6},{5,7},{6,4},{7,5},{8,10},{9,11},{10,... | collective-permute-start | bytes 3244040 | tf_op jit(solution)/shard_map/ppermute | solution.py:47
  91.1 27.5 %collective-permute-start.20 = (bf16[2,33,32,256]{3,2,1,0:T(8,128)(2,1)S(1)}, bf16[2,33,32,256]{3,2,1,0:T(8,128)(2,1)S(1)}, u32[]{:S(2)}, u32[]{:S(2)}) collective-permute-start(bf16[2,33,32,256]{3,2,1,0:T(8,128)(2,1)S(1)} %pad_maximum_fusion.1.refs_9_), channel_id=1, source_target_pairs={{0,2},{1,3},{2,0},{3,1},{4,6},{5,7},{6,4},{7,5},{8,10},{9,11},{10,... | collective-permute-start | bytes 3244040 | tf_op jit(solution)/shard_map/ppermute | solution.py:47
  91.3 27.8 %collective-permute-start.21 = (bf16[2,33,32,256]{3,2,1,0:T(8,128)(2,1)S(1)}, bf16[2,33,32,256]{3,2,1,0:T(8,128)(2,1)S(1)}, u32[]{:S(2)}, u32[]{:S(2)}) collective-permute-start(bf16[2,33,32,256]{3,2,1,0:T(8,128)(2,1)S(1)} %collective-permute-done.8.refs_10_), channel_id=1, source_target_pairs={{0,2},{1,3},{2,0},{3,1},{4,6},{5,7},{6,4},{7,5},{8,10},{9,11},{10,... | collective-permute-start | bytes 3244040 | tf_op jit(solution)/shard_map/ppermute | solution.py:47
  101.0 3.8 %collective-permute-start.24 = (bf16[33,32,256]{2,1,0:T(8,128)(2,1)S(1)}, bf16[33,32,256]{2,1,0:T(8,128)(2,1)S(1)}, u32[]{:S(2)}, u32[]{:S(2)}) collective-permute-start(bf16[33,32,256]{2,1,0:T(8,128)(2,1)S(1)} %collective-permute-done.11), channel_id=1, source_target_pairs={{0,2},{1,3},{2,0},{3,1},{4,6},{5,7},{6,4},{7,5},{8,10},{9,11},{10,... | collective-permute-start | bytes 1622024 | tf_op jit(solution)/shard_map/ppermute | solution.py:47
  102.2 14.7 %collective-permute-start.12 = (bf16[33,32,256]{2,1,0:T(8,128)(2,1)S(1)}, bf16[33,32,256]{2,1,0:T(8,128)(2,1)}, u32[]{:S(2)}, u32[]{:S(2)}) collective-permute-start(bf16[33,32,256]{2,1,0:T(8,128)(2,1)S(1)} %collective-permute-done.11), channel_id=1, source_target_pairs={{0,1},{1,0},{2,3},{3,2},{4,5},{5,4},{6,7},{7,6},{8,9},{9,8},{10,11... | collective-permute-start | bytes 1622024 | tf_op jit(solution)/shard_map/ppermute | solution.py:47
  104.7 18.7 %collective-permute-start.22 = (bf16[2,33,32,256]{3,2,1,0:T(8,128)(2,1)}, bf16[2,33,32,256]{3,2,1,0:T(8,128)(2,1)}, u32[]{:S(2)}, u32[]{:S(2)}) collective-permute-start(bf16[2,33,32,256]{3,2,1,0:T(8,128)(2,1)} %collective-permute-done.9.refs_11_), channel_id=1, source_target_pairs={{0,2},{1,3},{2,0},{3,1},{4,6},{5,7},{6,4},{7,5},{8,10},{9,11},{10,... | collective-permute-start | bytes 3244040 | tf_op jit(solution)/shard_map/ppermute | solution.py:47
  116.9 6.5 %collective-permute-start.23 = (bf16[2,33,32,256]{3,2,1,0:T(8,128)(2,1)}, bf16[2,33,32,256]{3,2,1,0:T(8,128)(2,1)}, u32[]{:S(2)}, u32[]{:S(2)}) collective-permute-start(bf16[2,33,32,256]{3,2,1,0:T(8,128)(2,1)} %collective-permute-done.10.refs_12_), channel_id=1, source_target_pairs={{0,2},{1,3},{2,0},{3,1},{4,6},{5,7},{6,4},{7,5},{8,10},{9,11},{10,... | collective-permute-start | bytes 3244040 | tf_op jit(solution)/shard_map/ppermute | solution.py:47
  118.5 4.0 %collective-permute-start.27 = (bf16[33,32,256]{2,1,0:T(8,128)(2,1)}, bf16[33,32,256]{2,1,0:T(8,128)(2,1)S(1)}, u32[]{:S(2)}, u32[]{:S(2)}) collective-permute-start(bf16[33,32,256]{2,1,0:T(8,128)(2,1)} %collective-permute-done.14), channel_id=1, source_target_pairs={{0,2},{1,3},{2,0},{3,1},{4,6},{5,7},{6,4},{7,5},{8,10},{9,11},{10,... | collective-permute-start | bytes 1622024 | tf_op jit(solution)/shard_map/ppermute | solution.py:47
  118.6 3.9 %collective-permute-start.26 = (bf16[33,32,256]{2,1,0:T(8,128)(2,1)S(1)}, bf16[33,32,256]{2,1,0:T(8,128)(2,1)S(1)}, u32[]{:S(2)}, u32[]{:S(2)}) collective-permute-start(bf16[33,32,256]{2,1,0:T(8,128)(2,1)S(1)} %collective-permute-done.13), channel_id=1, source_target_pairs={{0,2},{1,3},{2,0},{3,1},{4,6},{5,7},{6,4},{7,5},{8,10},{9,11},{10,... | collective-permute-start | bytes 1622024 | tf_op jit(solution)/shard_map/ppermute | solution.py:47
  121.0 2.4 %collective-permute-start.25 = (bf16[33,32,256]{2,1,0:T(8,128)(2,1)}, bf16[33,32,256]{2,1,0:T(8,128)(2,1)S(1)}, u32[]{:S(2)}, u32[]{:S(2)}) collective-permute-start(bf16[33,32,256]{2,1,0:T(8,128)(2,1)} %collective-permute-done.12), channel_id=1, source_target_pairs={{0,2},{1,3},{2,0},{3,1},{4,6},{5,7},{6,4},{7,5},{8,10},{9,11},{10,... | collective-permute-start | bytes 1622024 | tf_op jit(solution)/shard_map/ppermute | solution.py:47
  (16 other events, 202.2 us)

commit v3 on v2

--- a/solution.py
+++ b/solution.py
@@ -27,7 +27,7 @@
 CHUNK = 16
 ROWS = 2
 LINE = 4
-CSTEP = 4
+CSTEP = 8
 AXES = ("chan", "freq")
 VMEM = 60 * 1024 * 1024
 INTERPRET = False
@@ -398,24 +398,31 @@
     pairs[1], pairs[3] = along(pairs[0], 1), along(pairs[0], 3)
     two = reached(2)
     after_flip = moved(own_flip, (1, 0, 0))
-    singles = [own, own_flip, after, after_flip]
-    row_flip, row_pair_, pair_, *singles_ = lax.optimization_barrier(
-        (row_flip, row_pair, pairs[0], *singles)
+    row_flip, after_flip, *gated = lax.optimization_barrier(
+        (row_flip, after_flip, own, own_flip, after, pairs[0], row_pair)
     )
-    swapped = [swap(block) for block in (*singles_, pair_, row_pair_, row_flip)]
+    swapped = [
+        swap(jnp.stack([*gated[:3], after_flip])),
+        swap(jnp.concatenate([*gated[3:], row_flip])),
+    ]
     pairs[1], pairs[3], two = lax.optimization_barrier((pairs[1], pairs[3], two))
     two_flip = flip(two)
     cross_two = along(pairs[1][0], 1)
     cross_two_flip = along(pairs[3][1], 3)
-    held = [*singles, pairs[0], row_pair, row_flip, pairs[1], pairs[3]]
-    held += [two, two_flip, cross_two, cross_two_flip]
-    swapped = [*swapped, *(swap(block) for block in held[7:])]
-    names = [[(0, 0, 0)], [(0, 0, 1)], [(0, 2, 0)], [(0, 2, 1)], [(0, 1, 0), (0, 1, 1)]]
-    names += [[(1, 0, 0), (3, 0, 0)], [(1, 0, 1), (3, 0, 1)]]
-    names += [[(1, 1, 0), (1, 1, 1)], [(3, 1, 0), (3, 1, 1)]]
-    names += [[(2, 0, 0)], [(2, 0, 1)], [(2, 1, 0)], [(2, 1, 1)]]
+    late = lax.optimization_barrier(
+        (pairs[1], pairs[3], two, two_flip, cross_two, cross_two_flip)
+    )
+    swapped += [swap(block) for block in late]
+    held = [own, own_flip, after, after_flip, pairs[0], row_pair, row_flip, *late]
+    one_by_one = [[(0, 0, 0)], [(0, 0, 1)], [(0, 2, 0)], [(0, 2, 1)]]
+    in_pairs = [[(0, 1, 0), (0, 1, 1)], [(1, 0, 0), (3, 0, 0)], [(1, 0, 1), (3, 0, 1)]]
+    rest = [[(1, 1, 0), (1, 1, 1)], [(3, 1, 0), (3, 1, 1)]]
+    rest += [[(2, 0, 0)], [(2, 0, 1)], [(2, 1, 0)], [(2, 1, 1)]]
     arrays, lies = [], []
-    for layer, blocks in enumerate((held, swapped)):
+    for layer, blocks, names in (
+        (0, held, one_by_one + in_pairs + rest),
+        (1, swapped, [sum(one_by_one, []), sum(in_pairs, [])] + rest),
+    ):
         for listed, block in zip(names, blocks):
             arrays.append(block if block.ndim == 4 else block[None])
             lies.append([(*name, layer) for name in listed])

time: 159 us -> 146 us (0.918)
  waiting for transfers between devices: 63.2 us -> 46.6 us
  starting transfers between devices: 47.6 us -> 51.6 us
  other arithmetic: 2.57 us -> 4.87 us
    ppermute x28 -> x23, waiting for transfers between devices: 63.2 us -> 46.6 us  [moved(): return lax.ppermute(value, AXES, pairs)]
    ppermute x28 -> x23, starting transfers between devices: 47.6 us -> 51.6 us  [moved(): return lax.ppermute(value, AXES, pairs)]
    concatenate x0 -> x1, other arithmetic: none -> 2.02 us  [local(): jnp.concatenate([*gated[3:], row_flip])]
    unnamed x41 -> x29, local copies, waits for them, and re-layouts: 4.75 us -> 2.92 us
  transfers between devices with their start and end apart: 28 -> 23, of which waited for: 12 -> 13; matrix products, arithmetic and copies ran while one was open for 4% -> 6% of each run, Pallas kernels for 0% -> 0%
where the time goes in v3:
time: 146 us
  starting transfers between devices  51.6 us (35%)
  waiting for transfers between devices  46.6 us (32%)
  Pallas kernels  36.3 us (25%)
  local copies, waits for them, and re-layouts  5.93 us (4%)
  other arithmetic  4.87 us (3%)
    ppermute x23, starting transfers between devices, moved(): return lax.ppermute(value, AXES, pairs)  51.6 us
    ppermute x23, waiting for transfers between devices, moved(): return lax.ppermute(value, AXES, pairs)  46.6 us
    pallas_call x1, Pallas kernels, band_lags(): pl.pallas_call(lambda *refs: band_kernel(lies, *refs), grid=(corr_steps +...  33.1 us
    pallas_call x1, Pallas kernels, whiten(): pl.pallas_call(whiten_kernel, out_shape=jax.ShapeDtypeStruct((GROUPS + 1,...  3.13 us
  transfers between devices with their start and end apart: 23, of which 13 were waited for; matrix products, arithmetic and copies ran while one was open for 6% of the time, Pallas kernels for 0%

profile of v3, /device:TPU:1, one launch (start us, length us, event | category | flops | bytes accessed | tf_op | source)
XLA Modules:
  0.0 145.6 jit_solution(6974403182501347547)
XLA Ops:
  0.0 1.0 slice_select_fusion
  1.0 3.8 %collective-permute-start = (bf16[2,8,32,128]{3,2,1,0:T(8,128)(2,1)S(1)}, bf16[2,8,32,128]{3,2,1,0:T(8,128)(2,1)S(1)}, u32[]{:S(2)}, u32[]{:S(2)}) collective-permute-start(bf16[2,8,32,128]{3,2,1,0:T(8,128)(2,1)S(1)} %slice_select_fusion), channel_id=1, source_target_pairs={{0,1},{1,0},{2,3},{3,2},{4,5},{5,4},{6,7},{7,6},{8,9},{9,8},{10,11... | collective-permute-start | bytes 393224 | tf_op jit(solution)/shard_map/ppermute | solution.py:47
  4.8 1.4 copy.4.mask_ref
  6.2 1.0 collective-permute-done.rim_ref
  7.8 3.1 %whiten.1.refs_1_.refs_2_ = bf16[33,32,256]{2,1,0:T(8,128)(2,1)} custom-call(s32[1]{0:T(128)} %bitcast.3.rank_ref, bf16[2,8,32,512]{3,2,1,0:T(8,128)(2,1)} %spectra_ref.1, bf16[2,8,32,128]{3,2,1,0:T(8,128)(2,1)} %copy-done.7, s32[32,8]{1,0:T(8,128)} %copy.4.mask_ref), custom_call_target="tpu_custom_call" | custom-call | tf_op jit(solution)/shard_map/whiten/pallas_call | solution.py:104
  11.0 6.2 %collective-permute-start.1 = (bf16[33,32,256]{2,1,0:T(8,128)(2,1)}, bf16[33,32,256]{2,1,0:T(8,128)(2,1)S(1)}, u32[]{:S(2)}, u32[]{:S(2)}) collective-permute-start(bf16[33,32,256]{2,1,0:T(8,128)(2,1)} %whiten.1.refs_1_.refs_2_), channel_id=1, source_target_pairs={{0,224},{1,225},{2,226},{3,227},{4,228},{5,229},{6,230},{7,231},{8... | collective-permute-start | bytes 1622024 | tf_op jit(solution)/shard_map/ppermute | solution.py:47
  17.1 2.9 %collective-permute-start.6 = (bf16[33,32,256]{2,1,0:T(8,128)(2,1)}, bf16[33,32,256]{2,1,0:T(8,128)(2,1)S(1)}, u32[]{:S(2)}, u32[]{:S(2)}) collective-permute-start(bf16[33,32,256]{2,1,0:T(8,128)(2,1)} %whiten.1.refs_1_.refs_2_), channel_id=1, source_target_pairs={{0,1},{1,0},{2,3},{3,2},{4,5},{5,4},{6,7},{7,6},{8,9},{9,8},{10,11... | collective-permute-start | bytes 1622024 | tf_op jit(solution)/shard_map/ppermute | solution.py:47
  20.1 7.4 %collective-permute-done.1 = bf16[33,32,256]{2,1,0:T(8,128)(2,1)S(1)} collective-permute-done((bf16[33,32,256]{2,1,0:T(8,128)(2,1)}, bf16[33,32,256]{2,1,0:T(8,128)(2,1)S(1)}, u32[]{:S(2)}, u32[]{:S(2)}) %collective-permute-start.1) | collective-permute-done | bytes 540704 | tf_op jit(solution)/shard_map/ppermute | solution.py:47
  27.5 1.4 broadcast_select_fusion
  28.9 1.3 collective-permute-start.3
  30.2 1.5 %collective-permute-start.2 = (bf16[33,32,256]{2,1,0:T(8,128)(2,1)S(1)}, bf16[33,32,256]{2,1,0:T(8,128)(2,1)S(1)}, u32[]{:S(2)}, u32[]{:S(2)}) collective-permute-start(bf16[33,32,256]{2,1,0:T(8,128)(2,1)S(1)} %get-tuple-element.54), channel_id=1, source_target_pairs={{0,12},{1,13},{2,14},{3,15},{4,0},{5,1},{6,2},{7,3},{8,4},{9,5},{1... | collective-permute-start | bytes 1622024 | tf_op jit(solution)/shard_map/ppermute | solution.py:47
  31.6 2.7 %collective-permute-start.5 = (bf16[33,32,256]{2,1,0:T(8,128)(2,1)S(1)}, bf16[33,32,256]{2,1,0:T(8,128)(2,1)S(1)}, u32[]{:S(2)}, u32[]{:S(2)}) collective-permute-start(bf16[33,32,256]{2,1,0:T(8,128)(2,1)S(1)} %get-tuple-element.52), channel_id=1, source_target_pairs={{0,17},{1,16},{2,19},{3,18},{4,21},{5,20},{6,23},{7,22},{8,25},{9,... | collective-permute-start | bytes 1622024 | tf_op jit(solution)/shard_map/ppermute | solution.py:47
  34.4 7.1 %collective-permute-done.3 = bf16[33,32,256]{2,1,0:T(8,128)(2,1)S(1)} collective-permute-done((bf16[33,32,256]{2,1,0:T(8,128)(2,1)S(1)}, bf16[33,32,256]{2,1,0:T(8,128)(2,1)S(1)}, u32[]{:S(2)}, u32[]{:S(2)}) %collective-permute-start.3) | collective-permute-done | bytes 540704 | tf_op jit(solution)/shard_map/ppermute | solution.py:47
  41.5 2.3 %collective-permute-done.5 = bf16[33,32,256]{2,1,0:T(8,128)(2,1)S(1)} collective-permute-done((bf16[33,32,256]{2,1,0:T(8,128)(2,1)S(1)}, bf16[33,32,256]{2,1,0:T(8,128)(2,1)S(1)}, u32[]{:S(2)}, u32[]{:S(2)}) %collective-permute-start.5) | collective-permute-done | bytes 540704 | tf_op jit(solution)/shard_map/ppermute | solution.py:47
  43.7 1.1 collective-permute-done.4
  45.5 3.3 %collective-permute-start.8 = (bf16[33,32,256]{2,1,0:T(8,128)(2,1)S(1)}, bf16[33,32,256]{2,1,0:T(8,128)(2,1)S(1)}, u32[]{:S(2)}, u32[]{:S(2)}) collective-permute-start(bf16[33,32,256]{2,1,0:T(8,128)(2,1)S(1)} %collective-permute-done.6.refs_3_), channel_id=1, source_target_pairs={{0,224},{1,225},{2,226},{3,227},{4,228},{5,229},{6,230},{7,231},{8... | collective-permute-start | bytes 1622024 | tf_op jit(solution)/shard_map/ppermute | solution.py:47
  49.0 2.6 %collective-permute-start.9 = (bf16[2,33,32,256]{3,2,1,0:T(8,128)(2,1)S(1)}, bf16[2,33,32,256]{3,2,1,0:T(8,128)(2,1)}, u32[]{:S(2)}, u32[]{:S(2)}) collective-permute-start(bf16[2,33,32,256]{3,2,1,0:T(8,128)(2,1)S(1)} %pad_maximum_fusion.3.refs_8_), channel_id=1, source_target_pairs={{0,12},{1,13},{2,14},{3,15},{4,0},{5,1},{6,2},{7,3},{8,4},{9,5},{1... | collective-permute-start | bytes 3244040 | tf_op jit(solution)/shard_map/ppermute | solution.py:47
  52.0 4.0 %collective-permute-done.8 = bf16[33,32,256]{2,1,0:T(8,128)(2,1)S(1)} collective-permute-done((bf16[33,32,256]{2,1,0:T(8,128)(2,1)S(1)}, bf16[33,32,256]{2,1,0:T(8,128)(2,1)S(1)}, u32[]{:S(2)}, u32[]{:S(2)}) %collective-permute-start.8) | collective-permute-done | bytes 540704 | tf_op jit(solution)/shard_map/ppermute | solution.py:47
  56.0 11.4 %collective-permute-done.7.refs_10_ = bf16[2,33,32,256]{3,2,1,0:T(8,128)(2,1)S(1)} collective-permute-done((bf16[2,33,32,256]{3,2,1,0:T(8,128)(2,1)S(1)}, bf16[2,33,32,256]{3,2,1,0:T(8,128)(2,1)S(1)}, u32[]{:S(2)}, u32[]{:S(2)}) %collective-permute-start.7) | collective-permute-done | bytes 1081376 | tf_op jit(solution)/shard_map/ppermute | solution.py:47
  67.4 2.0 %pad_maximum_fusion = bf16[6,33,32,256]{3,2,1,0:T(8,128)(2,1)} fusion(bf16[2,33,32,256]{3,2,1,0:T(8,128)(2,1)S(1)} %collective-permute-done.7.refs_10_, bf16[2,33,32,256]{3,2,1,0:T(8,128)(2,1)S(1)} %pad_maximum_fusion.2.refs_9_, bf16[2,33,32,256]{3,2,1,0:T(8,128)(2,1)S(1)} %pad_maximum_fusion.3.refs_8_), kind=kLoop, calls=%fused_computation | loop fusion | flops 3244032 | bytes 6488064 | tf_op jit(solution)/shard_map/concatenate | solution.py:406
  69.5 5.4 %collective-permute-start.16 = (bf16[6,33,32,256]{3,2,1,0:T(8,128)(2,1)}, bf16[6,33,32,256]{3,2,1,0:T(8,128)(2,1)}, u32[]{:S(2)}, u32[]{:S(2)}) collective-permute-start(bf16[6,33,32,256]{3,2,1,0:T(8,128)(2,1)} %pad_maximum_fusion), channel_id=1, source_target_pairs={{0,2},{1,3},{2,0},{3,1},{4,6},{5,7},{6,4},{7,5},{8,10},{9,11},{10,... | collective-permute-start | bytes 9732104 | tf_op jit(solution)/shard_map/ppermute | solution.py:47
  74.9 7.8 %collective-permute-done.11 = bf16[33,32,256]{2,1,0:T(8,128)(2,1)S(1)} collective-permute-done((bf16[33,32,256]{2,1,0:T(8,128)(2,1)S(1)}, bf16[33,32,256]{2,1,0:T(8,128)(2,1)S(1)}, u32[]{:S(2)}, u32[]{:S(2)}) %collective-permute-start.11) | collective-permute-done | bytes 540704 | tf_op jit(solution)/shard_map/ppermute | solution.py:47
  82.7 1.3 slice_bitcast_fusion
  84.6 1.1 slice_bitcast_fusion.1
  85.7 2.2 %collective-permute-start.13 = (bf16[33,32,256]{2,1,0:T(8,128)(2,1)S(1)}, bf16[33,32,256]{2,1,0:T(8,128)(2,1)S(1)}, u32[]{:S(2)}, u32[]{:S(2)}) collective-permute-start(bf16[33,32,256]{2,1,0:T(8,128)(2,1)S(1)} %slice_bitcast_fusion.1), channel_id=1, source_target_pairs={{0,12},{1,13},{2,14},{3,15},{4,0},{5,1},{6,2},{7,3},{8,4},{9,5},{1... | collective-permute-start | bytes 1622024 | tf_op jit(solution)/shard_map/ppermute | solution.py:47
  87.9 1.7 %collective-permute-start.12 = (bf16[33,32,256]{2,1,0:T(8,128)(2,1)S(1)}, bf16[33,32,256]{2,1,0:T(8,128)(2,1)S(1)}, u32[]{:S(2)}, u32[]{:S(2)}) collective-permute-start(bf16[33,32,256]{2,1,0:T(8,128)(2,1)S(1)} %collective-permute-done.11), channel_id=1, source_target_pairs={{0,1},{1,0},{2,3},{3,2},{4,5},{5,4},{6,7},{7,6},{8,9},{9,8},{10,11... | collective-permute-start | bytes 1622024 | tf_op jit(solution)/shard_map/ppermute | solution.py:47
  89.9 7.4 %collective-permute-start.15 = (bf16[4,33,32,256]{3,2,1,0:T(8,128)(2,1)S(1)}, bf16[4,33,32,256]{3,2,1,0:T(8,128)(2,1)}, u32[]{:S(2)}, u32[]{:S(2)}) collective-permute-start(bf16[4,33,32,256]{3,2,1,0:T(8,128)(2,1)S(1)} %pad_maximum_fusion.1), channel_id=1, source_target_pairs={{0,2},{1,3},{2,0},{3,1},{4,6},{5,7},{6,4},{7,5},{8,10},{9,11},{10,... | collective-permute-start | bytes 6488072 | tf_op jit(solution)/shard_map/ppermute | solution.py:47
  97.6 7.3 %collective-permute-start.19 = (bf16[33,32,256]{2,1,0:T(8,128)(2,1)S(1)}, bf16[33,32,256]{2,1,0:T(8,128)(2,1)S(1)}, u32[]{:S(2)}, u32[]{:S(2)}) collective-permute-start(bf16[33,32,256]{2,1,0:T(8,128)(2,1)S(1)} %collective-permute-done.11), channel_id=1, source_target_pairs={{0,2},{1,3},{2,0},{3,1},{4,6},{5,7},{6,4},{7,5},{8,10},{9,11},{10,... | collective-permute-start | bytes 1622024 | tf_op jit(solution)/shard_map/ppermute | solution.py:47
  105.5 1.0 collective-permute-done.19
  108.1 0.8 copy-done.13
  109.9 2.4 %collective-permute-done.22 = bf16[33,32,256]{2,1,0:T(8,128)(2,1)} collective-permute-done((bf16[33,32,256]{2,1,0:T(8,128)(2,1)}, bf16[33,32,256]{2,1,0:T(8,128)(2,1)}, u32[]{:S(2)}, u32[]{:S(2)}) %collective-permute-start.22) | collective-permute-done | bytes 540704 | tf_op jit(solution)/shard_map/ppermute | solution.py:47
  112.3 33.1 %band_lags.1 = bf16[256,32,512]{2,1,0:T(8,128)(2,1)} custom-call(s32[5]{0:T(128)} %stack.50.refs_0_, bf16[33,32,256]{2,1,0:T(8,128)(2,1)} %whiten.1.refs_1_.refs_2_, bf16[33,32,256]{2,1,0:T(8,128)(2,1)} %whiten.1.refs_1_.refs_2_, bf16[33,32,256]{2,1,0:T(8,128)(2,1)} %copy-done.5, bf16[1,33,32,256]{3,2,1,0:T(8,128)(2,1)} %bitcast.28, ...), custom_call_target="tpu_custom_call" | custom-call | flops 17179869184 | bytes 27262976 | tf_op jit(solution)/shard_map/band_lags/pallas_call | solution.py:320
  (54 shorter events, 6.3 us)
Async XLA Ops:
  1.0 6.2 %collective-permute-start = (bf16[2,8,32,128]{3,2,1,0:T(8,128)(2,1)S(1)}, bf16[2,8,32,128]{3,2,1,0:T(8,128)(2,1)S(1)}, u32[]{:S(2)}, u32[]{:S(2)}) collective-permute-start(bf16[2,8,32,128]{3,2,1,0:T(8,128)(2,1)S(1)} %slice_select_fusion), channel_id=1, source_target_pairs={{0,1},{1,0},{2,3},{3,2},{4,5},{5,4},{6,7},{7,6},{8,9},{9,8},{10,11... | collective-permute-start | bytes 393224 | tf_op jit(solution)/shard_map/ppermute | solution.py:47
  11.0 16.5 %collective-permute-start.1 = (bf16[33,32,256]{2,1,0:T(8,128)(2,1)}, bf16[33,32,256]{2,1,0:T(8,128)(2,1)S(1)}, u32[]{:S(2)}, u32[]{:S(2)}) collective-permute-start(bf16[33,32,256]{2,1,0:T(8,128)(2,1)} %whiten.1.refs_1_.refs_2_), channel_id=1, source_target_pairs={{0,224},{1,225},{2,226},{3,227},{4,228},{5,229},{6,230},{7,231},{8... | collective-permute-start | bytes 1622024 | tf_op jit(solution)/shard_map/ppermute | solution.py:47
  17.1 17.2 %collective-permute-start.6 = (bf16[33,32,256]{2,1,0:T(8,128)(2,1)}, bf16[33,32,256]{2,1,0:T(8,128)(2,1)S(1)}, u32[]{:S(2)}, u32[]{:S(2)}) collective-permute-start(bf16[33,32,256]{2,1,0:T(8,128)(2,1)} %whiten.1.refs_1_.refs_2_), channel_id=1, source_target_pairs={{0,1},{1,0},{2,3},{3,2},{4,5},{5,4},{6,7},{7,6},{8,9},{9,8},{10,11... | collective-permute-start | bytes 1622024 | tf_op jit(solution)/shard_map/ppermute | solution.py:47
  27.5 62.1 %copy-start.3 = (bf16[33,32,256]{2,1,0:T(8,128)(2,1)}, bf16[33,32,256]{2,1,0:T(8,128)(2,1)S(1)}, u32[]{:S(2)}) copy-start(bf16[33,32,256]{2,1,0:T(8,128)(2,1)S(1)} %collective-permute-done.1) | copy-start | bytes 1622020
  28.9 12.6 %collective-permute-start.3 = (bf16[33,32,256]{2,1,0:T(8,128)(2,1)S(1)}, bf16[33,32,256]{2,1,0:T(8,128)(2,1)S(1)}, u32[]{:S(2)}, u32[]{:S(2)}) collective-permute-start(bf16[33,32,256]{2,1,0:T(8,128)(2,1)S(1)} %get-tuple-element.53), channel_id=1, source_target_pairs={{0,4},{1,5},{2,6},{3,7},{4,8},{5,9},{6,10},{7,11},{8,12},{9,13},{1... | collective-permute-start | bytes 1622024 | tf_op jit(solution)/shard_map/ppermute | solution.py:47
  30.2 11.3 %collective-permute-start.2 = (bf16[33,32,256]{2,1,0:T(8,128)(2,1)S(1)}, bf16[33,32,256]{2,1,0:T(8,128)(2,1)S(1)}, u32[]{:S(2)}, u32[]{:S(2)}) collective-permute-start(bf16[33,32,256]{2,1,0:T(8,128)(2,1)S(1)} %get-tuple-element.54), channel_id=1, source_target_pairs={{0,12},{1,13},{2,14},{3,15},{4,0},{5,1},{6,2},{7,3},{8,4},{9,5},{1... | collective-permute-start | bytes 1622024 | tf_op jit(solution)/shard_map/ppermute | solution.py:47
  31.6 12.1 %collective-permute-start.5 = (bf16[33,32,256]{2,1,0:T(8,128)(2,1)S(1)}, bf16[33,32,256]{2,1,0:T(8,128)(2,1)S(1)}, u32[]{:S(2)}, u32[]{:S(2)}) collective-permute-start(bf16[33,32,256]{2,1,0:T(8,128)(2,1)S(1)} %get-tuple-element.52), channel_id=1, source_target_pairs={{0,17},{1,16},{2,19},{3,18},{4,21},{5,20},{6,23},{7,22},{8,25},{9,... | collective-permute-start | bytes 1622024 | tf_op jit(solution)/shard_map/ppermute | solution.py:47
  34.4 10.5 %collective-permute-start.4 = (bf16[33,32,256]{2,1,0:T(8,128)(2,1)S(1)}, bf16[33,32,256]{2,1,0:T(8,128)(2,1)S(1)}, u32[]{:S(2)}, u32[]{:S(2)}) collective-permute-start(bf16[33,32,256]{2,1,0:T(8,128)(2,1)S(1)} %get-tuple-element.52), channel_id=1, source_target_pairs={{0,16},{1,17},{2,18},{3,19},{4,20},{5,21},{6,22},{7,23},{8,24},{9,... | collective-permute-start | bytes 1622024 | tf_op jit(solution)/shard_map/ppermute | solution.py:47
  34.4 55.2 %copy-start.5 = (bf16[33,32,256]{2,1,0:T(8,128)(2,1)}, bf16[33,32,256]{2,1,0:T(8,128)(2,1)S(1)}, u32[]{:S(2)}) copy-start(bf16[33,32,256]{2,1,0:T(8,128)(2,1)S(1)} %collective-permute-done.6.refs_3_) | copy-start | bytes 1622020
  44.9 22.5 %copy-start.1 = (bf16[2,33,32,256]{3,2,1,0:T(8,128)(2,1)}, bf16[2,33,32,256]{3,2,1,0:T(8,128)(2,1)S(1)}, u32[]{:S(2)}) copy-start(bf16[2,33,32,256]{3,2,1,0:T(8,128)(2,1)S(1)} %pad_maximum_fusion.2.refs_9_) | copy-start | bytes 3244036
  44.9 22.5 %collective-permute-start.7 = (bf16[2,33,32,256]{3,2,1,0:T(8,128)(2,1)S(1)}, bf16[2,33,32,256]{3,2,1,0:T(8,128)(2,1)S(1)}, u32[]{:S(2)}, u32[]{:S(2)}) collective-permute-start(bf16[2,33,32,256]{3,2,1,0:T(8,128)(2,1)S(1)} %pad_maximum_fusion.2.refs_9_), channel_id=1, source_target_pairs={{0,1},{1,0},{2,3},{3,2},{4,5},{5,4},{6,7},{7,6},{8,9},{9,8},{10,11... | collective-permute-start | bytes 3244040 | tf_op jit(solution)/shard_map/ppermute | solution.py:47
  45.5 10.5 %collective-permute-start.8 = (bf16[33,32,256]{2,1,0:T(8,128)(2,1)S(1)}, bf16[33,32,256]{2,1,0:T(8,128)(2,1)S(1)}, u32[]{:S(2)}, u32[]{:S(2)}) collective-permute-start(bf16[33,32,256]{2,1,0:T(8,128)(2,1)S(1)} %collective-permute-done.6.refs_3_), channel_id=1, source_target_pairs={{0,224},{1,225},{2,226},{3,227},{4,228},{5,229},{6,230},{7,231},{8... | collective-permute-start | bytes 1622024 | tf_op jit(solution)/shard_map/ppermute | solution.py:47
  48.9 20.5 %copy-start.2 = (bf16[2,33,32,256]{3,2,1,0:T(8,128)(2,1)}, bf16[2,33,32,256]{3,2,1,0:T(8,128)(2,1)S(1)}, u32[]{:S(2)}) copy-start(bf16[2,33,32,256]{3,2,1,0:T(8,128)(2,1)S(1)} %pad_maximum_fusion.3.refs_8_) | copy-start | bytes 3244036
  48.9 33.8 %collective-permute-start.10 = (bf16[2,33,32,256]{3,2,1,0:T(8,128)(2,1)S(1)}, bf16[2,33,32,256]{3,2,1,0:T(8,128)(2,1)}, u32[]{:S(2)}, u32[]{:S(2)}) collective-permute-start(bf16[2,33,32,256]{3,2,1,0:T(8,128)(2,1)S(1)} %pad_maximum_fusion.3.refs_8_), channel_id=1, source_target_pairs={{0,4},{1,5},{2,6},{3,7},{4,8},{5,9},{6,10},{7,11},{8,12},{9,13},{1... | collective-permute-start | bytes 3244040 | tf_op jit(solution)/shard_map/ppermute | solution.py:47
  49.0 33.7 %collective-permute-start.9 = (bf16[2,33,32,256]{3,2,1,0:T(8,128)(2,1)S(1)}, bf16[2,33,32,256]{3,2,1,0:T(8,128)(2,1)}, u32[]{:S(2)}, u32[]{:S(2)}) collective-permute-start(bf16[2,33,32,256]{3,2,1,0:T(8,128)(2,1)S(1)} %pad_maximum_fusion.3.refs_8_), channel_id=1, source_target_pairs={{0,12},{1,13},{2,14},{3,15},{4,0},{5,1},{6,2},{7,3},{8,4},{9,5},{1... | collective-permute-start | bytes 3244040 | tf_op jit(solution)/shard_map/ppermute | solution.py:47
  51.7 31.0 %collective-permute-start.11 = (bf16[33,32,256]{2,1,0:T(8,128)(2,1)S(1)}, bf16[33,32,256]{2,1,0:T(8,128)(2,1)S(1)}, u32[]{:S(2)}, u32[]{:S(2)}) collective-permute-start(bf16[33,32,256]{2,1,0:T(8,128)(2,1)S(1)} %get-tuple-element.51), channel_id=1, source_target_pairs={{0,8},{1,9},{2,10},{3,11},{4,12},{5,13},{6,14},{7,15},{8,0},{9,1},... | collective-permute-start | bytes 1622024 | tf_op jit(solution)/shard_map/ppermute | solution.py:47
  56.0 33.6 %copy-start.6 = (bf16[33,32,256]{2,1,0:T(8,128)(2,1)}, bf16[33,32,256]{2,1,0:T(8,128)(2,1)S(1)}, u32[]{:S(2)}) copy-start(bf16[33,32,256]{2,1,0:T(8,128)(2,1)S(1)} %collective-permute-done.8) | copy-start | bytes 1622020
  69.5 20.1 %copy-start = (bf16[33,32,256]{2,1,0:T(8,128)(2,1)S(1)}, bf16[33,32,256]{2,1,0:T(8,128)(2,1)}, u32[]{:S(2)}) copy-start(bf16[33,32,256]{2,1,0:T(8,128)(2,1)} %whiten.1.refs_1_.refs_2_) | copy-start | bytes 1622020
  69.5 42.8 %collective-permute-start.16 = (bf16[6,33,32,256]{3,2,1,0:T(8,128)(2,1)}, bf16[6,33,32,256]{3,2,1,0:T(8,128)(2,1)}, u32[]{:S(2)}, u32[]{:S(2)}) collective-permute-start(bf16[6,33,32,256]{3,2,1,0:T(8,128)(2,1)} %pad_maximum_fusion), channel_id=1, source_target_pairs={{0,2},{1,3},{2,0},{3,1},{4,6},{5,7},{6,4},{7,5},{8,10},{9,11},{10,... | collective-permute-start | bytes 9732104 | tf_op jit(solution)/shard_map/ppermute | solution.py:47
  82.7 14.9 %copy-start.8 = (bf16[33,32,256]{2,1,0:T(8,128)(2,1)}, bf16[33,32,256]{2,1,0:T(8,128)(2,1)S(1)}, u32[]{:S(2)}) copy-start(bf16[33,32,256]{2,1,0:T(8,128)(2,1)S(1)} %collective-permute-done.11) | copy-start | bytes 1622020
  84.0 13.3 %collective-permute-start.14 = (bf16[33,32,256]{2,1,0:T(8,128)(2,1)S(1)}, bf16[33,32,256]{2,1,0:T(8,128)(2,1)}, u32[]{:S(2)}, u32[]{:S(2)}) collective-permute-start(bf16[33,32,256]{2,1,0:T(8,128)(2,1)S(1)} %slice_bitcast_fusion), channel_id=1, source_target_pairs={{0,4},{1,5},{2,6},{3,7},{4,8},{5,9},{6,10},{7,11},{8,12},{9,13},{1... | collective-permute-start | bytes 1622024 | tf_op jit(solution)/shard_map/ppermute | solution.py:47
  85.7 11.5 %collective-permute-start.13 = (bf16[33,32,256]{2,1,0:T(8,128)(2,1)S(1)}, bf16[33,32,256]{2,1,0:T(8,128)(2,1)S(1)}, u32[]{:S(2)}, u32[]{:S(2)}) collective-permute-start(bf16[33,32,256]{2,1,0:T(8,128)(2,1)S(1)} %slice_bitcast_fusion.1), channel_id=1, source_target_pairs={{0,12},{1,13},{2,14},{3,15},{4,0},{5,1},{6,2},{7,3},{8,4},{9,5},{1... | collective-permute-start | bytes 1622024 | tf_op jit(solution)/shard_map/ppermute | solution.py:47
  87.9 9.7 %collective-permute-start.12 = (bf16[33,32,256]{2,1,0:T(8,128)(2,1)S(1)}, bf16[33,32,256]{2,1,0:T(8,128)(2,1)S(1)}, u32[]{:S(2)}, u32[]{:S(2)}) collective-permute-start(bf16[33,32,256]{2,1,0:T(8,128)(2,1)S(1)} %collective-permute-done.11), channel_id=1, source_target_pairs={{0,1},{1,0},{2,3},{3,2},{4,5},{5,4},{6,7},{7,6},{8,9},{9,8},{10,11... | collective-permute-start | bytes 1622024 | tf_op jit(solution)/shard_map/ppermute | solution.py:47
  89.9 22.4 %collective-permute-start.15 = (bf16[4,33,32,256]{3,2,1,0:T(8,128)(2,1)S(1)}, bf16[4,33,32,256]{3,2,1,0:T(8,128)(2,1)}, u32[]{:S(2)}, u32[]{:S(2)}) collective-permute-start(bf16[4,33,32,256]{3,2,1,0:T(8,128)(2,1)S(1)} %pad_maximum_fusion.1), channel_id=1, source_target_pairs={{0,2},{1,3},{2,0},{3,1},{4,6},{5,7},{6,4},{7,5},{8,10},{9,11},{10,... | collective-permute-start | bytes 6488072 | tf_op jit(solution)/shard_map/ppermute | solution.py:47
  97.2 9.3 %copy-start.9 = (bf16[33,32,256]{2,1,0:T(8,128)(2,1)}, bf16[33,32,256]{2,1,0:T(8,128)(2,1)S(1)}, u32[]{:S(2)}) copy-start(bf16[33,32,256]{2,1,0:T(8,128)(2,1)S(1)} %collective-permute-done.13) | copy-start | bytes 1622020
  97.6 10.5 %copy-start.10 = (bf16[33,32,256]{2,1,0:T(8,128)(2,1)}, bf16[33,32,256]{2,1,0:T(8,128)(2,1)S(1)}, u32[]{:S(2)}) copy-start(bf16[33,32,256]{2,1,0:T(8,128)(2,1)S(1)} %collective-permute-done.12) | copy-start | bytes 1622020
  97.6 8.9 %collective-permute-start.19 = (bf16[33,32,256]{2,1,0:T(8,128)(2,1)S(1)}, bf16[33,32,256]{2,1,0:T(8,128)(2,1)S(1)}, u32[]{:S(2)}, u32[]{:S(2)}) collective-permute-start(bf16[33,32,256]{2,1,0:T(8,128)(2,1)S(1)} %collective-permute-done.11), channel_id=1, source_target_pairs={{0,2},{1,3},{2,0},{3,1},{4,6},{5,7},{6,4},{7,5},{8,10},{9,11},{10,... | collective-permute-start | bytes 1622024 | tf_op jit(solution)/shard_map/ppermute | solution.py:47
  105.0 2.3 %collective-permute-start.20 = (bf16[33,32,256]{2,1,0:T(8,128)(2,1)S(1)}, bf16[33,32,256]{2,1,0:T(8,128)(2,1)S(1)}, u32[]{:S(2)}, u32[]{:S(2)}) collective-permute-start(bf16[33,32,256]{2,1,0:T(8,128)(2,1)S(1)} %collective-permute-done.12), channel_id=1, source_target_pairs={{0,2},{1,3},{2,0},{3,1},{4,6},{5,7},{6,4},{7,5},{8,10},{9,11},{10,... | collective-permute-start | bytes 1622024 | tf_op jit(solution)/shard_map/ppermute | solution.py:47
  105.0 3.0 %collective-permute-start.21 = (bf16[33,32,256]{2,1,0:T(8,128)(2,1)S(1)}, bf16[33,32,256]{2,1,0:T(8,128)(2,1)S(1)}, u32[]{:S(2)}, u32[]{:S(2)}) collective-permute-start(bf16[33,32,256]{2,1,0:T(8,128)(2,1)S(1)} %collective-permute-done.13), channel_id=1, source_target_pairs={{0,2},{1,3},{2,0},{3,1},{4,6},{5,7},{6,4},{7,5},{8,10},{9,11},{10,... | collective-permute-start | bytes 1622024 | tf_op jit(solution)/shard_map/ppermute | solution.py:47
  106.5 5.8 %collective-permute-start.17 = (bf16[2,33,32,256]{3,2,1,0:T(8,128)(2,1)}, bf16[2,33,32,256]{3,2,1,0:T(8,128)(2,1)}, u32[]{:S(2)}, u32[]{:S(2)}) collective-permute-start(bf16[2,33,32,256]{3,2,1,0:T(8,128)(2,1)} %collective-permute-done.9.refs_11_), channel_id=1, source_target_pairs={{0,2},{1,3},{2,0},{3,1},{4,6},{5,7},{6,4},{7,5},{8,10},{9,11},{10,... | collective-permute-start | bytes 3244040 | tf_op jit(solution)/shard_map/ppermute | solution.py:47
  107.3 5.0 %collective-permute-start.18 = (bf16[2,33,32,256]{3,2,1,0:T(8,128)(2,1)}, bf16[2,33,32,256]{3,2,1,0:T(8,128)(2,1)}, u32[]{:S(2)}, u32[]{:S(2)}) collective-permute-start(bf16[2,33,32,256]{3,2,1,0:T(8,128)(2,1)} %collective-permute-done.10.refs_12_), channel_id=1, source_target_pairs={{0,2},{1,3},{2,0},{3,1},{4,6},{5,7},{6,4},{7,5},{8,10},{9,11},{10,... | collective-permute-start | bytes 3244040 | tf_op jit(solution)/shard_map/ppermute | solution.py:47
  108.9 3.4 %collective-permute-start.22 = (bf16[33,32,256]{2,1,0:T(8,128)(2,1)}, bf16[33,32,256]{2,1,0:T(8,128)(2,1)}, u32[]{:S(2)}, u32[]{:S(2)}) collective-permute-start(bf16[33,32,256]{2,1,0:T(8,128)(2,1)} %collective-permute-done.14), channel_id=1, source_target_pairs={{0,2},{1,3},{2,0},{3,1},{4,6},{5,7},{6,4},{7,5},{8,10},{9,11},{10,... | collective-permute-start | bytes 1622024 | tf_op jit(solution)/shard_map/ppermute | solution.py:47
  (5 other events, 14.3 us)

commit v4 on v2

--- a/solution.py
+++ b/solution.py
@@ -27,7 +27,7 @@
 CHUNK = 16
 ROWS = 2
 LINE = 4
-CSTEP = 4
+CSTEP = 8
 AXES = ("chan", "freq")
 VMEM = 60 * 1024 * 1024
 INTERPRET = False
@@ -386,36 +386,39 @@
     own_flip = flip(own)
     own, after = lax.optimization_barrier((own, after))
     crossing = jnp.where(row == 1, own, after)
-    one, three = reached(1), reached(3)
+    one, three, two = reached(1), reached(3), reached(2)
     cross = moved(crossing, (0, 1, 0))
     cross_flip = moved(crossing, (0, 1, 0), freq=1)
-    one, three, cross, cross_flip, own_flip = lax.optimization_barrier(
-        (one, three, cross, cross_flip, own_flip)
+    one, three, two, cross, cross_flip, own_flip = lax.optimization_barrier(
+        (one, three, two, cross, cross_flip, own_flip)
     )
     pairs = {0: jnp.stack([cross, cross_flip])}
     row_pair = jnp.stack([one, three])
     row_flip = flip(row_pair)
     pairs[1], pairs[3] = along(pairs[0], 1), along(pairs[0], 3)
-    two = reached(2)
-    after_flip = moved(own_flip, (1, 0, 0))
-    singles = [own, own_flip, after, after_flip]
-    row_flip, row_pair_, pair_, *singles_ = lax.optimization_barrier(
-        (row_flip, row_pair, pairs[0], *singles)
+    first = [own, own_flip, after]
+    early = [swap(jnp.concatenate([jnp.stack(first), pairs[0]])), swap(row_pair)]
+    row_flip, pairs[1], pairs[3], own_flip_ = lax.optimization_barrier(
+        (row_flip, pairs[1], pairs[3], own_flip)
     )
-    swapped = [swap(block) for block in (*singles_, pair_, row_pair_, row_flip)]
-    pairs[1], pairs[3], two = lax.optimization_barrier((pairs[1], pairs[3], two))
     two_flip = flip(two)
     cross_two = along(pairs[1][0], 1)
     cross_two_flip = along(pairs[3][1], 3)
-    held = [*singles, pairs[0], row_pair, row_flip, pairs[1], pairs[3]]
-    held += [two, two_flip, cross_two, cross_two_flip]
-    swapped = [*swapped, *(swap(block) for block in held[7:])]
-    names = [[(0, 0, 0)], [(0, 0, 1)], [(0, 2, 0)], [(0, 2, 1)], [(0, 1, 0), (0, 1, 1)]]
-    names += [[(1, 0, 0), (3, 0, 0)], [(1, 0, 1), (3, 0, 1)]]
-    names += [[(1, 1, 0), (1, 1, 1)], [(3, 1, 0), (3, 1, 1)]]
-    names += [[(2, 0, 0)], [(2, 0, 1)], [(2, 1, 0)], [(2, 1, 1)]]
+    after_flip = moved(own_flip_, (1, 0, 0))
+    middle = [row_flip, pairs[1], pairs[3]]
+    early.append(swap(jnp.concatenate([*middle, two[None]])))
+    late = lax.optimization_barrier((after_flip, two_flip, cross_two, cross_two_flip))
+    swapped = [*early, *(swap(block) for block in late)]
+    held = [*first, pairs[0], row_pair, *middle, two, *late]
+    start = [[(0, 0, 0)], [(0, 0, 1)], [(0, 2, 0)], [(0, 1, 0), (0, 1, 1)]]
+    row_names = [[(1, 0, 0), (3, 0, 0)]]
+    more = [[(1, 0, 1), (3, 0, 1)], [(1, 1, 0), (1, 1, 1)], [(3, 1, 0), (3, 1, 1)], [(2, 0, 0)]]
+    rest = [[(0, 2, 1)], [(2, 0, 1)], [(2, 1, 0)], [(2, 1, 1)]]
     arrays, lies = [], []
-    for layer, blocks in enumerate((held, swapped)):
+    for layer, blocks, names in (
+        (0, held, start + row_names + more + rest),
+        (1, swapped, [sum(start, []), *row_names, sum(more, [])] + rest),
+    ):
         for listed, block in zip(names, blocks):
             arrays.append(block if block.ndim == 4 else block[None])
             lies.append([(*name, layer) for name in listed])

time: 159 us -> 163 us (1.025)
  waiting for transfers between devices: 63.2 us -> 70.4 us
  starting transfers between devices: 47.6 us -> 43.1 us
  other arithmetic: 2.57 us -> 4.74 us
    ppermute x28 -> x22, waiting for transfers between devices: 63.2 us -> 70.4 us  [moved(): return lax.ppermute(value, AXES, pairs)]
    ppermute x28 -> x22, starting transfers between devices: 47.6 us -> 43.1 us  [moved(): return lax.ppermute(value, AXES, pairs)]
    concatenate x0 -> x1, other arithmetic: none -> 2.17 us  [local(): early.append(swap(jnp.concatenate([*middle, two[None]])))]
    unnamed x41 -> x39, local copies, waits for them, and re-layouts: 4.75 us -> 6.41 us
  transfers between devices with their start and end apart: 28 -> 22, of which waited for: 12 -> 10; matrix products, arithmetic and copies ran while one was open for 4% -> 5% of each run, Pallas kernels for 0% -> 0%
where the time goes in v4:
time: 163 us
  waiting for transfers between devices  70.4 us (43%)
  starting transfers between devices  43.1 us (26%)
  Pallas kernels  36.3 us (22%)
  local copies, waits for them, and re-layouts  7.97 us (5%)
  other arithmetic  4.74 us (3%)
    ppermute x22, waiting for transfers between devices, moved(): return lax.ppermute(value, AXES, pairs)  70.4 us
    ppermute x22, starting transfers between devices, moved(): return lax.ppermute(value, AXES, pairs)  43.1 us
    pallas_call x1, Pallas kernels, band_lags(): pl.pallas_call(lambda *refs: band_kernel(lies, *refs), grid=(corr_steps +...  33.1 us
    unnamed x39, local copies, waits for them, and re-layouts  6.41 us
  transfers between devices with their start and end apart: 22, of which 10 were waited for; matrix products, arithmetic and copies ran while one was open for 5% of the time, Pallas kernels for 0%

profile of v4, /device:TPU:1, one launch (start us, length us, event | category | flops | bytes accessed | tf_op | source)
XLA Modules:
  0.0 162.9 jit_solution(4050318262664674051)
XLA Ops:
  0.0 1.0 slice_select_fusion
  1.0 3.8 %collective-permute-start = (bf16[2,8,32,128]{3,2,1,0:T(8,128)(2,1)S(1)}, bf16[2,8,32,128]{3,2,1,0:T(8,128)(2,1)S(1)}, u32[]{:S(2)}, u32[]{:S(2)}) collective-permute-start(bf16[2,8,32,128]{3,2,1,0:T(8,128)(2,1)S(1)} %slice_select_fusion), channel_id=1, source_target_pairs={{0,1},{1,0},{2,3},{3,2},{4,5},{5,4},{6,7},{7,6},{8,9},{9,8},{10,11... | collective-permute-start | bytes 393224 | tf_op jit(solution)/shard_map/ppermute | solution.py:47
  4.8 1.4 copy.4.mask_ref
  6.2 1.0 collective-permute-done.rim_ref
  7.8 3.1 %whiten.1.refs_1_.refs_2_ = bf16[33,32,256]{2,1,0:T(8,128)(2,1)} custom-call(s32[1]{0:T(128)} %bitcast.3.rank_ref, bf16[2,8,32,512]{3,2,1,0:T(8,128)(2,1)} %spectra_ref.1, bf16[2,8,32,128]{3,2,1,0:T(8,128)(2,1)} %copy-done.10, s32[32,8]{1,0:T(8,128)} %copy.4.mask_ref), custom_call_target="tpu_custom_call" | custom-call | tf_op jit(solution)/shard_map/whiten/pallas_call | solution.py:104
  11.0 6.2 %collective-permute-start.1 = (bf16[33,32,256]{2,1,0:T(8,128)(2,1)}, bf16[33,32,256]{2,1,0:T(8,128)(2,1)S(1)}, u32[]{:S(2)}, u32[]{:S(2)}) collective-permute-start(bf16[33,32,256]{2,1,0:T(8,128)(2,1)} %whiten.1.refs_1_.refs_2_), channel_id=1, source_target_pairs={{0,224},{1,225},{2,226},{3,227},{4,228},{5,229},{6,230},{7,231},{8... | collective-permute-start | bytes 1622024 | tf_op jit(solution)/shard_map/ppermute | solution.py:47
  17.2 2.9 %collective-permute-start.7 = (bf16[33,32,256]{2,1,0:T(8,128)(2,1)}, bf16[33,32,256]{2,1,0:T(8,128)(2,1)S(1)}, u32[]{:S(2)}, u32[]{:S(2)}) collective-permute-start(bf16[33,32,256]{2,1,0:T(8,128)(2,1)} %whiten.1.refs_1_.refs_2_), channel_id=1, source_target_pairs={{0,1},{1,0},{2,3},{3,2},{4,5},{5,4},{6,7},{7,6},{8,9},{9,8},{10,11... | collective-permute-start | bytes 1622024 | tf_op jit(solution)/shard_map/ppermute | solution.py:47
  20.1 7.4 %collective-permute-done.1 = bf16[33,32,256]{2,1,0:T(8,128)(2,1)S(1)} collective-permute-done((bf16[33,32,256]{2,1,0:T(8,128)(2,1)}, bf16[33,32,256]{2,1,0:T(8,128)(2,1)S(1)}, u32[]{:S(2)}, u32[]{:S(2)}) %collective-permute-start.1) | collective-permute-done | bytes 540704 | tf_op jit(solution)/shard_map/ppermute | solution.py:47
  27.5 1.4 broadcast_select_fusion
  28.9 2.8 %collective-permute-start.4 = (bf16[33,32,256]{2,1,0:T(8,128)(2,1)S(1)}, bf16[33,32,256]{2,1,0:T(8,128)(2,1)S(1)}, u32[]{:S(2)}, u32[]{:S(2)}) collective-permute-start(bf16[33,32,256]{2,1,0:T(8,128)(2,1)S(1)} %get-tuple-element.38), channel_id=1, source_target_pairs={{0,8},{1,9},{2,10},{3,11},{4,12},{5,13},{6,14},{7,15},{8,0},{9,1},... | collective-permute-start | bytes 1622024 | tf_op jit(solution)/shard_map/ppermute | solution.py:47
  32.0 2.4 %collective-permute-start.2 = (bf16[33,32,256]{2,1,0:T(8,128)(2,1)S(1)}, bf16[33,32,256]{2,1,0:T(8,128)(2,1)S(1)}, u32[]{:S(2)}, u32[]{:S(2)}) collective-permute-start(bf16[33,32,256]{2,1,0:T(8,128)(2,1)S(1)} %get-tuple-element.40), channel_id=1, source_target_pairs={{0,12},{1,13},{2,14},{3,15},{4,0},{5,1},{6,2},{7,3},{8,4},{9,5},{1... | collective-permute-start | bytes 1622024 | tf_op jit(solution)/shard_map/ppermute | solution.py:47
  34.4 2.7 %collective-permute-start.6 = (bf16[33,32,256]{2,1,0:T(8,128)(2,1)S(1)}, bf16[33,32,256]{2,1,0:T(8,128)(2,1)S(1)}, u32[]{:S(2)}, u32[]{:S(2)}) collective-permute-start(bf16[33,32,256]{2,1,0:T(8,128)(2,1)S(1)} %get-tuple-element.37), channel_id=1, source_target_pairs={{0,17},{1,16},{2,19},{3,18},{4,21},{5,20},{6,23},{7,22},{8,25},{9,... | collective-permute-start | bytes 1622024 | tf_op jit(solution)/shard_map/ppermute | solution.py:47
  37.1 4.7 %collective-permute-done.4 = bf16[33,32,256]{2,1,0:T(8,128)(2,1)S(1)} collective-permute-done((bf16[33,32,256]{2,1,0:T(8,128)(2,1)S(1)}, bf16[33,32,256]{2,1,0:T(8,128)(2,1)S(1)}, u32[]{:S(2)}, u32[]{:S(2)}) %collective-permute-start.4) | collective-permute-done | bytes 540704 | tf_op jit(solution)/shard_map/ppermute | solution.py:47
  41.8 14.4 %collective-permute-done.3 = bf16[33,32,256]{2,1,0:T(8,128)(2,1)S(1)} collective-permute-done((bf16[33,32,256]{2,1,0:T(8,128)(2,1)S(1)}, bf16[33,32,256]{2,1,0:T(8,128)(2,1)S(1)}, u32[]{:S(2)}, u32[]{:S(2)}) %collective-permute-start.3) | collective-permute-done | bytes 540704 | tf_op jit(solution)/shard_map/ppermute | solution.py:47
  56.4 1.3 collective-permute-start.10
  57.7 1.5 collective-permute-start.9
  59.3 3.0 %collective-permute-start.8 = (bf16[2,33,32,256]{3,2,1,0:T(8,128)(2,1)S(1)}, bf16[2,33,32,256]{3,2,1,0:T(8,128)(2,1)S(1)}, u32[]{:S(2)}, u32[]{:S(2)}) collective-permute-start(bf16[2,33,32,256]{3,2,1,0:T(8,128)(2,1)S(1)} %pad_maximum_fusion.2.refs_8_), channel_id=1, source_target_pairs={{0,1},{1,0},{2,3},{3,2},{4,5},{5,4},{6,7},{7,6},{8,9},{9,8},{10,11... | collective-permute-start | bytes 3244040 | tf_op jit(solution)/shard_map/ppermute | solution.py:47
  62.3 20.2 %collective-permute-done.10.refs_11_ = bf16[2,33,32,256]{3,2,1,0:T(8,128)(2,1)S(1)} collective-permute-done((bf16[2,33,32,256]{3,2,1,0:T(8,128)(2,1)S(1)}, bf16[2,33,32,256]{3,2,1,0:T(8,128)(2,1)S(1)}, u32[]{:S(2)}, u32[]{:S(2)}) %collective-permute-start.10) | collective-permute-done | bytes 1081376 | tf_op jit(solution)/shard_map/ppermute | solution.py:47
  82.5 2.5 %collective-permute-done.8.refs_9_ = bf16[2,33,32,256]{3,2,1,0:T(8,128)(2,1)S(1)} collective-permute-done((bf16[2,33,32,256]{3,2,1,0:T(8,128)(2,1)S(1)}, bf16[2,33,32,256]{3,2,1,0:T(8,128)(2,1)S(1)}, u32[]{:S(2)}, u32[]{:S(2)}) %collective-permute-start.8) | collective-permute-done | bytes 1081376 | tf_op jit(solution)/shard_map/ppermute | solution.py:47
  85.1 2.2 %pad_maximum_fusion = bf16[7,33,32,256]{3,2,1,0:T(8,128)(2,1)} fusion(bf16[1,33,32,256]{3,2,1,0:T(8,128)(2,1)S(1)} %bitcast.37, bf16[2,33,32,256]{3,2,1,0:T(8,128)(2,1)S(1)} %collective-permute-done.10.refs_11_, bf16[2,33,32,256]{3,2,1,0:T(8,128)(2,1)S(1)} %collective-permute-done.9.refs_10_, bf16[2,33,32,256]{3,2,1,0:T(8,128)(2,1)S(1)} %collective-permute-done.8.refs_9_), kind=kLoop, calls=%fused_computation | loop fusion | flops 5677056 | bytes 7569408 | tf_op jit(solution)/shard_map/concatenate | solution.py:409
  87.3 2.1 %collective-permute-start.17 = (bf16[7,33,32,256]{3,2,1,0:T(8,128)(2,1)}, bf16[7,33,32,256]{3,2,1,0:T(8,128)(2,1)}, u32[]{:S(2)}, u32[]{:S(2)}) collective-permute-start(bf16[7,33,32,256]{3,2,1,0:T(8,128)(2,1)} %pad_maximum_fusion), channel_id=1, source_target_pairs={{0,2},{1,3},{2,0},{3,1},{4,6},{5,7},{6,4},{7,5},{8,10},{9,11},{10,... | collective-permute-start | bytes 11354120 | tf_op jit(solution)/shard_map/ppermute | solution.py:47
  92.0 0.9 constant_dynamic-update-slice_fusion.1
  93.7 2.9 %collective-permute-start.12 = (bf16[33,32,256]{2,1,0:T(8,128)(2,1)S(1)}, bf16[33,32,256]{2,1,0:T(8,128)(2,1)S(1)}, u32[]{:S(2)}, u32[]{:S(2)}) collective-permute-start(bf16[33,32,256]{2,1,0:T(8,128)(2,1)S(1)} %collective-permute-done.4), channel_id=1, source_target_pairs={{0,1},{1,0},{2,3},{3,2},{4,5},{5,4},{6,7},{7,6},{8,9},{9,8},{10,11... | collective-permute-start | bytes 1622024 | tf_op jit(solution)/shard_map/ppermute | solution.py:47
  96.8 2.9 %collective-permute-start.13 = (bf16[33,32,256]{2,1,0:T(8,128)(2,1)S(1)}, bf16[33,32,256]{2,1,0:T(8,128)(2,1)S(1)}, u32[]{:S(2)}, u32[]{:S(2)}) collective-permute-start(bf16[33,32,256]{2,1,0:T(8,128)(2,1)S(1)} %slice_bitcast_fusion.1), channel_id=1, source_target_pairs={{0,12},{1,13},{2,14},{3,15},{4,0},{5,1},{6,2},{7,3},{8,4},{9,5},{1... | collective-permute-start | bytes 1622024 | tf_op jit(solution)/shard_map/ppermute | solution.py:47
  99.7 8.8 %collective-permute-done.12 = bf16[33,32,256]{2,1,0:T(8,128)(2,1)S(1)} collective-permute-done((bf16[33,32,256]{2,1,0:T(8,128)(2,1)S(1)}, bf16[33,32,256]{2,1,0:T(8,128)(2,1)S(1)}, u32[]{:S(2)}, u32[]{:S(2)}) %collective-permute-start.12) | collective-permute-done | bytes 540704 | tf_op jit(solution)/shard_map/ppermute | solution.py:47
  108.6 3.3 %collective-permute-start.11 = (bf16[33,32,256]{2,1,0:T(8,128)(2,1)S(1)}, bf16[33,32,256]{2,1,0:T(8,128)(2,1)S(1)}, u32[]{:S(2)}, u32[]{:S(2)}) collective-permute-start(bf16[33,32,256]{2,1,0:T(8,128)(2,1)S(1)} %copy-done.8), channel_id=1, source_target_pairs={{0,224},{1,225},{2,226},{3,227},{4,228},{5,229},{6,230},{7,231},{8... | collective-permute-start | bytes 1622024 | tf_op jit(solution)/shard_map/ppermute | solution.py:47
  111.9 1.7 %collective-permute-start.16 = (bf16[2,33,32,256]{3,2,1,0:T(8,128)(2,1)S(1)}, bf16[2,33,32,256]{3,2,1,0:T(8,128)(2,1)S(1)}, u32[]{:S(2)}, u32[]{:S(2)}) collective-permute-start(bf16[2,33,32,256]{3,2,1,0:T(8,128)(2,1)S(1)} %pad_maximum_fusion.2.refs_8_), channel_id=1, source_target_pairs={{0,2},{1,3},{2,0},{3,1},{4,6},{5,7},{6,4},{7,5},{8,10},{9,11},{10,... | collective-permute-start | bytes 3244040 | tf_op jit(solution)/shard_map/ppermute | solution.py:47
  113.6 8.5 %collective-permute-done.11 = bf16[33,32,256]{2,1,0:T(8,128)(2,1)S(1)} collective-permute-done((bf16[33,32,256]{2,1,0:T(8,128)(2,1)S(1)}, bf16[33,32,256]{2,1,0:T(8,128)(2,1)S(1)}, u32[]{:S(2)}, u32[]{:S(2)}) %collective-permute-start.11) | collective-permute-done | bytes 540704 | tf_op jit(solution)/shard_map/ppermute | solution.py:47
  122.1 2.3 %collective-permute-start.18 = (bf16[33,32,256]{2,1,0:T(8,128)(2,1)S(1)}, bf16[33,32,256]{2,1,0:T(8,128)(2,1)S(1)}, u32[]{:S(2)}, u32[]{:S(2)}) collective-permute-start(bf16[33,32,256]{2,1,0:T(8,128)(2,1)S(1)} %collective-permute-done.11), channel_id=1, source_target_pairs={{0,2},{1,3},{2,0},{3,1},{4,6},{5,7},{6,4},{7,5},{8,10},{9,11},{10,... | collective-permute-start | bytes 1622024 | tf_op jit(solution)/shard_map/ppermute | solution.py:47
  124.9 1.8 %collective-permute-done.18 = bf16[33,32,256]{2,1,0:T(8,128)(2,1)S(1)} collective-permute-done((bf16[33,32,256]{2,1,0:T(8,128)(2,1)S(1)}, bf16[33,32,256]{2,1,0:T(8,128)(2,1)S(1)}, u32[]{:S(2)}, u32[]{:S(2)}) %collective-permute-start.18) | collective-permute-done | bytes 540704 | tf_op jit(solution)/shard_map/ppermute | solution.py:47
  128.5 1.0 collective-permute-done.21
  129.6 33.1 %band_lags.1 = bf16[256,32,512]{2,1,0:T(8,128)(2,1)} custom-call(s32[5]{0:T(128)} %stack.40.refs_0_, bf16[33,32,256]{2,1,0:T(8,128)(2,1)} %whiten.1.refs_1_.refs_2_, bf16[33,32,256]{2,1,0:T(8,128)(2,1)} %whiten.1.refs_1_.refs_2_, bf16[33,32,256]{2,1,0:T(8,128)(2,1)} %copy-done.7, bf16[1,33,32,256]{3,2,1,0:T(8,128)(2,1)} %bitcast.30, ...), custom_call_target="tpu_custom_call" | custom-call | flops 17179869184 | bytes 27262976 | tf_op jit(solution)/shard_map/band_lags/pallas_call | solution.py:320
  (62 shorter events, 7.2 us)
Async XLA Ops:
  1.0 6.2 %collective-permute-start = (bf16[2,8,32,128]{3,2,1,0:T(8,128)(2,1)S(1)}, bf16[2,8,32,128]{3,2,1,0:T(8,128)(2,1)S(1)}, u32[]{:S(2)}, u32[]{:S(2)}) collective-permute-start(bf16[2,8,32,128]{3,2,1,0:T(8,128)(2,1)S(1)} %slice_select_fusion), channel_id=1, source_target_pairs={{0,1},{1,0},{2,3},{3,2},{4,5},{5,4},{6,7},{7,6},{8,9},{9,8},{10,11... | collective-permute-start | bytes 393224 | tf_op jit(solution)/shard_map/ppermute | solution.py:47
  11.0 16.5 %collective-permute-start.1 = (bf16[33,32,256]{2,1,0:T(8,128)(2,1)}, bf16[33,32,256]{2,1,0:T(8,128)(2,1)S(1)}, u32[]{:S(2)}, u32[]{:S(2)}) collective-permute-start(bf16[33,32,256]{2,1,0:T(8,128)(2,1)} %whiten.1.refs_1_.refs_2_), channel_id=1, source_target_pairs={{0,224},{1,225},{2,226},{3,227},{4,228},{5,229},{6,230},{7,231},{8... | collective-permute-start | bytes 1622024 | tf_op jit(solution)/shard_map/ppermute | solution.py:47
  17.2 20.0 %collective-permute-start.7 = (bf16[33,32,256]{2,1,0:T(8,128)(2,1)}, bf16[33,32,256]{2,1,0:T(8,128)(2,1)S(1)}, u32[]{:S(2)}, u32[]{:S(2)}) collective-permute-start(bf16[33,32,256]{2,1,0:T(8,128)(2,1)} %whiten.1.refs_1_.refs_2_), channel_id=1, source_target_pairs={{0,1},{1,0},{2,3},{3,2},{4,5},{5,4},{6,7},{7,6},{8,9},{9,8},{10,11... | collective-permute-start | bytes 1622024 | tf_op jit(solution)/shard_map/ppermute | solution.py:47
  27.5 63.6 %copy-start.3 = (bf16[33,32,256]{2,1,0:T(8,128)(2,1)}, bf16[33,32,256]{2,1,0:T(8,128)(2,1)S(1)}, u32[]{:S(2)}) copy-start(bf16[33,32,256]{2,1,0:T(8,128)(2,1)S(1)} %collective-permute-done.1) | copy-start | bytes 1622020
  28.9 12.9 %collective-permute-start.4 = (bf16[33,32,256]{2,1,0:T(8,128)(2,1)S(1)}, bf16[33,32,256]{2,1,0:T(8,128)(2,1)S(1)}, u32[]{:S(2)}, u32[]{:S(2)}) collective-permute-start(bf16[33,32,256]{2,1,0:T(8,128)(2,1)S(1)} %get-tuple-element.38), channel_id=1, source_target_pairs={{0,8},{1,9},{2,10},{3,11},{4,12},{5,13},{6,14},{7,15},{8,0},{9,1},... | collective-permute-start | bytes 1622024 | tf_op jit(solution)/shard_map/ppermute | solution.py:47
  31.7 24.5 %collective-permute-start.3 = (bf16[33,32,256]{2,1,0:T(8,128)(2,1)S(1)}, bf16[33,32,256]{2,1,0:T(8,128)(2,1)S(1)}, u32[]{:S(2)}, u32[]{:S(2)}) collective-permute-start(bf16[33,32,256]{2,1,0:T(8,128)(2,1)S(1)} %get-tuple-element.39), channel_id=1, source_target_pairs={{0,4},{1,5},{2,6},{3,7},{4,8},{5,9},{6,10},{7,11},{8,12},{9,13},{1... | collective-permute-start | bytes 1622024 | tf_op jit(solution)/shard_map/ppermute | solution.py:47
  32.0 24.2 %collective-permute-start.2 = (bf16[33,32,256]{2,1,0:T(8,128)(2,1)S(1)}, bf16[33,32,256]{2,1,0:T(8,128)(2,1)S(1)}, u32[]{:S(2)}, u32[]{:S(2)}) collective-permute-start(bf16[33,32,256]{2,1,0:T(8,128)(2,1)S(1)} %get-tuple-element.40), channel_id=1, source_target_pairs={{0,12},{1,13},{2,14},{3,15},{4,0},{5,1},{6,2},{7,3},{8,4},{9,5},{1... | collective-permute-start | bytes 1622024 | tf_op jit(solution)/shard_map/ppermute | solution.py:47
  34.4 21.9 %collective-permute-start.6 = (bf16[33,32,256]{2,1,0:T(8,128)(2,1)S(1)}, bf16[33,32,256]{2,1,0:T(8,128)(2,1)S(1)}, u32[]{:S(2)}, u32[]{:S(2)}) collective-permute-start(bf16[33,32,256]{2,1,0:T(8,128)(2,1)S(1)} %get-tuple-element.37), channel_id=1, source_target_pairs={{0,17},{1,16},{2,19},{3,18},{4,21},{5,20},{6,23},{7,22},{8,25},{9,... | collective-permute-start | bytes 1622024 | tf_op jit(solution)/shard_map/ppermute | solution.py:47
  37.1 47.9 %copy-start.7 = (bf16[33,32,256]{2,1,0:T(8,128)(2,1)}, bf16[33,32,256]{2,1,0:T(8,128)(2,1)S(1)}, u32[]{:S(2)}) copy-start(bf16[33,32,256]{2,1,0:T(8,128)(2,1)S(1)} %collective-permute-done.7.refs_3_) | copy-start | bytes 1622020
  37.1 19.1 %collective-permute-start.5 = (bf16[33,32,256]{2,1,0:T(8,128)(2,1)S(1)}, bf16[33,32,256]{2,1,0:T(8,128)(2,1)S(1)}, u32[]{:S(2)}, u32[]{:S(2)}) collective-permute-start(bf16[33,32,256]{2,1,0:T(8,128)(2,1)S(1)} %get-tuple-element.37), channel_id=1, source_target_pairs={{0,16},{1,17},{2,18},{3,19},{4,20},{5,21},{6,22},{7,23},{8,24},{9,... | collective-permute-start | bytes 1622024 | tf_op jit(solution)/shard_map/ppermute | solution.py:47
  41.8 51.9 %copy-start.9 = (bf16[33,32,256]{2,1,0:T(8,128)(2,1)}, bf16[33,32,256]{2,1,0:T(8,128)(2,1)S(1)}, u32[]{:S(2)}) copy-start(bf16[33,32,256]{2,1,0:T(8,128)(2,1)S(1)} %collective-permute-done.4) | copy-start | bytes 1622020
  56.4 28.7 %copy-start.4 = (bf16[2,33,32,256]{3,2,1,0:T(8,128)(2,1)}, bf16[2,33,32,256]{3,2,1,0:T(8,128)(2,1)S(1)}, u32[]{:S(2)}) copy-start(bf16[2,33,32,256]{3,2,1,0:T(8,128)(2,1)S(1)} %pad_maximum_fusion.1.refs_7_) | copy-start | bytes 3244036
  56.4 26.1 %collective-permute-start.10 = (bf16[2,33,32,256]{3,2,1,0:T(8,128)(2,1)S(1)}, bf16[2,33,32,256]{3,2,1,0:T(8,128)(2,1)S(1)}, u32[]{:S(2)}, u32[]{:S(2)}) collective-permute-start(bf16[2,33,32,256]{3,2,1,0:T(8,128)(2,1)S(1)} %pad_maximum_fusion.1.refs_7_), channel_id=1, source_target_pairs={{0,4},{1,5},{2,6},{3,7},{4,8},{5,9},{6,10},{7,11},{8,12},{9,13},{1... | collective-permute-start | bytes 3244040 | tf_op jit(solution)/shard_map/ppermute | solution.py:47
  57.7 24.8 %collective-permute-start.9 = (bf16[2,33,32,256]{3,2,1,0:T(8,128)(2,1)S(1)}, bf16[2,33,32,256]{3,2,1,0:T(8,128)(2,1)S(1)}, u32[]{:S(2)}, u32[]{:S(2)}) collective-permute-start(bf16[2,33,32,256]{3,2,1,0:T(8,128)(2,1)S(1)} %pad_maximum_fusion.1.refs_7_), channel_id=1, source_target_pairs={{0,12},{1,13},{2,14},{3,15},{4,0},{5,1},{6,2},{7,3},{8,4},{9,5},{1... | collective-permute-start | bytes 3244040 | tf_op jit(solution)/shard_map/ppermute | solution.py:47
  59.2 52.6 %copy-start.5 = (bf16[2,33,32,256]{3,2,1,0:T(8,128)(2,1)}, bf16[2,33,32,256]{3,2,1,0:T(8,128)(2,1)S(1)}, u32[]{:S(2)}) copy-start(bf16[2,33,32,256]{3,2,1,0:T(8,128)(2,1)S(1)} %pad_maximum_fusion.2.refs_8_) | copy-start | bytes 3244036
  59.3 25.8 %collective-permute-start.8 = (bf16[2,33,32,256]{3,2,1,0:T(8,128)(2,1)S(1)}, bf16[2,33,32,256]{3,2,1,0:T(8,128)(2,1)S(1)}, u32[]{:S(2)}, u32[]{:S(2)}) collective-permute-start(bf16[2,33,32,256]{3,2,1,0:T(8,128)(2,1)S(1)} %pad_maximum_fusion.2.refs_8_), channel_id=1, source_target_pairs={{0,1},{1,0},{2,3},{3,2},{4,5},{5,4},{6,7},{7,6},{8,9},{9,8},{10,11... | collective-permute-start | bytes 3244040 | tf_op jit(solution)/shard_map/ppermute | solution.py:47
  82.5 14.2 %copy-start.1 = (bf16[2,33,32,256]{3,2,1,0:T(8,128)(2,1)}, bf16[2,33,32,256]{3,2,1,0:T(8,128)(2,1)S(1)}, u32[]{:S(2)}) copy-start(bf16[2,33,32,256]{3,2,1,0:T(8,128)(2,1)S(1)} %collective-permute-done.10.refs_11_) | copy-start | bytes 3244036
  82.5 14.3 %copy-start.2 = (bf16[2,33,32,256]{3,2,1,0:T(8,128)(2,1)}, bf16[2,33,32,256]{3,2,1,0:T(8,128)(2,1)S(1)}, u32[]{:S(2)}) copy-start(bf16[2,33,32,256]{3,2,1,0:T(8,128)(2,1)S(1)} %collective-permute-done.9.refs_10_) | copy-start | bytes 3244036
  87.3 42.2 %collective-permute-start.17 = (bf16[7,33,32,256]{3,2,1,0:T(8,128)(2,1)}, bf16[7,33,32,256]{3,2,1,0:T(8,128)(2,1)}, u32[]{:S(2)}, u32[]{:S(2)}) collective-permute-start(bf16[7,33,32,256]{3,2,1,0:T(8,128)(2,1)} %pad_maximum_fusion), channel_id=1, source_target_pairs={{0,2},{1,3},{2,0},{3,1},{4,6},{5,7},{6,4},{7,5},{8,10},{9,11},{10,... | collective-permute-start | bytes 11354120 | tf_op jit(solution)/shard_map/ppermute | solution.py:47
  93.7 35.8 %collective-permute-start.15 = (bf16[5,33,32,256]{3,2,1,0:T(8,128)(2,1)}, bf16[5,33,32,256]{3,2,1,0:T(8,128)(2,1)}, u32[]{:S(2)}, u32[]{:S(2)}) collective-permute-start(bf16[5,33,32,256]{3,2,1,0:T(8,128)(2,1)} %constant_dynamic-update-slice_fusion), channel_id=1, source_target_pairs={{0,2},{1,3},{2,0},{3,1},{4,6},{5,7},{6,4},{7,5},{8,10},{9,11},{10,... | collective-permute-start | bytes 8110088 | tf_op jit(solution)/shard_map/ppermute | solution.py:47
  93.7 14.8 %collective-permute-start.12 = (bf16[33,32,256]{2,1,0:T(8,128)(2,1)S(1)}, bf16[33,32,256]{2,1,0:T(8,128)(2,1)S(1)}, u32[]{:S(2)}, u32[]{:S(2)}) collective-permute-start(bf16[33,32,256]{2,1,0:T(8,128)(2,1)S(1)} %collective-permute-done.4), channel_id=1, source_target_pairs={{0,1},{1,0},{2,3},{3,2},{4,5},{5,4},{6,7},{7,6},{8,9},{9,8},{10,11... | collective-permute-start | bytes 1622024 | tf_op jit(solution)/shard_map/ppermute | solution.py:47
  96.7 15.2 %collective-permute-start.14 = (bf16[33,32,256]{2,1,0:T(8,128)(2,1)S(1)}, bf16[33,32,256]{2,1,0:T(8,128)(2,1)S(1)}, u32[]{:S(2)}, u32[]{:S(2)}) collective-permute-start(bf16[33,32,256]{2,1,0:T(8,128)(2,1)S(1)} %slice_bitcast_fusion), channel_id=1, source_target_pairs={{0,4},{1,5},{2,6},{3,7},{4,8},{5,9},{6,10},{7,11},{8,12},{9,13},{1... | collective-permute-start | bytes 1622024 | tf_op jit(solution)/shard_map/ppermute | solution.py:47
  96.8 16.8 %collective-permute-start.13 = (bf16[33,32,256]{2,1,0:T(8,128)(2,1)S(1)}, bf16[33,32,256]{2,1,0:T(8,128)(2,1)S(1)}, u32[]{:S(2)}, u32[]{:S(2)}) collective-permute-start(bf16[33,32,256]{2,1,0:T(8,128)(2,1)S(1)} %slice_bitcast_fusion.1), channel_id=1, source_target_pairs={{0,12},{1,13},{2,14},{3,15},{4,0},{5,1},{6,2},{7,3},{8,4},{9,5},{1... | collective-permute-start | bytes 1622024 | tf_op jit(solution)/shard_map/ppermute | solution.py:47
  108.5 21.0 %copy-start.12 = (bf16[33,32,256]{2,1,0:T(8,128)(2,1)}, bf16[33,32,256]{2,1,0:T(8,128)(2,1)S(1)}, u32[]{:S(2)}) copy-start(bf16[33,32,256]{2,1,0:T(8,128)(2,1)S(1)} %collective-permute-done.12) | copy-start | bytes 1622020
  108.6 13.5 %collective-permute-start.11 = (bf16[33,32,256]{2,1,0:T(8,128)(2,1)S(1)}, bf16[33,32,256]{2,1,0:T(8,128)(2,1)S(1)}, u32[]{:S(2)}, u32[]{:S(2)}) collective-permute-start(bf16[33,32,256]{2,1,0:T(8,128)(2,1)S(1)} %copy-done.8), channel_id=1, source_target_pairs={{0,224},{1,225},{2,226},{3,227},{4,228},{5,229},{6,230},{7,231},{8... | collective-permute-start | bytes 1622024 | tf_op jit(solution)/shard_map/ppermute | solution.py:47
  111.9 17.7 %copy-start.13 = (bf16[33,32,256]{2,1,0:T(8,128)(2,1)}, bf16[33,32,256]{2,1,0:T(8,128)(2,1)S(1)}, u32[]{:S(2)}) copy-start(bf16[33,32,256]{2,1,0:T(8,128)(2,1)S(1)} %collective-permute-done.14) | copy-start | bytes 1622020
  111.9 12.5 %collective-permute-start.16 = (bf16[2,33,32,256]{3,2,1,0:T(8,128)(2,1)S(1)}, bf16[2,33,32,256]{3,2,1,0:T(8,128)(2,1)S(1)}, u32[]{:S(2)}, u32[]{:S(2)}) collective-permute-start(bf16[2,33,32,256]{3,2,1,0:T(8,128)(2,1)S(1)} %pad_maximum_fusion.2.refs_8_), channel_id=1, source_target_pairs={{0,2},{1,3},{2,0},{3,1},{4,6},{5,7},{6,4},{7,5},{8,10},{9,11},{10,... | collective-permute-start | bytes 3244040 | tf_op jit(solution)/shard_map/ppermute | solution.py:47
  113.6 15.9 %copy-start.14 = (bf16[33,32,256]{2,1,0:T(8,128)(2,1)}, bf16[33,32,256]{2,1,0:T(8,128)(2,1)S(1)}, u32[]{:S(2)}) copy-start(bf16[33,32,256]{2,1,0:T(8,128)(2,1)S(1)} %collective-permute-done.13) | copy-start | bytes 1622020
  122.1 4.6 %collective-permute-start.18 = (bf16[33,32,256]{2,1,0:T(8,128)(2,1)S(1)}, bf16[33,32,256]{2,1,0:T(8,128)(2,1)S(1)}, u32[]{:S(2)}, u32[]{:S(2)}) collective-permute-start(bf16[33,32,256]{2,1,0:T(8,128)(2,1)S(1)} %collective-permute-done.11), channel_id=1, source_target_pairs={{0,2},{1,3},{2,0},{3,1},{4,6},{5,7},{6,4},{7,5},{8,10},{9,11},{10,... | collective-permute-start | bytes 1622024 | tf_op jit(solution)/shard_map/ppermute | solution.py:47
  124.3 4.1 %collective-permute-start.19 = (bf16[33,32,256]{2,1,0:T(8,128)(2,1)S(1)}, bf16[33,32,256]{2,1,0:T(8,128)(2,1)}, u32[]{:S(2)}, u32[]{:S(2)}) collective-permute-start(bf16[33,32,256]{2,1,0:T(8,128)(2,1)S(1)} %collective-permute-done.12), channel_id=1, source_target_pairs={{0,2},{1,3},{2,0},{3,1},{4,6},{5,7},{6,4},{7,5},{8,10},{9,11},{10,... | collective-permute-start | bytes 1622024 | tf_op jit(solution)/shard_map/ppermute | solution.py:47
  124.4 4.1 %collective-permute-start.20 = (bf16[33,32,256]{2,1,0:T(8,128)(2,1)S(1)}, bf16[33,32,256]{2,1,0:T(8,128)(2,1)}, u32[]{:S(2)}, u32[]{:S(2)}) collective-permute-start(bf16[33,32,256]{2,1,0:T(8,128)(2,1)S(1)} %collective-permute-done.13), channel_id=1, source_target_pairs={{0,2},{1,3},{2,0},{3,1},{4,6},{5,7},{6,4},{7,5},{8,10},{9,11},{10,... | collective-permute-start | bytes 1622024 | tf_op jit(solution)/shard_map/ppermute | solution.py:47
  127.4 2.1 %collective-permute-start.21 = (bf16[33,32,256]{2,1,0:T(8,128)(2,1)S(1)}, bf16[33,32,256]{2,1,0:T(8,128)(2,1)}, u32[]{:S(2)}, u32[]{:S(2)}) collective-permute-start(bf16[33,32,256]{2,1,0:T(8,128)(2,1)S(1)} %collective-permute-done.14), channel_id=1, source_target_pairs={{0,2},{1,3},{2,0},{3,1},{4,6},{5,7},{6,4},{7,5},{8,10},{9,11},{10,... | collective-permute-start | bytes 1622024 | tf_op jit(solution)/shard_map/ppermute | solution.py:47
  (7 other events, 26.0 us)

commit v5 on v3

--- a/solution.py
+++ b/solution.py
@@ -54,7 +54,7 @@
     magnitude = jnp.sqrt(real * real + imag * imag).reshape(SEGMENTS * CH, BINS)
     rim_real = rim_ref[0].astype(jnp.float32)
     rim_imag = rim_ref[1].astype(jnp.float32)
-    rim = jnp.sqrt(rim_real * rim_real + rim_imag * rim_imag).reshape(SEGMENTS * CH, 128)
+    rim = jnp.sqrt(rim_real * rim_real + rim_imag * rim_imag).reshape(SEGMENTS * CH, HALF)
 
     def window_sum(values, positions):
         target = lax.broadcasted_iota(jnp.int32, (values.shape[1], BINS), 1)
@@ -67,7 +67,7 @@
         )
 
     inner = lax.broadcasted_iota(jnp.int32, (BINS, BINS), 0)
-    outer = lax.broadcasted_iota(jnp.int32, (128, BINS), 0) + jnp.where(rank == 0, BINS, -128)
+    outer = lax.broadcasted_iota(jnp.int32, (HALF, BINS), 0) + jnp.where(rank == 0, BINS, -HALF)
     summed = window_sum(magnitude, inner) + window_sum(rim, outer)
     bin_index = rank * BINS + lax.broadcasted_iota(jnp.int32, (1, BINS), 1)
     counted = (
@@ -366,7 +366,7 @@
     core, x, row = chan % 2, chan // 2 % LINE, chan // (2 * LINE) % ROWS
     chips = lax.axis_size("chan") // 2
     place = jnp.stack([core, x, chan // 2, jnp.int32(chips), rank]).astype(jnp.int32)
-    edge = jnp.where(rank == 0, spectra[..., BINS - 128 :], spectra[..., :128])
+    edge = jnp.where(rank == 0, spectra[..., BINS - HALF :], spectra[..., :HALF])
     rim = moved(edge, freq=1)
     own = whiten(rank.astype(jnp.int32).reshape(1), spectra, rim, seg_mask)
 

time: 146 us -> 146 us (level)
  no operation moved by 1% of the time
where the time goes in v5:
time: 146 us
  starting transfers between devices  51.7 us (35%)
  waiting for transfers between devices  46.5 us (32%)
  Pallas kernels  36.3 us (25%)
  local copies, waits for them, and re-layouts  5.93 us (4%)
  other arithmetic  4.96 us (3%)
    ppermute x23, starting transfers between devices, moved(): return lax.ppermute(value, AXES, pairs)  51.7 us
    ppermute x23, waiting for transfers between devices, moved(): return lax.ppermute(value, AXES, pairs)  46.5 us
    pallas_call x1, Pallas kernels, band_lags(): pl.pallas_call(lambda *refs: band_kernel(lies, *refs), grid=(corr_steps +...  33.1 us
    pallas_call x1, Pallas kernels, whiten(): pl.pallas_call(whiten_kernel, out_shape=jax.ShapeDtypeStruct((GROUPS + 1,...  3.13 us
  transfers between devices with their start and end apart: 23, of which 13 were waited for; matrix products, arithmetic and copies ran while one was open for 6% of the time, Pallas kernels for 0%

profile of v5, /device:TPU:1, one launch (start us, length us, event | category | flops | bytes accessed | tf_op | source)
XLA Modules:
  0.0 145.7 jit_solution(2764566490543802639)
XLA Ops:
  0.0 1.1 slice_select_fusion
  1.1 3.8 %collective-permute-start = (bf16[2,8,32,64]{3,2,1,0:T(8,128)(2,1)S(1)}, bf16[2,8,32,64]{3,2,1,0:T(8,128)(2,1)S(1)}, u32[]{:S(2)}, u32[]{:S(2)}) collective-permute-start(bf16[2,8,32,64]{3,2,1,0:T(8,128)(2,1)S(1)} %slice_select_fusion), channel_id=1, source_target_pairs={{0,1},{1,0},{2,3},{3,2},{4,5},{5,4},{6,7},{7,6},{8,9},{9,8},{10,11... | collective-permute-start | bytes 196616 | tf_op jit(solution)/shard_map/ppermute | solution.py:47
  4.9 1.4 copy.4.mask_ref
  6.3 1.0 collective-permute-done.rim_ref
  7.9 3.1 %whiten.1.refs_1_.refs_2_ = bf16[33,32,256]{2,1,0:T(8,128)(2,1)} custom-call(s32[1]{0:T(128)} %bitcast.3.rank_ref, bf16[2,8,32,512]{3,2,1,0:T(8,128)(2,1)} %spectra_ref.1, bf16[2,8,32,64]{3,2,1,0:T(8,128)(2,1)} %copy-done.7, s32[32,8]{1,0:T(8,128)} %copy.4.mask_ref), custom_call_target="tpu_custom_call" | custom-call | tf_op jit(solution)/shard_map/whiten/pallas_call | solution.py:104
  11.1 6.2 %collective-permute-start.1 = (bf16[33,32,256]{2,1,0:T(8,128)(2,1)}, bf16[33,32,256]{2,1,0:T(8,128)(2,1)S(1)}, u32[]{:S(2)}, u32[]{:S(2)}) collective-permute-start(bf16[33,32,256]{2,1,0:T(8,128)(2,1)} %whiten.1.refs_1_.refs_2_), channel_id=1, source_target_pairs={{0,224},{1,225},{2,226},{3,227},{4,228},{5,229},{6,230},{7,231},{8... | collective-permute-start | bytes 1622024 | tf_op jit(solution)/shard_map/ppermute | solution.py:47
  17.2 2.9 %collective-permute-start.6 = (bf16[33,32,256]{2,1,0:T(8,128)(2,1)}, bf16[33,32,256]{2,1,0:T(8,128)(2,1)S(1)}, u32[]{:S(2)}, u32[]{:S(2)}) collective-permute-start(bf16[33,32,256]{2,1,0:T(8,128)(2,1)} %whiten.1.refs_1_.refs_2_), channel_id=1, source_target_pairs={{0,1},{1,0},{2,3},{3,2},{4,5},{5,4},{6,7},{7,6},{8,9},{9,8},{10,11... | collective-permute-start | bytes 1622024 | tf_op jit(solution)/shard_map/ppermute | solution.py:47
  20.1 7.4 %collective-permute-done.1 = bf16[33,32,256]{2,1,0:T(8,128)(2,1)S(1)} collective-permute-done((bf16[33,32,256]{2,1,0:T(8,128)(2,1)}, bf16[33,32,256]{2,1,0:T(8,128)(2,1)S(1)}, u32[]{:S(2)}, u32[]{:S(2)}) %collective-permute-start.1) | collective-permute-done | bytes 540704 | tf_op jit(solution)/shard_map/ppermute | solution.py:47
  27.6 1.4 broadcast_select_fusion
  29.0 1.3 collective-permute-start.3
  30.2 1.5 %collective-permute-start.2 = (bf16[33,32,256]{2,1,0:T(8,128)(2,1)S(1)}, bf16[33,32,256]{2,1,0:T(8,128)(2,1)S(1)}, u32[]{:S(2)}, u32[]{:S(2)}) collective-permute-start(bf16[33,32,256]{2,1,0:T(8,128)(2,1)S(1)} %get-tuple-element.54), channel_id=1, source_target_pairs={{0,12},{1,13},{2,14},{3,15},{4,0},{5,1},{6,2},{7,3},{8,4},{9,5},{1... | collective-permute-start | bytes 1622024 | tf_op jit(solution)/shard_map/ppermute | solution.py:47
  31.7 2.7 %collective-permute-start.5 = (bf16[33,32,256]{2,1,0:T(8,128)(2,1)S(1)}, bf16[33,32,256]{2,1,0:T(8,128)(2,1)S(1)}, u32[]{:S(2)}, u32[]{:S(2)}) collective-permute-start(bf16[33,32,256]{2,1,0:T(8,128)(2,1)S(1)} %get-tuple-element.52), channel_id=1, source_target_pairs={{0,17},{1,16},{2,19},{3,18},{4,21},{5,20},{6,23},{7,22},{8,25},{9,... | collective-permute-start | bytes 1622024 | tf_op jit(solution)/shard_map/ppermute | solution.py:47
  34.5 7.1 %collective-permute-done.3 = bf16[33,32,256]{2,1,0:T(8,128)(2,1)S(1)} collective-permute-done((bf16[33,32,256]{2,1,0:T(8,128)(2,1)S(1)}, bf16[33,32,256]{2,1,0:T(8,128)(2,1)S(1)}, u32[]{:S(2)}, u32[]{:S(2)}) %collective-permute-start.3) | collective-permute-done | bytes 540704 | tf_op jit(solution)/shard_map/ppermute | solution.py:47
  41.5 2.2 %collective-permute-done.5 = bf16[33,32,256]{2,1,0:T(8,128)(2,1)S(1)} collective-permute-done((bf16[33,32,256]{2,1,0:T(8,128)(2,1)S(1)}, bf16[33,32,256]{2,1,0:T(8,128)(2,1)S(1)}, u32[]{:S(2)}, u32[]{:S(2)}) %collective-permute-start.5) | collective-permute-done | bytes 540704 | tf_op jit(solution)/shard_map/ppermute | solution.py:47
  43.8 1.1 collective-permute-done.4
  45.6 3.3 %collective-permute-start.8 = (bf16[33,32,256]{2,1,0:T(8,128)(2,1)S(1)}, bf16[33,32,256]{2,1,0:T(8,128)(2,1)S(1)}, u32[]{:S(2)}, u32[]{:S(2)}) collective-permute-start(bf16[33,32,256]{2,1,0:T(8,128)(2,1)S(1)} %collective-permute-done.6.refs_3_), channel_id=1, source_target_pairs={{0,224},{1,225},{2,226},{3,227},{4,228},{5,229},{6,230},{7,231},{8... | collective-permute-start | bytes 1622024 | tf_op jit(solution)/shard_map/ppermute | solution.py:47
  49.1 2.6 %collective-permute-start.9 = (bf16[2,33,32,256]{3,2,1,0:T(8,128)(2,1)S(1)}, bf16[2,33,32,256]{3,2,1,0:T(8,128)(2,1)}, u32[]{:S(2)}, u32[]{:S(2)}) collective-permute-start(bf16[2,33,32,256]{3,2,1,0:T(8,128)(2,1)S(1)} %pad_maximum_fusion.3.refs_8_), channel_id=1, source_target_pairs={{0,12},{1,13},{2,14},{3,15},{4,0},{5,1},{6,2},{7,3},{8,4},{9,5},{1... | collective-permute-start | bytes 3244040 | tf_op jit(solution)/shard_map/ppermute | solution.py:47
  52.1 4.0 %collective-permute-done.8 = bf16[33,32,256]{2,1,0:T(8,128)(2,1)S(1)} collective-permute-done((bf16[33,32,256]{2,1,0:T(8,128)(2,1)S(1)}, bf16[33,32,256]{2,1,0:T(8,128)(2,1)S(1)}, u32[]{:S(2)}, u32[]{:S(2)}) %collective-permute-start.8) | collective-permute-done | bytes 540704 | tf_op jit(solution)/shard_map/ppermute | solution.py:47
  56.0 11.4 %collective-permute-done.7.refs_10_ = bf16[2,33,32,256]{3,2,1,0:T(8,128)(2,1)S(1)} collective-permute-done((bf16[2,33,32,256]{3,2,1,0:T(8,128)(2,1)S(1)}, bf16[2,33,32,256]{3,2,1,0:T(8,128)(2,1)S(1)}, u32[]{:S(2)}, u32[]{:S(2)}) %collective-permute-start.7) | collective-permute-done | bytes 1081376 | tf_op jit(solution)/shard_map/ppermute | solution.py:47
  67.5 2.0 %pad_maximum_fusion = bf16[6,33,32,256]{3,2,1,0:T(8,128)(2,1)} fusion(bf16[2,33,32,256]{3,2,1,0:T(8,128)(2,1)S(1)} %collective-permute-done.7.refs_10_, bf16[2,33,32,256]{3,2,1,0:T(8,128)(2,1)S(1)} %pad_maximum_fusion.2.refs_9_, bf16[2,33,32,256]{3,2,1,0:T(8,128)(2,1)S(1)} %pad_maximum_fusion.3.refs_8_), kind=kLoop, calls=%fused_computation | loop fusion | flops 3244032 | bytes 6488064 | tf_op jit(solution)/shard_map/concatenate | solution.py:406
  69.5 5.4 %collective-permute-start.16 = (bf16[6,33,32,256]{3,2,1,0:T(8,128)(2,1)}, bf16[6,33,32,256]{3,2,1,0:T(8,128)(2,1)}, u32[]{:S(2)}, u32[]{:S(2)}) collective-permute-start(bf16[6,33,32,256]{3,2,1,0:T(8,128)(2,1)} %pad_maximum_fusion), channel_id=1, source_target_pairs={{0,2},{1,3},{2,0},{3,1},{4,6},{5,7},{6,4},{7,5},{8,10},{9,11},{10,... | collective-permute-start | bytes 9732104 | tf_op jit(solution)/shard_map/ppermute | solution.py:47
  75.0 7.8 %collective-permute-done.11 = bf16[33,32,256]{2,1,0:T(8,128)(2,1)S(1)} collective-permute-done((bf16[33,32,256]{2,1,0:T(8,128)(2,1)S(1)}, bf16[33,32,256]{2,1,0:T(8,128)(2,1)S(1)}, u32[]{:S(2)}, u32[]{:S(2)}) %collective-permute-start.11) | collective-permute-done | bytes 540704 | tf_op jit(solution)/shard_map/ppermute | solution.py:47
  82.8 1.3 slice_bitcast_fusion
  84.7 1.1 slice_bitcast_fusion.1
  85.8 2.2 %collective-permute-start.13 = (bf16[33,32,256]{2,1,0:T(8,128)(2,1)S(1)}, bf16[33,32,256]{2,1,0:T(8,128)(2,1)S(1)}, u32[]{:S(2)}, u32[]{:S(2)}) collective-permute-start(bf16[33,32,256]{2,1,0:T(8,128)(2,1)S(1)} %slice_bitcast_fusion.1), channel_id=1, source_target_pairs={{0,12},{1,13},{2,14},{3,15},{4,0},{5,1},{6,2},{7,3},{8,4},{9,5},{1... | collective-permute-start | bytes 1622024 | tf_op jit(solution)/shard_map/ppermute | solution.py:47
  88.0 1.7 %collective-permute-start.12 = (bf16[33,32,256]{2,1,0:T(8,128)(2,1)S(1)}, bf16[33,32,256]{2,1,0:T(8,128)(2,1)S(1)}, u32[]{:S(2)}, u32[]{:S(2)}) collective-permute-start(bf16[33,32,256]{2,1,0:T(8,128)(2,1)S(1)} %collective-permute-done.11), channel_id=1, source_target_pairs={{0,1},{1,0},{2,3},{3,2},{4,5},{5,4},{6,7},{7,6},{8,9},{9,8},{10,11... | collective-permute-start | bytes 1622024 | tf_op jit(solution)/shard_map/ppermute | solution.py:47
  90.0 7.4 %collective-permute-start.15 = (bf16[4,33,32,256]{3,2,1,0:T(8,128)(2,1)S(1)}, bf16[4,33,32,256]{3,2,1,0:T(8,128)(2,1)}, u32[]{:S(2)}, u32[]{:S(2)}) collective-permute-start(bf16[4,33,32,256]{3,2,1,0:T(8,128)(2,1)S(1)} %pad_maximum_fusion.1), channel_id=1, source_target_pairs={{0,2},{1,3},{2,0},{3,1},{4,6},{5,7},{6,4},{7,5},{8,10},{9,11},{10,... | collective-permute-start | bytes 6488072 | tf_op jit(solution)/shard_map/ppermute | solution.py:47
  97.7 7.3 %collective-permute-start.19 = (bf16[33,32,256]{2,1,0:T(8,128)(2,1)S(1)}, bf16[33,32,256]{2,1,0:T(8,128)(2,1)S(1)}, u32[]{:S(2)}, u32[]{:S(2)}) collective-permute-start(bf16[33,32,256]{2,1,0:T(8,128)(2,1)S(1)} %collective-permute-done.11), channel_id=1, source_target_pairs={{0,2},{1,3},{2,0},{3,1},{4,6},{5,7},{6,4},{7,5},{8,10},{9,11},{10,... | collective-permute-start | bytes 1622024 | tf_op jit(solution)/shard_map/ppermute | solution.py:47
  105.5 1.0 collective-permute-done.19
  108.1 0.8 copy-done.13
  110.0 2.4 %collective-permute-done.22 = bf16[33,32,256]{2,1,0:T(8,128)(2,1)} collective-permute-done((bf16[33,32,256]{2,1,0:T(8,128)(2,1)}, bf16[33,32,256]{2,1,0:T(8,128)(2,1)}, u32[]{:S(2)}, u32[]{:S(2)}) %collective-permute-start.22) | collective-permute-done | bytes 540704 | tf_op jit(solution)/shard_map/ppermute | solution.py:47
  112.4 33.1 %band_lags.1 = bf16[256,32,512]{2,1,0:T(8,128)(2,1)} custom-call(s32[5]{0:T(128)} %stack.50.refs_0_, bf16[33,32,256]{2,1,0:T(8,128)(2,1)} %whiten.1.refs_1_.refs_2_, bf16[33,32,256]{2,1,0:T(8,128)(2,1)} %whiten.1.refs_1_.refs_2_, bf16[33,32,256]{2,1,0:T(8,128)(2,1)} %copy-done.5, bf16[1,33,32,256]{3,2,1,0:T(8,128)(2,1)} %bitcast.28, ...), custom_call_target="tpu_custom_call" | custom-call | flops 17179869184 | bytes 27262976 | tf_op jit(solution)/shard_map/band_lags/pallas_call | solution.py:320
  (54 shorter events, 6.3 us)
Async XLA Ops:
  1.1 6.2 %collective-permute-start = (bf16[2,8,32,64]{3,2,1,0:T(8,128)(2,1)S(1)}, bf16[2,8,32,64]{3,2,1,0:T(8,128)(2,1)S(1)}, u32[]{:S(2)}, u32[]{:S(2)}) collective-permute-start(bf16[2,8,32,64]{3,2,1,0:T(8,128)(2,1)S(1)} %slice_select_fusion), channel_id=1, source_target_pairs={{0,1},{1,0},{2,3},{3,2},{4,5},{5,4},{6,7},{7,6},{8,9},{9,8},{10,11... | collective-permute-start | bytes 196616 | tf_op jit(solution)/shard_map/ppermute | solution.py:47
  11.1 16.5 %collective-permute-start.1 = (bf16[33,32,256]{2,1,0:T(8,128)(2,1)}, bf16[33,32,256]{2,1,0:T(8,128)(2,1)S(1)}, u32[]{:S(2)}, u32[]{:S(2)}) collective-permute-start(bf16[33,32,256]{2,1,0:T(8,128)(2,1)} %whiten.1.refs_1_.refs_2_), channel_id=1, source_target_pairs={{0,224},{1,225},{2,226},{3,227},{4,228},{5,229},{6,230},{7,231},{8... | collective-permute-start | bytes 1622024 | tf_op jit(solution)/shard_map/ppermute | solution.py:47
  17.2 17.2 %collective-permute-start.6 = (bf16[33,32,256]{2,1,0:T(8,128)(2,1)}, bf16[33,32,256]{2,1,0:T(8,128)(2,1)S(1)}, u32[]{:S(2)}, u32[]{:S(2)}) collective-permute-start(bf16[33,32,256]{2,1,0:T(8,128)(2,1)} %whiten.1.refs_1_.refs_2_), channel_id=1, source_target_pairs={{0,1},{1,0},{2,3},{3,2},{4,5},{5,4},{6,7},{7,6},{8,9},{9,8},{10,11... | collective-permute-start | bytes 1622024 | tf_op jit(solution)/shard_map/ppermute | solution.py:47
  27.6 62.1 %copy-start.3 = (bf16[33,32,256]{2,1,0:T(8,128)(2,1)}, bf16[33,32,256]{2,1,0:T(8,128)(2,1)S(1)}, u32[]{:S(2)}) copy-start(bf16[33,32,256]{2,1,0:T(8,128)(2,1)S(1)} %collective-permute-done.1) | copy-start | bytes 1622020
  29.0 12.6 %collective-permute-start.3 = (bf16[33,32,256]{2,1,0:T(8,128)(2,1)S(1)}, bf16[33,32,256]{2,1,0:T(8,128)(2,1)S(1)}, u32[]{:S(2)}, u32[]{:S(2)}) collective-permute-start(bf16[33,32,256]{2,1,0:T(8,128)(2,1)S(1)} %get-tuple-element.53), channel_id=1, source_target_pairs={{0,4},{1,5},{2,6},{3,7},{4,8},{5,9},{6,10},{7,11},{8,12},{9,13},{1... | collective-permute-start | bytes 1622024 | tf_op jit(solution)/shard_map/ppermute | solution.py:47
  30.2 11.3 %collective-permute-start.2 = (bf16[33,32,256]{2,1,0:T(8,128)(2,1)S(1)}, bf16[33,32,256]{2,1,0:T(8,128)(2,1)S(1)}, u32[]{:S(2)}, u32[]{:S(2)}) collective-permute-start(bf16[33,32,256]{2,1,0:T(8,128)(2,1)S(1)} %get-tuple-element.54), channel_id=1, source_target_pairs={{0,12},{1,13},{2,14},{3,15},{4,0},{5,1},{6,2},{7,3},{8,4},{9,5},{1... | collective-permute-start | bytes 1622024 | tf_op jit(solution)/shard_map/ppermute | solution.py:47
  31.7 12.1 %collective-permute-start.5 = (bf16[33,32,256]{2,1,0:T(8,128)(2,1)S(1)}, bf16[33,32,256]{2,1,0:T(8,128)(2,1)S(1)}, u32[]{:S(2)}, u32[]{:S(2)}) collective-permute-start(bf16[33,32,256]{2,1,0:T(8,128)(2,1)S(1)} %get-tuple-element.52), channel_id=1, source_target_pairs={{0,17},{1,16},{2,19},{3,18},{4,21},{5,20},{6,23},{7,22},{8,25},{9,... | collective-permute-start | bytes 1622024 | tf_op jit(solution)/shard_map/ppermute | solution.py:47
  34.4 10.5 %collective-permute-start.4 = (bf16[33,32,256]{2,1,0:T(8,128)(2,1)S(1)}, bf16[33,32,256]{2,1,0:T(8,128)(2,1)S(1)}, u32[]{:S(2)}, u32[]{:S(2)}) collective-permute-start(bf16[33,32,256]{2,1,0:T(8,128)(2,1)S(1)} %get-tuple-element.52), channel_id=1, source_target_pairs={{0,16},{1,17},{2,18},{3,19},{4,20},{5,21},{6,22},{7,23},{8,24},{9,... | collective-permute-start | bytes 1622024 | tf_op jit(solution)/shard_map/ppermute | solution.py:47
  34.4 55.2 %copy-start.5 = (bf16[33,32,256]{2,1,0:T(8,128)(2,1)}, bf16[33,32,256]{2,1,0:T(8,128)(2,1)S(1)}, u32[]{:S(2)}) copy-start(bf16[33,32,256]{2,1,0:T(8,128)(2,1)S(1)} %collective-permute-done.6.refs_3_) | copy-start | bytes 1622020
  45.0 22.5 %copy-start.1 = (bf16[2,33,32,256]{3,2,1,0:T(8,128)(2,1)}, bf16[2,33,32,256]{3,2,1,0:T(8,128)(2,1)S(1)}, u32[]{:S(2)}) copy-start(bf16[2,33,32,256]{3,2,1,0:T(8,128)(2,1)S(1)} %pad_maximum_fusion.2.refs_9_) | copy-start | bytes 3244036
  45.0 22.5 %collective-permute-start.7 = (bf16[2,33,32,256]{3,2,1,0:T(8,128)(2,1)S(1)}, bf16[2,33,32,256]{3,2,1,0:T(8,128)(2,1)S(1)}, u32[]{:S(2)}, u32[]{:S(2)}) collective-permute-start(bf16[2,33,32,256]{3,2,1,0:T(8,128)(2,1)S(1)} %pad_maximum_fusion.2.refs_9_), channel_id=1, source_target_pairs={{0,1},{1,0},{2,3},{3,2},{4,5},{5,4},{6,7},{7,6},{8,9},{9,8},{10,11... | collective-permute-start | bytes 3244040 | tf_op jit(solution)/shard_map/ppermute | solution.py:47
  45.6 10.5 %collective-permute-start.8 = (bf16[33,32,256]{2,1,0:T(8,128)(2,1)S(1)}, bf16[33,32,256]{2,1,0:T(8,128)(2,1)S(1)}, u32[]{:S(2)}, u32[]{:S(2)}) collective-permute-start(bf16[33,32,256]{2,1,0:T(8,128)(2,1)S(1)} %collective-permute-done.6.refs_3_), channel_id=1, source_target_pairs={{0,224},{1,225},{2,226},{3,227},{4,228},{5,229},{6,230},{7,231},{8... | collective-permute-start | bytes 1622024 | tf_op jit(solution)/shard_map/ppermute | solution.py:47
  49.0 20.5 %copy-start.2 = (bf16[2,33,32,256]{3,2,1,0:T(8,128)(2,1)}, bf16[2,33,32,256]{3,2,1,0:T(8,128)(2,1)S(1)}, u32[]{:S(2)}) copy-start(bf16[2,33,32,256]{3,2,1,0:T(8,128)(2,1)S(1)} %pad_maximum_fusion.3.refs_8_) | copy-start | bytes 3244036
  49.0 33.8 %collective-permute-start.10 = (bf16[2,33,32,256]{3,2,1,0:T(8,128)(2,1)S(1)}, bf16[2,33,32,256]{3,2,1,0:T(8,128)(2,1)}, u32[]{:S(2)}, u32[]{:S(2)}) collective-permute-start(bf16[2,33,32,256]{3,2,1,0:T(8,128)(2,1)S(1)} %pad_maximum_fusion.3.refs_8_), channel_id=1, source_target_pairs={{0,4},{1,5},{2,6},{3,7},{4,8},{5,9},{6,10},{7,11},{8,12},{9,13},{1... | collective-permute-start | bytes 3244040 | tf_op jit(solution)/shard_map/ppermute | solution.py:47
  49.1 33.7 %collective-permute-start.9 = (bf16[2,33,32,256]{3,2,1,0:T(8,128)(2,1)S(1)}, bf16[2,33,32,256]{3,2,1,0:T(8,128)(2,1)}, u32[]{:S(2)}, u32[]{:S(2)}) collective-permute-start(bf16[2,33,32,256]{3,2,1,0:T(8,128)(2,1)S(1)} %pad_maximum_fusion.3.refs_8_), channel_id=1, source_target_pairs={{0,12},{1,13},{2,14},{3,15},{4,0},{5,1},{6,2},{7,3},{8,4},{9,5},{1... | collective-permute-start | bytes 3244040 | tf_op jit(solution)/shard_map/ppermute | solution.py:47
  51.7 31.0 %collective-permute-start.11 = (bf16[33,32,256]{2,1,0:T(8,128)(2,1)S(1)}, bf16[33,32,256]{2,1,0:T(8,128)(2,1)S(1)}, u32[]{:S(2)}, u32[]{:S(2)}) collective-permute-start(bf16[33,32,256]{2,1,0:T(8,128)(2,1)S(1)} %get-tuple-element.51), channel_id=1, source_target_pairs={{0,8},{1,9},{2,10},{3,11},{4,12},{5,13},{6,14},{7,15},{8,0},{9,1},... | collective-permute-start | bytes 1622024 | tf_op jit(solution)/shard_map/ppermute | solution.py:47
  56.0 33.7 %copy-start.6 = (bf16[33,32,256]{2,1,0:T(8,128)(2,1)}, bf16[33,32,256]{2,1,0:T(8,128)(2,1)S(1)}, u32[]{:S(2)}) copy-start(bf16[33,32,256]{2,1,0:T(8,128)(2,1)S(1)} %collective-permute-done.8) | copy-start | bytes 1622020
  69.5 20.1 %copy-start = (bf16[33,32,256]{2,1,0:T(8,128)(2,1)S(1)}, bf16[33,32,256]{2,1,0:T(8,128)(2,1)}, u32[]{:S(2)}) copy-start(bf16[33,32,256]{2,1,0:T(8,128)(2,1)} %whiten.1.refs_1_.refs_2_) | copy-start | bytes 1622020
  69.5 42.8 %collective-permute-start.16 = (bf16[6,33,32,256]{3,2,1,0:T(8,128)(2,1)}, bf16[6,33,32,256]{3,2,1,0:T(8,128)(2,1)}, u32[]{:S(2)}, u32[]{:S(2)}) collective-permute-start(bf16[6,33,32,256]{3,2,1,0:T(8,128)(2,1)} %pad_maximum_fusion), channel_id=1, source_target_pairs={{0,2},{1,3},{2,0},{3,1},{4,6},{5,7},{6,4},{7,5},{8,10},{9,11},{10,... | collective-permute-start | bytes 9732104 | tf_op jit(solution)/shard_map/ppermute | solution.py:47
  82.8 14.9 %copy-start.8 = (bf16[33,32,256]{2,1,0:T(8,128)(2,1)}, bf16[33,32,256]{2,1,0:T(8,128)(2,1)S(1)}, u32[]{:S(2)}) copy-start(bf16[33,32,256]{2,1,0:T(8,128)(2,1)S(1)} %collective-permute-done.11) | copy-start | bytes 1622020
  84.0 13.3 %collective-permute-start.14 = (bf16[33,32,256]{2,1,0:T(8,128)(2,1)S(1)}, bf16[33,32,256]{2,1,0:T(8,128)(2,1)}, u32[]{:S(2)}, u32[]{:S(2)}) collective-permute-start(bf16[33,32,256]{2,1,0:T(8,128)(2,1)S(1)} %slice_bitcast_fusion), channel_id=1, source_target_pairs={{0,4},{1,5},{2,6},{3,7},{4,8},{5,9},{6,10},{7,11},{8,12},{9,13},{1... | collective-permute-start | bytes 1622024 | tf_op jit(solution)/shard_map/ppermute | solution.py:47
  85.8 11.6 %collective-permute-start.13 = (bf16[33,32,256]{2,1,0:T(8,128)(2,1)S(1)}, bf16[33,32,256]{2,1,0:T(8,128)(2,1)S(1)}, u32[]{:S(2)}, u32[]{:S(2)}) collective-permute-start(bf16[33,32,256]{2,1,0:T(8,128)(2,1)S(1)} %slice_bitcast_fusion.1), channel_id=1, source_target_pairs={{0,12},{1,13},{2,14},{3,15},{4,0},{5,1},{6,2},{7,3},{8,4},{9,5},{1... | collective-permute-start | bytes 1622024 | tf_op jit(solution)/shard_map/ppermute | solution.py:47
  88.0 9.7 %collective-permute-start.12 = (bf16[33,32,256]{2,1,0:T(8,128)(2,1)S(1)}, bf16[33,32,256]{2,1,0:T(8,128)(2,1)S(1)}, u32[]{:S(2)}, u32[]{:S(2)}) collective-permute-start(bf16[33,32,256]{2,1,0:T(8,128)(2,1)S(1)} %collective-permute-done.11), channel_id=1, source_target_pairs={{0,1},{1,0},{2,3},{3,2},{4,5},{5,4},{6,7},{7,6},{8,9},{9,8},{10,11... | collective-permute-start | bytes 1622024 | tf_op jit(solution)/shard_map/ppermute | solution.py:47
  90.0 22.4 %collective-permute-start.15 = (bf16[4,33,32,256]{3,2,1,0:T(8,128)(2,1)S(1)}, bf16[4,33,32,256]{3,2,1,0:T(8,128)(2,1)}, u32[]{:S(2)}, u32[]{:S(2)}) collective-permute-start(bf16[4,33,32,256]{3,2,1,0:T(8,128)(2,1)S(1)} %pad_maximum_fusion.1), channel_id=1, source_target_pairs={{0,2},{1,3},{2,0},{3,1},{4,6},{5,7},{6,4},{7,5},{8,10},{9,11},{10,... | collective-permute-start | bytes 6488072 | tf_op jit(solution)/shard_map/ppermute | solution.py:47
  97.4 9.2 %copy-start.9 = (bf16[33,32,256]{2,1,0:T(8,128)(2,1)}, bf16[33,32,256]{2,1,0:T(8,128)(2,1)S(1)}, u32[]{:S(2)}) copy-start(bf16[33,32,256]{2,1,0:T(8,128)(2,1)S(1)} %collective-permute-done.13) | copy-start | bytes 1622020
  97.7 10.5 %copy-start.10 = (bf16[33,32,256]{2,1,0:T(8,128)(2,1)}, bf16[33,32,256]{2,1,0:T(8,128)(2,1)S(1)}, u32[]{:S(2)}) copy-start(bf16[33,32,256]{2,1,0:T(8,128)(2,1)S(1)} %collective-permute-done.12) | copy-start | bytes 1622020
  97.7 8.9 %collective-permute-start.19 = (bf16[33,32,256]{2,1,0:T(8,128)(2,1)S(1)}, bf16[33,32,256]{2,1,0:T(8,128)(2,1)S(1)}, u32[]{:S(2)}, u32[]{:S(2)}) collective-permute-start(bf16[33,32,256]{2,1,0:T(8,128)(2,1)S(1)} %collective-permute-done.11), channel_id=1, source_target_pairs={{0,2},{1,3},{2,0},{3,1},{4,6},{5,7},{6,4},{7,5},{8,10},{9,11},{10,... | collective-permute-start | bytes 1622024 | tf_op jit(solution)/shard_map/ppermute | solution.py:47
  105.0 2.3 %collective-permute-start.20 = (bf16[33,32,256]{2,1,0:T(8,128)(2,1)S(1)}, bf16[33,32,256]{2,1,0:T(8,128)(2,1)S(1)}, u32[]{:S(2)}, u32[]{:S(2)}) collective-permute-start(bf16[33,32,256]{2,1,0:T(8,128)(2,1)S(1)} %collective-permute-done.12), channel_id=1, source_target_pairs={{0,2},{1,3},{2,0},{3,1},{4,6},{5,7},{6,4},{7,5},{8,10},{9,11},{10,... | collective-permute-start | bytes 1622024 | tf_op jit(solution)/shard_map/ppermute | solution.py:47
  105.1 3.0 %collective-permute-start.21 = (bf16[33,32,256]{2,1,0:T(8,128)(2,1)S(1)}, bf16[33,32,256]{2,1,0:T(8,128)(2,1)S(1)}, u32[]{:S(2)}, u32[]{:S(2)}) collective-permute-start(bf16[33,32,256]{2,1,0:T(8,128)(2,1)S(1)} %collective-permute-done.13), channel_id=1, source_target_pairs={{0,2},{1,3},{2,0},{3,1},{4,6},{5,7},{6,4},{7,5},{8,10},{9,11},{10,... | collective-permute-start | bytes 1622024 | tf_op jit(solution)/shard_map/ppermute | solution.py:47
  106.6 5.8 %collective-permute-start.17 = (bf16[2,33,32,256]{3,2,1,0:T(8,128)(2,1)}, bf16[2,33,32,256]{3,2,1,0:T(8,128)(2,1)}, u32[]{:S(2)}, u32[]{:S(2)}) collective-permute-start(bf16[2,33,32,256]{3,2,1,0:T(8,128)(2,1)} %collective-permute-done.9.refs_11_), channel_id=1, source_target_pairs={{0,2},{1,3},{2,0},{3,1},{4,6},{5,7},{6,4},{7,5},{8,10},{9,11},{10,... | collective-permute-start | bytes 3244040 | tf_op jit(solution)/shard_map/ppermute | solution.py:47
  107.4 5.0 %collective-permute-start.18 = (bf16[2,33,32,256]{3,2,1,0:T(8,128)(2,1)}, bf16[2,33,32,256]{3,2,1,0:T(8,128)(2,1)}, u32[]{:S(2)}, u32[]{:S(2)}) collective-permute-start(bf16[2,33,32,256]{3,2,1,0:T(8,128)(2,1)} %collective-permute-done.10.refs_12_), channel_id=1, source_target_pairs={{0,2},{1,3},{2,0},{3,1},{4,6},{5,7},{6,4},{7,5},{8,10},{9,11},{10,... | collective-permute-start | bytes 3244040 | tf_op jit(solution)/shard_map/ppermute | solution.py:47
  109.0 3.4 %collective-permute-start.22 = (bf16[33,32,256]{2,1,0:T(8,128)(2,1)}, bf16[33,32,256]{2,1,0:T(8,128)(2,1)}, u32[]{:S(2)}, u32[]{:S(2)}) collective-permute-start(bf16[33,32,256]{2,1,0:T(8,128)(2,1)} %collective-permute-done.14), channel_id=1, source_target_pairs={{0,2},{1,3},{2,0},{3,1},{4,6},{5,7},{6,4},{7,5},{8,10},{9,11},{10,... | collective-permute-start | bytes 1622024 | tf_op jit(solution)/shard_map/ppermute | solution.py:47
  (5 other events, 14.3 us)

commit v6 on v5

--- a/solution.py
+++ b/solution.py
@@ -386,17 +386,16 @@
     own_flip = flip(own)
     own, after = lax.optimization_barrier((own, after))
     crossing = jnp.where(row == 1, own, after)
-    one, three = reached(1), reached(3)
+    one, three, two = reached(1), reached(3), reached(2)
     cross = moved(crossing, (0, 1, 0))
     cross_flip = moved(crossing, (0, 1, 0), freq=1)
-    one, three, cross, cross_flip, own_flip = lax.optimization_barrier(
-        (one, three, cross, cross_flip, own_flip)
+    one, three, two, cross, cross_flip, own_flip = lax.optimization_barrier(
+        (one, three, two, cross, cross_flip, own_flip)
     )
     pairs = {0: jnp.stack([cross, cross_flip])}
     row_pair = jnp.stack([one, three])
     row_flip = flip(row_pair)
     pairs[1], pairs[3] = along(pairs[0], 1), along(pairs[0], 3)
-    two = reached(2)
     after_flip = moved(own_flip, (1, 0, 0))
     row_flip, after_flip, *gated = lax.optimization_barrier(
         (row_flip, after_flip, own, own_flip, after, pairs[0], row_pair)
@@ -405,7 +404,7 @@
         swap(jnp.stack([*gated[:3], after_flip])),
         swap(jnp.concatenate([*gated[3:], row_flip])),
     ]
-    pairs[1], pairs[3], two = lax.optimization_barrier((pairs[1], pairs[3], two))
+    pairs[1], pairs[3] = lax.optimization_barrier((pairs[1], pairs[3]))
     two_flip = flip(two)
     cross_two = along(pairs[1][0], 1)
     cross_two_flip = along(pairs[3][1], 3)

time: 146 us -> 149 us (1.021)
  waiting for transfers between devices: 46.5 us -> 58.5 us
  starting transfers between devices: 51.7 us -> 42.8 us
    ppermute x23, waiting for transfers between devices: 46.5 us -> 58.5 us  [moved(): return lax.ppermute(value, AXES, pairs)]
    ppermute x23, starting transfers between devices: 51.7 us -> 42.8 us  [moved(): return lax.ppermute(value, AXES, pairs)]
  transfers between devices with their start and end apart: 23 -> 23, of which waited for: 13 -> 13; matrix products, arithmetic and copies ran while one was open for 6% -> 5% of each run, Pallas kernels for 0% -> 0%
where the time goes in v6:
time: 149 us; the launch traced here: 148 us
  waiting for transfers between devices  58.5 us (39%)
  starting transfers between devices  42.8 us (29%)
  Pallas kernels  36.3 us (24%)
  local copies, waits for them, and re-layouts  5.71 us (4%)
  other arithmetic  4.97 us (3%)
    ppermute x23, waiting for transfers between devices, moved(): return lax.ppermute(value, AXES, pairs)  58.5 us
    ppermute x23, starting transfers between devices, moved(): return lax.ppermute(value, AXES, pairs)  42.8 us
    pallas_call x1, Pallas kernels, band_lags(): pl.pallas_call(lambda *refs: band_kernel(lies, *refs), grid=(corr_steps +...  33.1 us
    pallas_call x1, Pallas kernels, whiten(): pl.pallas_call(whiten_kernel, out_shape=jax.ShapeDtypeStruct((GROUPS + 1,...  3.12 us
  transfers between devices with their start and end apart: 23, of which 13 were waited for; matrix products, arithmetic and copies ran while one was open for 5% of the time, Pallas kernels for 0%

profile of v6, /device:TPU:1, one launch (start us, length us, event | category | flops | bytes accessed | tf_op | source)
XLA Modules:
  0.0 148.5 jit_solution(13674722649875900668)
XLA Ops:
  1.1 3.8 %collective-permute-start = (bf16[2,8,32,64]{3,2,1,0:T(8,128)(2,1)S(1)}, bf16[2,8,32,64]{3,2,1,0:T(8,128)(2,1)S(1)}, u32[]{:S(2)}, u32[]{:S(2)}) collective-permute-start(bf16[2,8,32,64]{3,2,1,0:T(8,128)(2,1)S(1)} %slice_select_fusion), channel_id=1, source_target_pairs={{0,1},{1,0},{2,3},{3,2},{4,5},{5,4},{6,7},{7,6},{8,9},{9,8},{10,11... | collective-permute-start | bytes 196616 | tf_op jit(solution)/shard_map/ppermute | solution.py:47
  4.9 1.4 copy.4.mask_ref
  7.9 3.1 %whiten.1.refs_1_.refs_2_ = bf16[33,32,256]{2,1,0:T(8,128)(2,1)} custom-call(s32[1]{0:T(128)} %bitcast.3.rank_ref, bf16[2,8,32,512]{3,2,1,0:T(8,128)(2,1)} %spectra_ref.1, bf16[2,8,32,64]{3,2,1,0:T(8,128)(2,1)} %copy-done.8, s32[32,8]{1,0:T(8,128)} %copy.4.mask_ref), custom_call_target="tpu_custom_call" | custom-call | tf_op jit(solution)/shard_map/whiten/pallas_call | solution.py:104
  11.1 6.2 %collective-permute-start.1 = (bf16[33,32,256]{2,1,0:T(8,128)(2,1)}, bf16[33,32,256]{2,1,0:T(8,128)(2,1)S(1)}, u32[]{:S(2)}, u32[]{:S(2)}) collective-permute-start(bf16[33,32,256]{2,1,0:T(8,128)(2,1)} %whiten.1.refs_1_.refs_2_), channel_id=1, source_target_pairs={{0,224},{1,225},{2,226},{3,227},{4,228},{5,229},{6,230},{7,231},{8... | collective-permute-start | bytes 1622024 | tf_op jit(solution)/shard_map/ppermute | solution.py:47
  17.2 2.9 %collective-permute-start.7 = (bf16[33,32,256]{2,1,0:T(8,128)(2,1)}, bf16[33,32,256]{2,1,0:T(8,128)(2,1)S(1)}, u32[]{:S(2)}, u32[]{:S(2)}) collective-permute-start(bf16[33,32,256]{2,1,0:T(8,128)(2,1)} %whiten.1.refs_1_.refs_2_), channel_id=1, source_target_pairs={{0,1},{1,0},{2,3},{3,2},{4,5},{5,4},{6,7},{7,6},{8,9},{9,8},{10,11... | collective-permute-start | bytes 1622024 | tf_op jit(solution)/shard_map/ppermute | solution.py:47
  20.1 7.4 %collective-permute-done.1 = bf16[33,32,256]{2,1,0:T(8,128)(2,1)S(1)} collective-permute-done((bf16[33,32,256]{2,1,0:T(8,128)(2,1)}, bf16[33,32,256]{2,1,0:T(8,128)(2,1)S(1)}, u32[]{:S(2)}, u32[]{:S(2)}) %collective-permute-start.1) | collective-permute-done | bytes 540704 | tf_op jit(solution)/shard_map/ppermute | solution.py:47
  27.6 1.4 broadcast_select_fusion
  29.0 2.8 %collective-permute-start.4 = (bf16[33,32,256]{2,1,0:T(8,128)(2,1)S(1)}, bf16[33,32,256]{2,1,0:T(8,128)(2,1)S(1)}, u32[]{:S(2)}, u32[]{:S(2)}) collective-permute-start(bf16[33,32,256]{2,1,0:T(8,128)(2,1)S(1)} %get-tuple-element.52), channel_id=1, source_target_pairs={{0,8},{1,9},{2,10},{3,11},{4,12},{5,13},{6,14},{7,15},{8,0},{9,1},... | collective-permute-start | bytes 1622024 | tf_op jit(solution)/shard_map/ppermute | solution.py:47
  32.1 2.4 %collective-permute-start.2 = (bf16[33,32,256]{2,1,0:T(8,128)(2,1)S(1)}, bf16[33,32,256]{2,1,0:T(8,128)(2,1)S(1)}, u32[]{:S(2)}, u32[]{:S(2)}) collective-permute-start(bf16[33,32,256]{2,1,0:T(8,128)(2,1)S(1)} %get-tuple-element.54), channel_id=1, source_target_pairs={{0,12},{1,13},{2,14},{3,15},{4,0},{5,1},{6,2},{7,3},{8,4},{9,5},{1... | collective-permute-start | bytes 1622024 | tf_op jit(solution)/shard_map/ppermute | solution.py:47
  34.5 2.7 %collective-permute-start.6 = (bf16[33,32,256]{2,1,0:T(8,128)(2,1)S(1)}, bf16[33,32,256]{2,1,0:T(8,128)(2,1)S(1)}, u32[]{:S(2)}, u32[]{:S(2)}) collective-permute-start(bf16[33,32,256]{2,1,0:T(8,128)(2,1)S(1)} %get-tuple-element.51), channel_id=1, source_target_pairs={{0,17},{1,16},{2,19},{3,18},{4,21},{5,20},{6,23},{7,22},{8,25},{9,... | collective-permute-start | bytes 1622024 | tf_op jit(solution)/shard_map/ppermute | solution.py:47
  37.2 4.7 %collective-permute-done.4 = bf16[33,32,256]{2,1,0:T(8,128)(2,1)S(1)} collective-permute-done((bf16[33,32,256]{2,1,0:T(8,128)(2,1)S(1)}, bf16[33,32,256]{2,1,0:T(8,128)(2,1)S(1)}, u32[]{:S(2)}, u32[]{:S(2)}) %collective-permute-start.4) | collective-permute-done | bytes 540704 | tf_op jit(solution)/shard_map/ppermute | solution.py:47
  41.9 14.4 %collective-permute-done.3 = bf16[33,32,256]{2,1,0:T(8,128)(2,1)S(1)} collective-permute-done((bf16[33,32,256]{2,1,0:T(8,128)(2,1)S(1)}, bf16[33,32,256]{2,1,0:T(8,128)(2,1)S(1)}, u32[]{:S(2)}, u32[]{:S(2)}) %collective-permute-start.3) | collective-permute-done | bytes 540704 | tf_op jit(solution)/shard_map/ppermute | solution.py:47
  56.5 3.0 %collective-permute-start.8 = (bf16[2,33,32,256]{3,2,1,0:T(8,128)(2,1)S(1)}, bf16[2,33,32,256]{3,2,1,0:T(8,128)(2,1)S(1)}, u32[]{:S(2)}, u32[]{:S(2)}) collective-permute-start(bf16[2,33,32,256]{3,2,1,0:T(8,128)(2,1)S(1)} %pad_maximum_fusion.2.refs_9_), channel_id=1, source_target_pairs={{0,1},{1,0},{2,3},{3,2},{4,5},{5,4},{6,7},{7,6},{8,9},{9,8},{10,11... | collective-permute-start | bytes 3244040 | tf_op jit(solution)/shard_map/ppermute | solution.py:47
  59.5 3.3 %collective-permute-start.9 = (bf16[33,32,256]{2,1,0:T(8,128)(2,1)S(1)}, bf16[33,32,256]{2,1,0:T(8,128)(2,1)S(1)}, u32[]{:S(2)}, u32[]{:S(2)}) collective-permute-start(bf16[33,32,256]{2,1,0:T(8,128)(2,1)S(1)} %collective-permute-done.7.refs_3_), channel_id=1, source_target_pairs={{0,224},{1,225},{2,226},{3,227},{4,228},{5,229},{6,230},{7,231},{8... | collective-permute-start | bytes 1622024 | tf_op jit(solution)/shard_map/ppermute | solution.py:47
  62.9 1.3 collective-permute-start.11
  64.2 1.5 collective-permute-start.10
  65.6 7.8 %collective-permute-done.9 = bf16[33,32,256]{2,1,0:T(8,128)(2,1)S(1)} collective-permute-done((bf16[33,32,256]{2,1,0:T(8,128)(2,1)S(1)}, bf16[33,32,256]{2,1,0:T(8,128)(2,1)S(1)}, u32[]{:S(2)}, u32[]{:S(2)}) %collective-permute-start.9) | collective-permute-done | bytes 540704 | tf_op jit(solution)/shard_map/ppermute | solution.py:47
  73.5 9.4 %collective-permute-done.8.refs_10_ = bf16[2,33,32,256]{3,2,1,0:T(8,128)(2,1)S(1)} collective-permute-done((bf16[2,33,32,256]{3,2,1,0:T(8,128)(2,1)S(1)}, bf16[2,33,32,256]{3,2,1,0:T(8,128)(2,1)S(1)}, u32[]{:S(2)}, u32[]{:S(2)}) %collective-permute-start.8) | collective-permute-done | bytes 1081376 | tf_op jit(solution)/shard_map/ppermute | solution.py:47
  82.9 2.0 %pad_maximum_fusion = bf16[6,33,32,256]{3,2,1,0:T(8,128)(2,1)} fusion(bf16[2,33,32,256]{3,2,1,0:T(8,128)(2,1)S(1)} %collective-permute-done.8.refs_10_, bf16[2,33,32,256]{3,2,1,0:T(8,128)(2,1)S(1)} %pad_maximum_fusion.2.refs_9_, bf16[2,33,32,256]{3,2,1,0:T(8,128)(2,1)S(1)} %pad_maximum_fusion.3.refs_8_), kind=kLoop, calls=%fused_computation | loop fusion | flops 3244032 | bytes 6488064 | tf_op jit(solution)/shard_map/concatenate | solution.py:405
  85.0 1.5 %collective-permute-start.16 = (bf16[6,33,32,256]{3,2,1,0:T(8,128)(2,1)}, bf16[6,33,32,256]{3,2,1,0:T(8,128)(2,1)}, u32[]{:S(2)}, u32[]{:S(2)}) collective-permute-start(bf16[6,33,32,256]{3,2,1,0:T(8,128)(2,1)} %pad_maximum_fusion), channel_id=1, source_target_pairs={{0,2},{1,3},{2,0},{3,1},{4,6},{5,7},{6,4},{7,5},{8,10},{9,11},{10,... | collective-permute-start | bytes 9732104 | tf_op jit(solution)/shard_map/ppermute | solution.py:47
  86.5 2.9 %collective-permute-start.12 = (bf16[33,32,256]{2,1,0:T(8,128)(2,1)S(1)}, bf16[33,32,256]{2,1,0:T(8,128)(2,1)S(1)}, u32[]{:S(2)}, u32[]{:S(2)}) collective-permute-start(bf16[33,32,256]{2,1,0:T(8,128)(2,1)S(1)} %collective-permute-done.4), channel_id=1, source_target_pairs={{0,1},{1,0},{2,3},{3,2},{4,5},{5,4},{6,7},{7,6},{8,9},{9,8},{10,11... | collective-permute-start | bytes 1622024 | tf_op jit(solution)/shard_map/ppermute | solution.py:47
  89.4 1.1 slice_bitcast_fusion
  90.5 1.3 collective-permute-start.14
  91.8 1.1 slice_bitcast_fusion.1
  92.9 1.7 %collective-permute-start.13 = (bf16[33,32,256]{2,1,0:T(8,128)(2,1)S(1)}, bf16[33,32,256]{2,1,0:T(8,128)(2,1)S(1)}, u32[]{:S(2)}, u32[]{:S(2)}) collective-permute-start(bf16[33,32,256]{2,1,0:T(8,128)(2,1)S(1)} %slice_bitcast_fusion.1), channel_id=1, source_target_pairs={{0,12},{1,13},{2,14},{3,15},{4,0},{5,1},{6,2},{7,3},{8,4},{9,5},{1... | collective-permute-start | bytes 1622024 | tf_op jit(solution)/shard_map/ppermute | solution.py:47
  94.9 1.8 %collective-permute-start.15 = (bf16[4,33,32,256]{3,2,1,0:T(8,128)(2,1)S(1)}, bf16[4,33,32,256]{3,2,1,0:T(8,128)(2,1)}, u32[]{:S(2)}, u32[]{:S(2)}) collective-permute-start(bf16[4,33,32,256]{3,2,1,0:T(8,128)(2,1)S(1)} %pad_maximum_fusion.1), channel_id=1, source_target_pairs={{0,2},{1,3},{2,0},{3,1},{4,6},{5,7},{6,4},{7,5},{8,10},{9,11},{10,... | collective-permute-start | bytes 6488072 | tf_op jit(solution)/shard_map/ppermute | solution.py:47
  96.7 5.1 %collective-permute-done.12 = bf16[33,32,256]{2,1,0:T(8,128)(2,1)S(1)} collective-permute-done((bf16[33,32,256]{2,1,0:T(8,128)(2,1)S(1)}, bf16[33,32,256]{2,1,0:T(8,128)(2,1)S(1)}, u32[]{:S(2)}, u32[]{:S(2)}) %collective-permute-start.12) | collective-permute-done | bytes 540704 | tf_op jit(solution)/shard_map/ppermute | solution.py:47
  101.8 2.7 %collective-permute-done.14 = bf16[33,32,256]{2,1,0:T(8,128)(2,1)} collective-permute-done((bf16[33,32,256]{2,1,0:T(8,128)(2,1)S(1)}, bf16[33,32,256]{2,1,0:T(8,128)(2,1)}, u32[]{:S(2)}, u32[]{:S(2)}) %collective-permute-start.14) | collective-permute-done | bytes 540704 | tf_op jit(solution)/shard_map/ppermute | solution.py:47
  104.5 1.6 %collective-permute-done.13 = bf16[33,32,256]{2,1,0:T(8,128)(2,1)S(1)} collective-permute-done((bf16[33,32,256]{2,1,0:T(8,128)(2,1)S(1)}, bf16[33,32,256]{2,1,0:T(8,128)(2,1)S(1)}, u32[]{:S(2)}, u32[]{:S(2)}) %collective-permute-start.13) | collective-permute-done | bytes 540704 | tf_op jit(solution)/shard_map/ppermute | solution.py:47
  106.1 1.7 %collective-permute-start.19 = (bf16[33,32,256]{2,1,0:T(8,128)(2,1)S(1)}, bf16[33,32,256]{2,1,0:T(8,128)(2,1)S(1)}, u32[]{:S(2)}, u32[]{:S(2)}) collective-permute-start(bf16[33,32,256]{2,1,0:T(8,128)(2,1)S(1)} %collective-permute-done.4), channel_id=1, source_target_pairs={{0,2},{1,3},{2,0},{3,1},{4,6},{5,7},{6,4},{7,5},{8,10},{9,11},{10,... | collective-permute-start | bytes 1622024 | tf_op jit(solution)/shard_map/ppermute | solution.py:47
  112.7 2.4 %collective-permute-done.22 = bf16[33,32,256]{2,1,0:T(8,128)(2,1)} collective-permute-done((bf16[33,32,256]{2,1,0:T(8,128)(2,1)}, bf16[33,32,256]{2,1,0:T(8,128)(2,1)}, u32[]{:S(2)}, u32[]{:S(2)}) %collective-permute-start.22) | collective-permute-done | bytes 540704 | tf_op jit(solution)/shard_map/ppermute | solution.py:47
  115.2 33.1 %band_lags.1 = bf16[256,32,512]{2,1,0:T(8,128)(2,1)} custom-call(s32[5]{0:T(128)} %stack.50.refs_0_, bf16[33,32,256]{2,1,0:T(8,128)(2,1)} %whiten.1.refs_1_.refs_2_, bf16[33,32,256]{2,1,0:T(8,128)(2,1)} %whiten.1.refs_1_.refs_2_, bf16[33,32,256]{2,1,0:T(8,128)(2,1)} %copy-done.5, bf16[1,33,32,256]{3,2,1,0:T(8,128)(2,1)} %bitcast.28, ...), custom_call_target="tpu_custom_call" | custom-call | flops 17179869184 | bytes 27262976 | tf_op jit(solution)/shard_map/band_lags/pallas_call | solution.py:320
  (56 shorter events, 8.6 us)
Async XLA Ops:
  1.1 6.2 %collective-permute-start = (bf16[2,8,32,64]{3,2,1,0:T(8,128)(2,1)S(1)}, bf16[2,8,32,64]{3,2,1,0:T(8,128)(2,1)S(1)}, u32[]{:S(2)}, u32[]{:S(2)}) collective-permute-start(bf16[2,8,32,64]{3,2,1,0:T(8,128)(2,1)S(1)} %slice_select_fusion), channel_id=1, source_target_pairs={{0,1},{1,0},{2,3},{3,2},{4,5},{5,4},{6,7},{7,6},{8,9},{9,8},{10,11... | collective-permute-start | bytes 196616 | tf_op jit(solution)/shard_map/ppermute | solution.py:47
  11.1 16.5 %collective-permute-start.1 = (bf16[33,32,256]{2,1,0:T(8,128)(2,1)}, bf16[33,32,256]{2,1,0:T(8,128)(2,1)S(1)}, u32[]{:S(2)}, u32[]{:S(2)}) collective-permute-start(bf16[33,32,256]{2,1,0:T(8,128)(2,1)} %whiten.1.refs_1_.refs_2_), channel_id=1, source_target_pairs={{0,224},{1,225},{2,226},{3,227},{4,228},{5,229},{6,230},{7,231},{8... | collective-permute-start | bytes 1622024 | tf_op jit(solution)/shard_map/ppermute | solution.py:47
  17.2 20.0 %collective-permute-start.7 = (bf16[33,32,256]{2,1,0:T(8,128)(2,1)}, bf16[33,32,256]{2,1,0:T(8,128)(2,1)S(1)}, u32[]{:S(2)}, u32[]{:S(2)}) collective-permute-start(bf16[33,32,256]{2,1,0:T(8,128)(2,1)} %whiten.1.refs_1_.refs_2_), channel_id=1, source_target_pairs={{0,1},{1,0},{2,3},{3,2},{4,5},{5,4},{6,7},{7,6},{8,9},{9,8},{10,11... | collective-permute-start | bytes 1622024 | tf_op jit(solution)/shard_map/ppermute | solution.py:47
  27.6 67.0 %copy-start.3 = (bf16[33,32,256]{2,1,0:T(8,128)(2,1)}, bf16[33,32,256]{2,1,0:T(8,128)(2,1)S(1)}, u32[]{:S(2)}) copy-start(bf16[33,32,256]{2,1,0:T(8,128)(2,1)S(1)} %collective-permute-done.1) | copy-start | bytes 1622020
  29.0 12.9 %collective-permute-start.4 = (bf16[33,32,256]{2,1,0:T(8,128)(2,1)S(1)}, bf16[33,32,256]{2,1,0:T(8,128)(2,1)S(1)}, u32[]{:S(2)}, u32[]{:S(2)}) collective-permute-start(bf16[33,32,256]{2,1,0:T(8,128)(2,1)S(1)} %get-tuple-element.52), channel_id=1, source_target_pairs={{0,8},{1,9},{2,10},{3,11},{4,12},{5,13},{6,14},{7,15},{8,0},{9,1},... | collective-permute-start | bytes 1622024 | tf_op jit(solution)/shard_map/ppermute | solution.py:47
  31.8 24.5 %collective-permute-start.3 = (bf16[33,32,256]{2,1,0:T(8,128)(2,1)S(1)}, bf16[33,32,256]{2,1,0:T(8,128)(2,1)S(1)}, u32[]{:S(2)}, u32[]{:S(2)}) collective-permute-start(bf16[33,32,256]{2,1,0:T(8,128)(2,1)S(1)} %get-tuple-element.53), channel_id=1, source_target_pairs={{0,4},{1,5},{2,6},{3,7},{4,8},{5,9},{6,10},{7,11},{8,12},{9,13},{1... | collective-permute-start | bytes 1622024 | tf_op jit(solution)/shard_map/ppermute | solution.py:47
  32.1 24.2 %collective-permute-start.2 = (bf16[33,32,256]{2,1,0:T(8,128)(2,1)S(1)}, bf16[33,32,256]{2,1,0:T(8,128)(2,1)S(1)}, u32[]{:S(2)}, u32[]{:S(2)}) collective-permute-start(bf16[33,32,256]{2,1,0:T(8,128)(2,1)S(1)} %get-tuple-element.54), channel_id=1, source_target_pairs={{0,12},{1,13},{2,14},{3,15},{4,0},{5,1},{6,2},{7,3},{8,4},{9,5},{1... | collective-permute-start | bytes 1622024 | tf_op jit(solution)/shard_map/ppermute | solution.py:47
  34.5 21.9 %collective-permute-start.6 = (bf16[33,32,256]{2,1,0:T(8,128)(2,1)S(1)}, bf16[33,32,256]{2,1,0:T(8,128)(2,1)S(1)}, u32[]{:S(2)}, u32[]{:S(2)}) collective-permute-start(bf16[33,32,256]{2,1,0:T(8,128)(2,1)S(1)} %get-tuple-element.51), channel_id=1, source_target_pairs={{0,17},{1,16},{2,19},{3,18},{4,21},{5,20},{6,23},{7,22},{8,25},{9,... | collective-permute-start | bytes 1622024 | tf_op jit(solution)/shard_map/ppermute | solution.py:47
  37.2 22.3 %copy-start.5 = (bf16[33,32,256]{2,1,0:T(8,128)(2,1)}, bf16[33,32,256]{2,1,0:T(8,128)(2,1)S(1)}, u32[]{:S(2)}) copy-start(bf16[33,32,256]{2,1,0:T(8,128)(2,1)S(1)} %collective-permute-done.7.refs_3_) | copy-start | bytes 1622020
  37.2 19.1 %collective-permute-start.5 = (bf16[33,32,256]{2,1,0:T(8,128)(2,1)S(1)}, bf16[33,32,256]{2,1,0:T(8,128)(2,1)S(1)}, u32[]{:S(2)}, u32[]{:S(2)}) collective-permute-start(bf16[33,32,256]{2,1,0:T(8,128)(2,1)S(1)} %get-tuple-element.51), channel_id=1, source_target_pairs={{0,16},{1,17},{2,18},{3,19},{4,20},{5,21},{6,22},{7,23},{8,24},{9,... | collective-permute-start | bytes 1622024 | tf_op jit(solution)/shard_map/ppermute | solution.py:47
  41.9 64.2 %copy-start.9 = (bf16[33,32,256]{2,1,0:T(8,128)(2,1)}, bf16[33,32,256]{2,1,0:T(8,128)(2,1)S(1)}, u32[]{:S(2)}) copy-start(bf16[33,32,256]{2,1,0:T(8,128)(2,1)S(1)} %collective-permute-done.4) | copy-start | bytes 1622020
  56.5 26.4 %copy-start.1 = (bf16[2,33,32,256]{3,2,1,0:T(8,128)(2,1)}, bf16[2,33,32,256]{3,2,1,0:T(8,128)(2,1)S(1)}, u32[]{:S(2)}) copy-start(bf16[2,33,32,256]{3,2,1,0:T(8,128)(2,1)S(1)} %pad_maximum_fusion.2.refs_9_) | copy-start | bytes 3244036
  56.5 26.4 %collective-permute-start.8 = (bf16[2,33,32,256]{3,2,1,0:T(8,128)(2,1)S(1)}, bf16[2,33,32,256]{3,2,1,0:T(8,128)(2,1)S(1)}, u32[]{:S(2)}, u32[]{:S(2)}) collective-permute-start(bf16[2,33,32,256]{3,2,1,0:T(8,128)(2,1)S(1)} %pad_maximum_fusion.2.refs_9_), channel_id=1, source_target_pairs={{0,1},{1,0},{2,3},{3,2},{4,5},{5,4},{6,7},{7,6},{8,9},{9,8},{10,11... | collective-permute-start | bytes 3244040 | tf_op jit(solution)/shard_map/ppermute | solution.py:47
  59.5 14.0 %collective-permute-start.9 = (bf16[33,32,256]{2,1,0:T(8,128)(2,1)S(1)}, bf16[33,32,256]{2,1,0:T(8,128)(2,1)S(1)}, u32[]{:S(2)}, u32[]{:S(2)}) collective-permute-start(bf16[33,32,256]{2,1,0:T(8,128)(2,1)S(1)} %collective-permute-done.7.refs_3_), channel_id=1, source_target_pairs={{0,224},{1,225},{2,226},{3,227},{4,228},{5,229},{6,230},{7,231},{8... | collective-permute-start | bytes 1622024 | tf_op jit(solution)/shard_map/ppermute | solution.py:47
  62.9 22.0 %copy-start.2 = (bf16[2,33,32,256]{3,2,1,0:T(8,128)(2,1)}, bf16[2,33,32,256]{3,2,1,0:T(8,128)(2,1)S(1)}, u32[]{:S(2)}) copy-start(bf16[2,33,32,256]{3,2,1,0:T(8,128)(2,1)S(1)} %pad_maximum_fusion.3.refs_8_) | copy-start | bytes 3244036
  62.9 26.5 %collective-permute-start.11 = (bf16[2,33,32,256]{3,2,1,0:T(8,128)(2,1)S(1)}, bf16[2,33,32,256]{3,2,1,0:T(8,128)(2,1)}, u32[]{:S(2)}, u32[]{:S(2)}) collective-permute-start(bf16[2,33,32,256]{3,2,1,0:T(8,128)(2,1)S(1)} %pad_maximum_fusion.3.refs_8_), channel_id=1, source_target_pairs={{0,4},{1,5},{2,6},{3,7},{4,8},{5,9},{6,10},{7,11},{8,12},{9,13},{1... | collective-permute-start | bytes 3244040 | tf_op jit(solution)/shard_map/ppermute | solution.py:47
  64.2 25.2 %collective-permute-start.10 = (bf16[2,33,32,256]{3,2,1,0:T(8,128)(2,1)S(1)}, bf16[2,33,32,256]{3,2,1,0:T(8,128)(2,1)}, u32[]{:S(2)}, u32[]{:S(2)}) collective-permute-start(bf16[2,33,32,256]{3,2,1,0:T(8,128)(2,1)S(1)} %pad_maximum_fusion.3.refs_8_), channel_id=1, source_target_pairs={{0,12},{1,13},{2,14},{3,15},{4,0},{5,1},{6,2},{7,3},{8,4},{9,5},{1... | collective-permute-start | bytes 3244040 | tf_op jit(solution)/shard_map/ppermute | solution.py:47
  73.4 21.1 %copy-start.7 = (bf16[33,32,256]{2,1,0:T(8,128)(2,1)}, bf16[33,32,256]{2,1,0:T(8,128)(2,1)S(1)}, u32[]{:S(2)}) copy-start(bf16[33,32,256]{2,1,0:T(8,128)(2,1)S(1)} %collective-permute-done.9) | copy-start | bytes 1622020
  85.0 9.6 %copy-start = (bf16[33,32,256]{2,1,0:T(8,128)(2,1)S(1)}, bf16[33,32,256]{2,1,0:T(8,128)(2,1)}, u32[]{:S(2)}) copy-start(bf16[33,32,256]{2,1,0:T(8,128)(2,1)} %whiten.1.refs_1_.refs_2_) | copy-start | bytes 1622020
  85.0 9.6 %copy-start.6 = (bf16[33,32,256]{2,1,0:T(8,128)(2,1)S(1)}, bf16[33,32,256]{2,1,0:T(8,128)(2,1)}, u32[]{:S(2)}) copy-start(bf16[33,32,256]{2,1,0:T(8,128)(2,1)} %copy-done.5) | copy-start | bytes 1622020
  85.0 30.2 %collective-permute-start.16 = (bf16[6,33,32,256]{3,2,1,0:T(8,128)(2,1)}, bf16[6,33,32,256]{3,2,1,0:T(8,128)(2,1)}, u32[]{:S(2)}, u32[]{:S(2)}) collective-permute-start(bf16[6,33,32,256]{3,2,1,0:T(8,128)(2,1)} %pad_maximum_fusion), channel_id=1, source_target_pairs={{0,2},{1,3},{2,0},{3,1},{4,6},{5,7},{6,4},{7,5},{8,10},{9,11},{10,... | collective-permute-start | bytes 9732104 | tf_op jit(solution)/shard_map/ppermute | solution.py:47
  86.5 15.3 %collective-permute-start.12 = (bf16[33,32,256]{2,1,0:T(8,128)(2,1)S(1)}, bf16[33,32,256]{2,1,0:T(8,128)(2,1)S(1)}, u32[]{:S(2)}, u32[]{:S(2)}) collective-permute-start(bf16[33,32,256]{2,1,0:T(8,128)(2,1)S(1)} %collective-permute-done.4), channel_id=1, source_target_pairs={{0,1},{1,0},{2,3},{3,2},{4,5},{5,4},{6,7},{7,6},{8,9},{9,8},{10,11... | collective-permute-start | bytes 1622024 | tf_op jit(solution)/shard_map/ppermute | solution.py:47
  90.5 14.0 %collective-permute-start.14 = (bf16[33,32,256]{2,1,0:T(8,128)(2,1)S(1)}, bf16[33,32,256]{2,1,0:T(8,128)(2,1)}, u32[]{:S(2)}, u32[]{:S(2)}) collective-permute-start(bf16[33,32,256]{2,1,0:T(8,128)(2,1)S(1)} %slice_bitcast_fusion), channel_id=1, source_target_pairs={{0,4},{1,5},{2,6},{3,7},{4,8},{5,9},{6,10},{7,11},{8,12},{9,13},{1... | collective-permute-start | bytes 1622024 | tf_op jit(solution)/shard_map/ppermute | solution.py:47
  92.9 13.3 %collective-permute-start.13 = (bf16[33,32,256]{2,1,0:T(8,128)(2,1)S(1)}, bf16[33,32,256]{2,1,0:T(8,128)(2,1)S(1)}, u32[]{:S(2)}, u32[]{:S(2)}) collective-permute-start(bf16[33,32,256]{2,1,0:T(8,128)(2,1)S(1)} %slice_bitcast_fusion.1), channel_id=1, source_target_pairs={{0,12},{1,13},{2,14},{3,15},{4,0},{5,1},{6,2},{7,3},{8,4},{9,5},{1... | collective-permute-start | bytes 1622024 | tf_op jit(solution)/shard_map/ppermute | solution.py:47
  94.9 20.3 %collective-permute-start.15 = (bf16[4,33,32,256]{3,2,1,0:T(8,128)(2,1)S(1)}, bf16[4,33,32,256]{3,2,1,0:T(8,128)(2,1)}, u32[]{:S(2)}, u32[]{:S(2)}) collective-permute-start(bf16[4,33,32,256]{3,2,1,0:T(8,128)(2,1)S(1)} %pad_maximum_fusion.1), channel_id=1, source_target_pairs={{0,2},{1,3},{2,0},{3,1},{4,6},{5,7},{6,4},{7,5},{8,10},{9,11},{10,... | collective-permute-start | bytes 6488072 | tf_op jit(solution)/shard_map/ppermute | solution.py:47
  101.8 7.6 %copy-start.10 = (bf16[33,32,256]{2,1,0:T(8,128)(2,1)}, bf16[33,32,256]{2,1,0:T(8,128)(2,1)S(1)}, u32[]{:S(2)}) copy-start(bf16[33,32,256]{2,1,0:T(8,128)(2,1)S(1)} %collective-permute-done.12) | copy-start | bytes 1622020
  106.1 3.2 %collective-permute-start.19 = (bf16[33,32,256]{2,1,0:T(8,128)(2,1)S(1)}, bf16[33,32,256]{2,1,0:T(8,128)(2,1)S(1)}, u32[]{:S(2)}, u32[]{:S(2)}) collective-permute-start(bf16[33,32,256]{2,1,0:T(8,128)(2,1)S(1)} %collective-permute-done.4), channel_id=1, source_target_pairs={{0,2},{1,3},{2,0},{3,1},{4,6},{5,7},{6,4},{7,5},{8,10},{9,11},{10,... | collective-permute-start | bytes 1622024 | tf_op jit(solution)/shard_map/ppermute | solution.py:47
  107.8 2.3 %collective-permute-start.20 = (bf16[33,32,256]{2,1,0:T(8,128)(2,1)S(1)}, bf16[33,32,256]{2,1,0:T(8,128)(2,1)S(1)}, u32[]{:S(2)}, u32[]{:S(2)}) collective-permute-start(bf16[33,32,256]{2,1,0:T(8,128)(2,1)S(1)} %collective-permute-done.12), channel_id=1, source_target_pairs={{0,2},{1,3},{2,0},{3,1},{4,6},{5,7},{6,4},{7,5},{8,10},{9,11},{10,... | collective-permute-start | bytes 1622024 | tf_op jit(solution)/shard_map/ppermute | solution.py:47
  107.9 3.0 %collective-permute-start.21 = (bf16[33,32,256]{2,1,0:T(8,128)(2,1)S(1)}, bf16[33,32,256]{2,1,0:T(8,128)(2,1)S(1)}, u32[]{:S(2)}, u32[]{:S(2)}) collective-permute-start(bf16[33,32,256]{2,1,0:T(8,128)(2,1)S(1)} %collective-permute-done.13), channel_id=1, source_target_pairs={{0,2},{1,3},{2,0},{3,1},{4,6},{5,7},{6,4},{7,5},{8,10},{9,11},{10,... | collective-permute-start | bytes 1622024 | tf_op jit(solution)/shard_map/ppermute | solution.py:47
  109.4 5.8 %collective-permute-start.17 = (bf16[2,33,32,256]{3,2,1,0:T(8,128)(2,1)}, bf16[2,33,32,256]{3,2,1,0:T(8,128)(2,1)}, u32[]{:S(2)}, u32[]{:S(2)}) collective-permute-start(bf16[2,33,32,256]{3,2,1,0:T(8,128)(2,1)} %collective-permute-done.10.refs_11_), channel_id=1, source_target_pairs={{0,2},{1,3},{2,0},{3,1},{4,6},{5,7},{6,4},{7,5},{8,10},{9,11},{10,... | collective-permute-start | bytes 3244040 | tf_op jit(solution)/shard_map/ppermute | solution.py:47
  110.2 5.0 %collective-permute-start.18 = (bf16[2,33,32,256]{3,2,1,0:T(8,128)(2,1)}, bf16[2,33,32,256]{3,2,1,0:T(8,128)(2,1)}, u32[]{:S(2)}, u32[]{:S(2)}) collective-permute-start(bf16[2,33,32,256]{3,2,1,0:T(8,128)(2,1)} %collective-permute-done.11.refs_12_), channel_id=1, source_target_pairs={{0,2},{1,3},{2,0},{3,1},{4,6},{5,7},{6,4},{7,5},{8,10},{9,11},{10,... | collective-permute-start | bytes 3244040 | tf_op jit(solution)/shard_map/ppermute | solution.py:47
  111.7 3.4 %collective-permute-start.22 = (bf16[33,32,256]{2,1,0:T(8,128)(2,1)}, bf16[33,32,256]{2,1,0:T(8,128)(2,1)}, u32[]{:S(2)}, u32[]{:S(2)}) collective-permute-start(bf16[33,32,256]{2,1,0:T(8,128)(2,1)} %collective-permute-done.14), channel_id=1, source_target_pairs={{0,2},{1,3},{2,0},{3,1},{4,6},{5,7},{6,4},{7,5},{8,10},{9,11},{10,... | collective-permute-start | bytes 1622024 | tf_op jit(solution)/shard_map/ppermute | solution.py:47
  (6 other events, 18.4 us)
